TPU v7x, 32 devices: a whole 2x2x4 slice. The times are simulated.
32 devices in a mesh: group: 4 (over y, x), mp: 8 (over z, core).
Axes of the slice: x: 2, y: 2, z: 4, core: 2. Of those that a mesh axis runs over, the one named last changes fastest.
Arguments:
- tokens: bfloat16 [640, 4096], P(None, 'group'), may hold values from -6 to 6
- trunk_gate: bfloat16 [4096, 11008], P('group', 'mp'), may hold values from -0.09375 to 0.09375
- trunk_up: bfloat16 [4096, 11008], P('group', 'mp'), may hold values from -0.09375 to 0.09375
- trunk_down: bfloat16 [11008, 4096], P('mp', 'group'), may hold values from -0.0546875 to 0.0546875
- head_gate: bfloat16 [4, 4096, 11008], P('group', None, 'mp'), may hold values from -0.09375 to 0.09375
- head_up: bfloat16 [4, 4096, 11008], P('group', None, 'mp'), may hold values from -0.09375 to 0.09375
- head_down: bfloat16 [4, 11008, 4096], P('group', 'mp'), may hold values from -0.0546875 to 0.0546875
- head_grads: bfloat16 [4, 640, 4096], P('group', None, 'mp'), may hold values from -6 to 6
Outputs:
- grad_x: bfloat16 [640, 4096], P('mp', 'group')
- grad_gate: float32 [4096, 11008], P('group', 'mp')
- grad_up: float32 [4096, 11008], P('group', 'mp')
- grad_down: float32 [11008, 4096], P('mp', 'group')
All inputs are finite; a program needn't handle non-finite values.
Results may differ from a plain program's by a relative error of at most 0.009.
Values may be sent and summed in bfloat16 or wider, within the bound.
No kernel may reach another device: no remote copies, remote signals or barrier semaphores. Data moves between devices by JAX's collectives and lax.ppermute only.
A program may use at most 192 MiB of HBM per device.

v0:
```python
import jax
import jax.numpy as jnp
from jax import lax
from jax.sharding import PartitionSpec as P


def silu_grad(pre_act):
    sig = jax.nn.sigmoid(pre_act)
    return sig * (1.0 + pre_act * (1.0 - sig))


def contract_last(left, right):
    return lax.dot_general(
        left, right, (((1,), (1,)), ((), ())), preferred_element_type=jnp.float32
    )


def contract_first(left, right):
    return lax.dot_general(
        left, right, (((0,), (0,)), ((), ())), preferred_element_type=jnp.float32
    )


def body(tokens, trunk_gate, trunk_up, trunk_down, head_gate, head_up, head_down, head_grads):
    gate_part = jnp.dot(tokens, trunk_gate, preferred_element_type=jnp.float32)
    up_part = jnp.dot(tokens, trunk_up, preferred_element_type=jnp.float32)
    gate_t, up_t = lax.psum((gate_part, up_part), "group")
    hidden_t = (jax.nn.silu(gate_t) * up_t).astype(jnp.bfloat16)
    down_part = jnp.dot(hidden_t, trunk_down, preferred_element_type=jnp.float32)
    col_width = down_part.shape[1]
    scattered = lax.psum_scatter(down_part, "mp", scatter_dimension=0, tiled=True)
    share_rows = scattered.shape[0]
    own_tok = lax.dynamic_slice_in_dim(tokens, lax.axis_index("mp") * share_rows, share_rows, 0)
    shard_rows = (own_tok.astype(jnp.float32) + scattered).astype(jnp.bfloat16)
    wide_rows = lax.all_gather(shard_rows, "group", axis=1, tiled=True)
    trunk_out = lax.all_gather(wide_rows, "mp", axis=0, tiled=True)
    gate_mat = head_gate[0]
    up_mat = head_up[0]
    down_mat = head_down[0]
    cot_local = head_grads[0]
    cot_full = lax.all_gather(cot_local, "mp", axis=1, tiled=True)
    head_pre = jnp.dot(trunk_out, gate_mat, preferred_element_type=jnp.float32)
    head_lin = jnp.dot(trunk_out, up_mat, preferred_element_type=jnp.float32)
    grad_hid = contract_last(cot_full, down_mat)
    gate_grad = (grad_hid * head_lin * silu_grad(head_pre)).astype(jnp.bfloat16)
    lin_grad = (grad_hid * jax.nn.silu(head_pre)).astype(jnp.bfloat16)
    partial_sum = contract_last(gate_grad, gate_mat) + contract_last(lin_grad, up_mat)
    col_count = cot_local.shape[1]
    col_start = lax.axis_index("mp") * col_count
    own_block = lax.dynamic_slice_in_dim(partial_sum, col_start, col_count, 1)
    partial_sum = lax.dynamic_update_slice_in_dim(
        partial_sum, own_block + cot_local.astype(jnp.float32), col_start, 1
    )
    total_sum = lax.psum(partial_sum, ("group", "mp"))
    col_begin = lax.axis_index("group") * col_width
    grad_mid = lax.dynamic_slice_in_dim(total_sum, col_begin, col_width, 1).astype(jnp.bfloat16)
    back_part = contract_last(grad_mid, trunk_down)
    ghid_t = lax.psum(back_part, "group")
    dgate_t = (ghid_t * up_t * silu_grad(gate_t)).astype(jnp.bfloat16)
    dup_t = (ghid_t * jax.nn.silu(gate_t)).astype(jnp.bfloat16)
    grad_gate = contract_first(tokens, dgate_t)
    grad_up = contract_first(tokens, dup_t)
    grad_down = contract_first(hidden_t, grad_mid)
    input_part = contract_last(dgate_t, trunk_gate) + contract_last(dup_t, trunk_up)
    row_terms = lax.psum_scatter(input_part, "mp", scatter_dimension=0, tiled=True)
    row_count = row_terms.shape[0]
    own_rows = lax.dynamic_slice_in_dim(grad_mid, lax.axis_index("mp") * row_count, row_count, 0)
    grad_x = (own_rows.astype(jnp.float32) + row_terms).astype(jnp.bfloat16)
    return (grad_x, grad_gate, grad_up, grad_down)


def solution(mesh):
    return jax.shard_map(
        body,
        mesh=mesh,
        in_specs=(
            P(None, "group"),
            P("group", "mp"),
            P("group", "mp"),
            P("mp", "group"),
            P("group", None, "mp"),
            P("group", None, "mp"),
            P("group", "mp", None),
            P("group", None, "mp"),
        ),
        out_specs=(P("mp", "group"), P("group", "mp"), P("group", "mp"), P("mp", "group")),
        check_vma=False,
    )
```

profile of v0, /device:TPU:18, one launch (start us, length us, event | category | flops | bytes accessed | tf_op | source)
XLA Modules:
  0.0 743.6 jit_solution(11324365242817237621)
XLA Ops:
  7.2 0.0 copy-start
  7.2 0.0 all-reduce.7.cloned.1.call-start
  7.2 0.0 copy-start.7
  7.2 0.0 copy-start.11
  7.2 6.5 fusion.30
  13.8 4.2 fusion.31
  18.0 0.0 all-reduce.7.cloned.1.call-update
  18.0 0.0 reduce-scatter.3.cloned.1.call-start
  18.1 152.4 %all-reduce.7.cloned.1.call-done = (f32[640,1376]{0,1:T(8,128)}, f32[640,1376]{0,1:T(8,128)}) async-done(((f32[640,1376]{0,1:T(8,128)}, f32[640,1376]{0,1:T(8,128)}), (f32[640,1376]{0,1:T(8,128)}, f32[640,1376]{0,1:T(8,128)})) %all-reduce.7.cloned.1.call-update) | async-done | bytes 7045136 | tf_op jit(solution)/shard_map/psum | solution.py:27
  170.5 4.0 multiply_convert_fusion.3
  174.5 1.3 copy-done.5
  175.8 3.8 fusion.32
  179.6 0.0 reduce-scatter.3.cloned.1.call-update
  179.6 0.0 all-gather.6.cloned.1.call-start
  179.6 0.7 all-gather.6.cloned.1.call-update
  180.3 0.0 all-gather.4.cloned.1.call-start
  180.4 31.6 %reduce-scatter.3.cloned.1.call-done = f32[80,1024]{1,0:T(8,128)} async-done(((f32[640,1024]{1,0:T(8,128)}), f32[80,1024]{1,0:T(8,128)}) %reduce-scatter.3.cloned.1.call-update) | async-done | bytes 327696 | tf_op jit(solution)/shard_map/reduce_scatter | solution.py:31
  212.0 1.0 add_convert_fusion.1
  213.1 13.1 %all_gather.10 = bf16[80,4096]{1,0:T(8,128)(2,1)} all-gather(bf16[80,1024]{1,0:T(8,128)(2,1)S(1)} %add_convert_fusion.1), channel_id=1, replica_groups=mesh['group'=4,'mp'=8] {'group'}, dimensions={1}, use_global_device_ids=true | all-gather | bytes 819200 | tf_op jit(solution)/shard_map/all_gather | solution.py:35
  226.2 0.0 all-gather.4.cloned.1.call-update
  226.2 0.3 all-reduce.5.cloned.1.call-start
  226.4 46.7 %all-gather.6.cloned.1.call-done = bf16[1,640,4096]{2,1,0:T(8,128)(2,1)} async-done(((bf16[1,640,512]{2,1,0:T(8,128)(2,1)}), bf16[1,640,4096]{2,1,0:T(8,128)(2,1)}) %all-gather.6.cloned.1.call-update) | async-done | bytes 5242896 | tf_op jit(solution)/shard_map/all_gather | solution.py:41
  273.2 14.5 %fusion.8 = f32[640,1376]{0,1:T(8,128)} fusion(bf16[1,1376,4096]{2,1,0:T(8,128)(2,1)} %param.14, bf16[1,640,4096]{2,1,0:T(8,128)(2,1)} %all-gather.6.cloned.1.call-done), kind=kOutput, calls=%fused_computation.8 | convolution fusion | flops 7214202880 | bytes 20037632 | tf_op jit(solution)/shard_map/dot_general | solution.py:13
  287.7 41.9 %all-gather.4.cloned.1.call-done = bf16[640,4096]{1,0:T(8,128)(2,1)} async-done(((bf16[80,4096]{1,0:T(8,128)(2,1)}), bf16[640,4096]{1,0:T(8,128)(2,1)}) %all-gather.4.cloned.1.call-update) | async-done | bytes 5242896 | tf_op jit(solution)/shard_map/all_gather | solution.py:36
  329.5 14.9 %fusion.2 = f32[640,1376]{0,1:T(8,128)} fusion(bf16[640,4096]{1,0:T(8,128)(2,1)} %all-gather.4.cloned.1.call-done, bf16[1,4096,1376]{1,2,0:T(8,128)(2,1)} %param.12), kind=kOutput, calls=%fused_computation.2 | convolution fusion | flops 7214202880 | bytes 20037632 | tf_op jit(solution)/shard_map/dot_general | solution.py:42
  344.4 48.6 %fusion = f32[640,4096]{1,0:T(8,128)} fusion(bf16[1,4096,1376]{1,2,0:T(8,128)(2,1)} %param.12, f32[640,1376]{0,1:T(8,128)} %fusion.2, f32[640,1376]{0,1:T(8,128)} %fusion.8, bf16[640,4096]{1,0:T(8,128)(2,1)} %all-gather.4.cloned.1.call-done, bf16[1,4096,1376]{1,2,0:T(8,128)(2,1)} %param.13), kind=kOutput, calls=%fused_computation | convolution fusion | flops 14437212160 | bytes 45318144 | tf_op jit(solution)/shard_map/dot_general | solution.py:13
  393.0 17.4 %fusion.10 = f32[640,4096]{1,0:T(8,128)} fusion(f32[640,4096]{1,0:T(8,128)} %fusion, bf16[1,4096,1376]{1,2,0:T(8,128)(2,1)} %param.13, f32[640,1376]{0,1:T(8,128)} %fusion.8, f32[640,1376]{0,1:T(8,128)} %fusion.2), kind=kOutput, calls=%fused_computation.10 | convolution fusion | flops 7222108160 | bytes 39288832 | tf_op jit(solution)/shard_map/dot_general | solution.py:13
  410.4 2.6 fusion.27
  413.0 176.9 %all-reduce.8 = bf16[640,4096]{1,0:T(8,128)(2,1)} all-reduce(f32[640,4096]{1,0:T(8,128)} %fusion.27), channel_id=1, replica_groups=mesh['group'=4,'mp'=8] {'group','mp'}, use_global_device_ids=true, to_apply=%region_3.4 | all-reduce | flops 2621440 | bytes 15728640 | tf_op jit(solution)/shard_map/psum | solution.py:54
  589.9 1.4 dynamic-slice_convert_fusion
  591.4 1.1 copy-done.10
  592.4 4.2 fusion.33
  596.6 0.0 all-reduce.5.cloned.1.call-update
  596.6 0.0 reduce-scatter.5.cloned.1.call-start
  596.7 93.5 %all-reduce.5.cloned.1.call-done = f32[640,1376]{0,1:T(8,128)} async-done(((f32[640,1376]{0,1:T(8,128)}), f32[640,1376]{0,1:T(8,128)}) %all-reduce.5.cloned.1.call-update) | async-done | bytes 3522576 | tf_op jit(solution)/shard_map/psum | solution.py:58
  690.2 5.3 multiply_convert_fusion
  695.6 0.0 copy-start.3
  695.6 0.0 copy-start.8
  695.6 2.3 fusion.34
  697.9 0.7 copy-done.8
  698.6 3.8 convolution_add_fusion
  702.4 0.0 reduce-scatter.5.cloned.1.call-update
  702.5 0.0 copy-start.4
  702.5 6.8 fusion.35
  709.3 4.9 convolution_bitcast_fusion
  714.2 4.9 convolution_bitcast_fusion.1
  719.1 15.5 %reduce-scatter.5.cloned.1.call-done = f32[80,1024]{1,0:T(8,128)} async-done(((f32[640,1024]{1,0:T(8,128)}), f32[80,1024]{1,0:T(8,128)}) %reduce-scatter.5.cloned.1.call-update) | async-done | bytes 327696 | tf_op jit(solution)/shard_map/reduce_scatter | solution.py:65
  734.6 1.7 add_convert_fusion
  (17 shorter events, 0.0 us)
Async XLA Ops:
  7.2 168.6 %copy-start = (bf16[1376,1024]{1,0:T(8,128)(2,1)S(1)}, bf16[1376,1024]{1,0:T(8,128)(2,1)}, u32[]{:S(2)}) copy-start(bf16[1376,1024]{1,0:T(8,128)(2,1)} %param.11) | copy-start | bytes 8454148
  7.2 163.3 %all-reduce.7.cloned.1.call-start = ((), (), s32[]{:S(2)}) async-start(), calls=%async_computation.7 | async-start | bytes 14090240 | tf_op jit(solution)/shard_map/psum | solution.py:27
  7.2 6.5 copy-start.7
  7.2 6.5 copy-start.11
  18.0 194.0 %reduce-scatter.3.cloned.1.call-start = ((), (), s32[]{:S(2)}) async-start(), calls=%async_computation.2 | async-start | bytes 2949120 | tf_op jit(solution)/shard_map/reduce_scatter | solution.py:31
  174.5 1.3 copy-start.5
  179.6 93.6 %all-gather.6.cloned.1.call-start = ((), (), s32[]{:S(2)}) async-start(), calls=%async_computation.6 | async-start | bytes 5898240 | tf_op jit(solution)/shard_map/all_gather | solution.py:41
  180.3 149.2 %all-gather.4.cloned.1.call-start = ((), (), s32[]{:S(2)}) async-start(), calls=%async_computation.3 | async-start | bytes 5898240 | tf_op jit(solution)/shard_map/all_gather | solution.py:36
  226.2 464.1 %all-reduce.5.cloned.1.call-start = ((), (), s32[]{:S(2)}) async-start(), calls=%async_computation.4 | async-start | bytes 7045120 | tf_op jit(solution)/shard_map/psum | solution.py:58
  393.0 17.4 %copy-start.9 = (bf16[1,640,512]{2,1,0:T(8,128)(2,1)S(1)}, bf16[1,640,512]{2,1,0:T(8,128)(2,1)}, u32[]{:S(2)}) copy-start(bf16[1,640,512]{2,1,0:T(8,128)(2,1)} %param.15) | copy-start | bytes 1966084
  591.4 1.1 copy-start.10
  596.6 138.0 %reduce-scatter.5.cloned.1.call-start = ((), (), s32[]{:S(2)}) async-start(), calls=%async_computation.5 | async-start | bytes 2949120 | tf_op jit(solution)/shard_map/reduce_scatter | solution.py:65
  690.2 5.3 copy-start.6
  695.5 2.3 copy-start.1
  695.6 2.3 copy-start.3
  695.6 3.1 copy-start.8
  702.5 6.9 copy-start.4
  702.5 6.9 copy-start.12
  709.3 4.9 copy-start.2
Sparse Core Ops, SparseCore 0:
  18.1 152.3 all-reduce.6
  179.7 32.2 reduce-scatter.2
  213.6 59.5 all-gather.5
  274.7 54.8 all-gather.3
  596.8 93.4 all-reduce.4
  702.6 31.9 reduce-scatter.4
where the time goes:
time: 757 us; the launch traced here: 744 us
  waiting for transfers between devices  382 us (50%)
  blocking collectives  190 us (25%)
  matrix products  137 us (18%)
  other arithmetic  14.7 us (2%)
  between operations  14.7 us (2%)
    psum x1, blocking collectives, body(): total_sum = lax.psum(partial_sum, ('group', 'mp'))  177 us
    psum x1, waiting for transfers between devices, body(): gate_t, up_t = lax.psum((gate_part, up_part), 'group')  152 us
    psum x1, waiting for transfers between devices, body(): ghid_t = lax.psum(back_part, 'group')  93.5 us
    dot_general x6, matrix products, contract_last(): lax.dot_general(left, right, (((1,), (1,)), ((), ())), preferred_element_...  90.7 us
    all_gather x1, waiting for transfers between devices, body(): cot_full = lax.all_gather(cot_local, 'mp', axis=1, tiled=True)  46.7 us
    all_gather x1, waiting for transfers between devices, body(): trunk_out = lax.all_gather(wide_rows, 'mp', axis=0, tiled=True)  41.9 us
    reduce_scatter x1, waiting for transfers between devices, body(): lax.psum_scatter(down_part, 'mp', scatter_dimension=0, tiled=True)  31.6 us
    dot_general x3, matrix products, contract_first(): lax.dot_general(left, right, (((0,), (0,)), ((), ())), preferred_element_...  16.6 us
  transfers between devices with their start and end apart: 6, of which 6 were waited for; matrix products, arithmetic and copies ran while one was open for 4% of the time, Pallas kernels for 0%

commit v1 on v0

v1 whole, which is shorter than its diff:
```python
import functools

import jax
import jax.numpy as jnp
from jax import lax
from jax.experimental import pallas as pl
from jax.experimental.pallas import tpu as pltpu
from jax.sharding import PartitionSpec as P

BF = jnp.bfloat16
F32 = jnp.float32
MIB = 1 << 20


def silu_grad(pre_act):
    sig = jax.nn.sigmoid(pre_act)
    return sig * (1.0 + pre_act * (1.0 - sig))


def dot(left, right, dims):
    return lax.dot_general(left, right, (dims, ((), ())), preferred_element_type=F32)


def dot_nt(left, right):
    return dot(left, right, ((1,), (1,)))


def dot_nn(left, right):
    return dot(left, right, ((1,), (0,)))


def row(stack, index):
    return lax.dynamic_index_in_dim(stack, index, 0, keepdims=False)


def whole(shape):
    return pl.BlockSpec(shape, lambda *_: (0,) * len(shape))


def call(kernel, name, grid, index, in_specs, out_specs, out_shape, operands, flops, vmem, scratch=()):
    moved = sum(o.size * o.dtype.itemsize for o in operands)
    return pl.pallas_call(
        kernel,
        grid_spec=pltpu.PrefetchScalarGridSpec(
            num_scalar_prefetch=1, grid=grid, in_specs=in_specs, out_specs=out_specs, scratch_shapes=scratch
        ),
        out_shape=out_shape,
        name=name,
        cost_estimate=pl.CostEstimate(flops=flops, bytes_accessed=moved, transcendentals=0),
        compiler_params=pltpu.CompilerParams(vmem_limit_bytes=vmem * MIB),
    )(index, *operands)


class Plan:
    def __init__(self, mesh):
        self.groups = mesh.shape["group"]
        self.members = mesh.shape["mp"]
        self.places = self.members // 2

    def group_swap(self, value, mask):
        return lax.ppermute(value, "group", [(i, i ^ mask) for i in range(self.groups)])

    def core_swap(self, value):
        return lax.ppermute(value, "mp", [(i, i ^ 1) for i in range(self.members)])

    def place_swap(self, value, mask):
        return lax.ppermute(value, "mp", [(i, i ^ (2 * mask)) for i in range(self.members)])

    def gather(self, pair):
        have = {0: pair}
        if self.groups == 4:
            have[1] = self.group_swap(pair, 1)
            have[2] = self.group_swap(pair, 2)
            have[3] = (self.group_swap(have[2][0], 1), self.group_swap(have[1][1], 2))
        else:
            for k in range(1, self.groups):
                have[k] = self.group_swap(pair, k)
        return have

    def scatter(self, parts):
        if self.groups == 4:
            first = self.group_swap(parts[3][0].astype(BF), 1)
            second = self.group_swap(parts[3][1].astype(BF), 2)
            to_x = jnp.stack([parts[1][0].astype(F32), parts[1][1].astype(F32) + second.astype(F32)])
            to_y = jnp.stack([parts[2][0].astype(F32) + first.astype(F32), parts[2][1].astype(F32)])
            came_x = self.group_swap(to_x.astype(BF), 1)
            came_y = self.group_swap(to_y.astype(BF), 2)
            return parts[0].astype(F32) + (came_x.astype(F32) + came_y.astype(F32))
        total = parts[0].astype(F32)
        for k in range(1, self.groups):
            total = total + self.group_swap(parts[k].astype(BF), k).astype(F32)
        return total

    def halving(self, keep, send, first):
        current = keep.astype(F32) + self.group_swap(send, first).astype(F32)
        keys = [k for k in range(self.groups) if not k & first]
        current = {k: current[i] for i, k in enumerate(keys)}
        mask = 1
        while mask < self.groups:
            if mask != first:
                keys = [k for k in current if not k & mask]
                came = self.group_swap(jnp.stack([current[k | mask] for k in keys]).astype(BF), mask)
                current = {k: current[k] + came[i].astype(F32) for i, k in enumerate(keys)}
            mask *= 2
        return current[0]

    def place_sum(self, parts, me):
        total = row(parts, me).astype(F32)
        for mask in range(1, self.places):
            total = total + self.place_swap(row(parts, me ^ mask).astype(BF), mask).astype(F32)
        return total

    def place_gather(self, piece, me):
        out = jnp.zeros((self.places,) + piece.shape, piece.dtype)
        out = lax.dynamic_update_index_in_dim(out, piece, me, 0)
        for mask in range(1, self.places):
            out = lax.dynamic_update_index_in_dim(out, self.place_swap(piece, mask), me ^ mask, 0)
        return out


def chunks_kernel(order, index, *refs):
    n = len(order)
    value = jnp.concatenate([refs[k][...] for k in order], 0)
    product = dot_nt(value, refs[n][...])
    first, second = refs[n + 1], refs[n + 2]
    half = product.shape[0] // 2
    first[...] = product[:half].astype(BF)
    second[...] = product[half:].astype(BF)


def chunks_product(index, value, weight_t, order, name):
    n = len(order)
    rows, depth = value.shape
    units = weight_t.shape[0]
    share = rows // n
    specs = [pl.BlockSpec((share, depth), lambda i, index, k=k: (index[k], 0)) for k in range(n)]
    shape = (rows // 2, units)
    first, second = call(
        functools.partial(chunks_kernel, order),
        name,
        (1,),
        index,
        specs + [whole(weight_t.shape)],
        [whole(shape)] * 2,
        [jax.ShapeDtypeStruct(shape, BF)] * 2,
        [value] * n + [weight_t],
        2 * rows * depth * units,
        32,
    )
    return first.reshape(n // 2, share, units), second.reshape(n // 2, share, units)


def ghid_kernel(index, cot, weight, out):
    product = dot_nt(cot[0], weight[...])

    @pl.when(pl.program_id(0) == 0)
    def _():
        out[...] = product

    @pl.when(pl.program_id(0) > 0)
    def _():
        out[...] += product


def ghid_product(index, cot, weight):
    parts, rows, depth = cot.shape
    units = weight.shape[0]
    return call(
        ghid_kernel,
        "head_hidden_grad",
        (parts,),
        index,
        [
            pl.BlockSpec((1, rows, depth), lambda i, index: (i, 0, 0)),
            pl.BlockSpec((units, depth), lambda i, index: (0, i)),
        ],
        whole((rows, units)),
        jax.ShapeDtypeStruct((rows, units), F32),
        [cot, weight],
        2 * rows * units * depth * parts,
        40,
    )


def pre_kernel(n, index, *refs):
    pieces, (gate_w, up_w, pre, lin) = refs[:n], refs[n:]
    per = 2
    for j in range(n // per):

        @pl.when(pl.program_id(0) == j)
        def _(j=j):
            value = jnp.concatenate([p[...] for p in pieces[per * j : per * j + per]], 0)
            a, b = dot_nt(value, gate_w[...]), dot_nt(value, up_w[...])
            if j == 0:
                pre[...] = a
                lin[...] = b
            else:
                pre[...] += a
                lin[...] += b


def pre_product(index, pieces, gate_t, up_t):
    flat = [piece for k in range(len(pieces)) for piece in pieces[k]]
    half, depth = flat[0].shape
    units = gate_t.shape[0]
    weight = pl.BlockSpec((units, depth), lambda i, index: (0, index[i]))
    shape = jax.ShapeDtypeStruct((2 * half, units), F32)
    return call(
        functools.partial(pre_kernel, len(flat)),
        "head_pre_first",
        (len(pieces),),
        index,
        [whole((half, depth))] * len(flat) + [weight] * 2,
        [whole((2 * half, units))] * 2,
        [shape] * 2,
        flat + [gate_t, up_t],
        8 * half * depth * units * len(pieces),
        56,
    )


def act_kernel(index, own, mate, gate_w, up_w, pre, lin, ghid_own, ghid_mate, dgate, dup):
    half = own.shape[0]
    value = jnp.concatenate([own[...], mate[...]], 0)
    gate = pre[...] + dot_nt(value, gate_w[...])
    up = lin[...] + dot_nt(value, up_w[...])
    for side, ghid in enumerate((ghid_own, ghid_mate)):
        rows = slice(side * half, side * half + half)
        g, u, h = gate[rows], up[rows], ghid[0]
        sig = jax.nn.sigmoid(g)
        dgate[rows] = (h * u * (sig * (1.0 + g * (1.0 - sig)))).astype(BF)
        dup[rows] = (h * (g * sig)).astype(BF)


def act_product(index, offset, own, mate, gate_t, up_t, pre, lin, ghid, core_at):
    half, depth = own.shape
    units = gate_t.shape[0]
    weight = pl.BlockSpec((units, depth), lambda i, index: (0, index[offset]))
    ghid = ghid.reshape(2, half, units)
    ghid_own = pl.BlockSpec((1, half, units), lambda i, index: (index[core_at], 0, 0))
    ghid_mate = pl.BlockSpec((1, half, units), lambda i, index: (index[core_at + 1], 0, 0))
    return call(
        act_kernel,
        "head_act",
        (1,),
        index,
        [whole((half, depth))] * 2 + [weight] * 2 + [whole((2 * half, units))] * 2 + [ghid_own, ghid_mate],
        [whole((2 * half, units))] * 2,
        [jax.ShapeDtypeStruct((2 * half, units), BF)] * 2,
        [own, mate, gate_t, up_t, pre, lin, ghid, ghid],
        8 * half * depth * units,
        56,
    )


def back_kernel(places, place_at, index, dgate, dup, gate_w, up_w, cot, own, mate):
    product = dot_nn(dgate[...], gate_w[...]) + dot_nn(dup[...], up_w[...])
    half, depth = product.shape[0] // 2, product.shape[1]
    mate[0] = product[half:].astype(BF)
    extra = jnp.concatenate([cot[j, 0] for j in range(cot.shape[0])], 1).astype(F32)
    rows = product[:half].reshape(places, half // places, depth)
    at = lax.broadcasted_iota(jnp.int32, rows.shape, 0)
    rows = rows + jnp.where(at == index[place_at], extra[None], 0.0)
    own[0] = rows.reshape(half, depth).astype(BF)


def back_product(index, offset, count, dgate, dup, gate_t, up_t, cot, places, core_at):
    rows, units = dgate.shape
    parts, _, cot_width = cot.shape
    per = gate_t.shape[1] // cot_width
    groups = core_at
    depth = gate_t.shape[1] // groups
    per = depth // cot_width
    half = rows // 2
    cot = cot.reshape(parts, 2 * places, half // places, cot_width)
    weight = pl.BlockSpec((units, depth), lambda i, index: (0, index[offset + i]))
    cot_spec = pl.BlockSpec(
        (per, 1, half // places, cot_width), lambda i, index: (index[offset + i], index[core_at + 2], 0, 0)
    )
    out = pl.BlockSpec((1, half, depth), lambda i, index: (i, 0, 0))
    return call(
        functools.partial(back_kernel, places, core_at + 3),
        "head_back",
        (count,),
        index,
        [whole((rows, units))] * 2 + [weight] * 2 + [cot_spec],
        [out] * 2,
        [jax.ShapeDtypeStruct((count, half, depth), BF)] * 2,
        [dgate, dup, gate_t, up_t, cot],
        4 * rows * units * depth * count,
        48,
    )


def make_body(plan):
    groups, places = plan.groups, plan.places

    def body(tokens, trunk_gate, trunk_up, trunk_down, head_gate, head_up, head_down, head_grads):
        g = lax.axis_index("group")
        m = lax.axis_index("mp")
        z, c = m // 2, m % 2
        total_rows, width = tokens.shape
        rows = total_rows // plan.members
        units = trunk_gate.shape[1]
        half_rows = places * rows
        share = total_rows // groups
        offsets = [g ^ k for k in range(groups)]
        index = jnp.stack(offsets + [c, 1 - c, c * places + z, z]).astype(jnp.int32)

        toks = tokens.reshape(places, 2, rows, width).transpose(1, 0, 2, 3)
        own_tok = row(row(toks, c), z)
        toks = toks.reshape(total_rows, width)
        cot_width = head_grads.shape[2]
        cot_own = head_grads[0].reshape(places, 2, rows, cot_width).transpose(1, 0, 2, 3)
        cot_own, toks = lax.optimization_barrier((cot_own.reshape(total_rows, cot_width), toks))
        cot = lax.all_gather(cot_own, "mp", axis=0, tiled=False)

        def in_order(pieces):
            out = jnp.zeros((groups, 2, share // 2, units), BF)
            for k, pair in pieces.items():
                if isinstance(pair, tuple):
                    for side in range(2):
                        out = lax.dynamic_update_slice(out, pair[side][None, None], (g ^ k, side, 0, 0))
                else:
                    out = lax.dynamic_update_slice(out, pair[None], (g ^ k, 0, 0, 0))
            return out.reshape(total_rows, units)

        def order(first):
            return [k for k in range(groups) if not k & first] + [k for k in range(groups) if k & first]

        gate_keep, gate_send = chunks_product(index, toks, trunk_gate.T, order(1), "trunk_gate")
        up_keep, up_send = chunks_product(index, toks, trunk_up.T, order(2), "trunk_up")
        gate_r = plan.halving(gate_keep, gate_send, 1)
        up_r = plan.halving(up_keep, up_send, 2)
        hid_r = (jax.nn.silu(gate_r) * up_r).astype(BF)
        hidden = in_order(plan.gather(hid_r.reshape(2, share // 2, units)))
        down = dot_nn(hidden, trunk_down).astype(BF).reshape(2, half_rows, width)
        came = plan.core_swap(row(down, 1 - c))
        part = (row(down, c).astype(F32) + came.astype(F32)).astype(BF)
        summed = plan.place_sum(part.reshape(places, rows, width), z)
        shard = (own_tok.astype(F32) + summed).astype(BF)
        block = plan.place_gather(shard, z).reshape(2, half_rows // 2, width)

        wide = plan.gather(block)
        pieces = {}
        for k, pair in wide.items():
            if isinstance(pair, tuple):
                pair = jnp.stack(pair)
            own = pair.reshape(half_rows, width)
            pieces[k] = (own, plan.core_swap(own))

        gate_t, up_t = head_gate[0].T, head_up[0].T
        ghid = ghid_product(index, cot, head_down[0])
        last = groups - 1
        pre, lin = pre_product(index, {k: pieces[k] for k in range(last)}, gate_t, up_t)
        dgate, dup = act_product(index, last, *pieces[last], gate_t, up_t, pre, lin, ghid, groups)

        parts = {}
        for offset, count in ((last, 1), (1, last - 1), (0, 1)):
            own, mate = back_product(index, offset, count, dgate, dup, gate_t, up_t, cot, places, groups)
            came = plan.core_swap(mate)
            for i in range(count):
                total = own[i].astype(F32) + came[i].astype(F32)
                parts[offset + i] = total.reshape(2, half_rows // 2, width)
        cols = plan.scatter(parts)
        dshard = plan.place_sum(cols.astype(BF).reshape(places, rows, width), z).astype(BF)
        dhalf = plan.place_gather(dshard, z).reshape(half_rows, width)
        dmate = plan.core_swap(dhalf)
        grad_mid = jnp.zeros((2, half_rows, width), BF)
        grad_mid = lax.dynamic_update_index_in_dim(grad_mid, dhalf, c, 0)
        grad_mid = lax.dynamic_update_index_in_dim(grad_mid, dmate, 1 - c, 0).reshape(total_rows, width)

        low, high = chunks_product(index, grad_mid, trunk_down, list(range(groups)), "trunk_hidden_grad")
        back = jnp.concatenate([low, high], 0).reshape(groups, 2, share // 2, units)
        ghid_t = plan.scatter({k: back[k] for k in range(groups)}).reshape(share, units)
        dgate_r = (ghid_t * up_r * silu_grad(gate_r)).astype(BF)
        dup_r = (ghid_t * jax.nn.silu(gate_r)).astype(BF)
        both = plan.gather(jnp.stack([dgate_r, dup_r]))
        dgate_t = jnp.zeros((groups, share, units), BF)
        dup_t = jnp.zeros((groups, share, units), BF)
        for k, pair in both.items():
            dgate_t = lax.dynamic_update_index_in_dim(dgate_t, pair[0], g ^ k, 0)
            dup_t = lax.dynamic_update_index_in_dim(dup_t, pair[1], g ^ k, 0)
        dgate_t = dgate_t.reshape(total_rows, units)
        dup_t = dup_t.reshape(total_rows, units)
        back_in = (dot_nt(dgate_t, trunk_gate) + dot_nt(dup_t, trunk_up)).astype(BF)
        back_in = back_in.reshape(2, half_rows, width)
        came = plan.core_swap(row(back_in, 1 - c))
        part = (row(back_in, c).astype(F32) + came.astype(F32)).astype(BF)
        summed = plan.place_sum(part.reshape(places, rows, width), z)
        grad_x = (dshard.astype(F32) + summed).astype(BF)
        grad_gate = dot(toks, dgate_t, ((0,), (0,)))
        grad_up = dot(toks, dup_t, ((0,), (0,)))
        grad_down = dot(hidden, grad_mid, ((0,), (0,)))
        return (grad_x, grad_gate, grad_up, grad_down)

    return body


def solution(mesh):
    return jax.shard_map(
        make_body(Plan(mesh)),
        mesh=mesh,
        in_specs=(
            P(None, "group"),
            P("group", "mp"),
            P("group", "mp"),
            P("mp", "group"),
            P("group", None, "mp"),
            P("group", None, "mp"),
            P("group", "mp", None),
            P("group", None, "mp"),
        ),
        out_specs=(P("mp", "group"), P("group", "mp"), P("group", "mp"), P("mp", "group")),
        check_vma=False,
    )
```

time: 757 us -> 401 us (0.53)
  blocking collectives: 190 us -> 0 us
  waiting for transfers between devices: 382 us -> 202 us
  matrix products: 137 us -> 21.6 us
  Pallas kernels: 0 us -> 86.1 us
  starting transfers between devices: 0.46 us -> 38.7 us
  local copies, waits for them, and re-layouts: 4.55 us -> 18.8 us
    psum x2 -> x0, waiting for transfers between devices: 246 us -> none  [the longest x1 152 us: body(): gate_t, up_t = lax.psum((gate_part, up_part), 'group')]
    ppermute x0 -> x49, waiting for transfers between devices: none -> 202 us  [the longest x24 135 us: group_swap(): lax.ppermute(value, 'group', [(i, i ^ mask) for i in range(self.groups)])]
    psum x1 -> x0, blocking collectives: 177 us -> none  [body(): total_sum = lax.psum(partial_sum, ('group', 'mp'))]
    dot_general x13 -> x6, matrix products: 137 us -> 21.6 us  [dot(): lax.dot_general(left, right, (dims, ((), ())), preferred_element_type=F32)]
    all_gather x2 -> x1, waiting for transfers between devices: 88.6 us -> 0.01 us  [body(): cot = lax.all_gather(cot_own, 'mp', axis=0, tiled=False)]
    pallas_call x0 -> x9, Pallas kernels: none -> 86.1 us  [call(): pl.pallas_call(kernel, grid_spec=pltpu.PrefetchScalarGridSpec(num_scalar_...]
    reduce_scatter x2 -> x0, waiting for transfers between devices: 47.1 us -> none  [the longest x1 31.6 us: body(): lax.psum_scatter(down_part, 'mp', scatter_dimension=0, tiled=True)]
    ppermute x0 -> x49, starting transfers between devices: none -> 38.7 us  [the longest x24 18.8 us: group_swap(): lax.ppermute(value, 'group', [(i, i ^ mask) for i in range(self.groups)])]
  transfers between devices with their start and end apart: 6 -> 50, of which waited for: 6 -> 36; matrix products, arithmetic and copies ran while one was open for 4% -> 8% of each run, Pallas kernels for 0% -> 15%
where the time goes in v1:
time: 401 us; the launch traced here: 394 us
  waiting for transfers between devices  202 us (50%)
  Pallas kernels  86.1 us (21%)
  starting transfers between devices  38.7 us (10%)
  matrix products  21.6 us (5%)
  local copies, waits for them, and re-layouts  18.8 us (5%)
  between operations  15.3 us (4%)
  other arithmetic  10.9 us (3%)
    ppermute x24, waiting for transfers between devices, group_swap(): lax.ppermute(value, 'group', [(i, i ^ mask) for i in range(self.groups)])  135 us
    pallas_call x9, Pallas kernels, call(): pl.pallas_call(kernel, grid_spec=pltpu.PrefetchScalarGridSpec(num_scalar_...  86.1 us
    ppermute x15, waiting for transfers between devices, place_swap(): lax.ppermute(value, 'mp', [(i, i ^ 2 * mask) for i in range(self.members)])  62.8 us
    dot_general x6, matrix products, dot(): lax.dot_general(left, right, (dims, ((), ())), preferred_element_type=F32)  21.6 us
    ppermute x24, starting transfers between devices, group_swap(): lax.ppermute(value, 'group', [(i, i ^ mask) for i in range(self.groups)])  18.8 us
    ppermute x15, starting transfers between devices, place_swap(): lax.ppermute(value, 'mp', [(i, i ^ 2 * mask) for i in range(self.members)])  18.6 us
    unnamed x50, local copies, waits for them, and re-layouts  12.6 us
  transfers between devices with their start and end apart: 50, of which 36 were waited for; matrix products, arithmetic and copies ran while one was open for 8% of the time, Pallas kernels for 15%

profile of v1, /device:TPU:18, one launch (start us, length us, event | category | flops | bytes accessed | tf_op | source)
XLA Modules:
  0.0 393.9 jit_solution(775267989378753374)
XLA Ops:
  11.6 3.7 trunk_up.1
  16.8 3.7 trunk_gate.1
  21.1 16.2 %collective-permute-done.2 = bf16[2,160,1376]{2,1,0:T(8,128)(2,1)} collective-permute-done((bf16[2,160,1376]{2,1,0:T(8,128)(2,1)}, bf16[2,160,1376]{2,1,0:T(8,128)(2,1)}, u32[]{:S(2)}, u32[]{:S(2)}) %collective-permute-start.2) | collective-permute-done | bytes 880672 | tf_op jit(solution)/shard_map/ppermute | solution.py:61
  39.3 4.4 %collective-permute-done = bf16[2,160,1376]{2,1,0:T(8,128)(2,1)} collective-permute-done((bf16[2,160,1376]{2,1,0:T(8,128)(2,1)}, bf16[2,160,1376]{2,1,0:T(8,128)(2,1)}, u32[]{:S(2)}, u32[]{:S(2)}) %collective-permute-start) | collective-permute-done | bytes 880672 | tf_op jit(solution)/shard_map/ppermute | solution.py:61
  45.2 6.6 %collective-permute-done.3 = bf16[1,160,1376]{2,1,0:T(8,128)(2,1)S(1)} collective-permute-done((bf16[1,160,1376]{2,1,0:T(8,128)(2,1)S(1)}, bf16[1,160,1376]{2,1,0:T(8,128)(2,1)S(1)}, u32[]{:S(2)}, u32[]{:S(2)}) %collective-permute-start.3) | collective-permute-done | bytes 440352 | tf_op jit(solution)/shard_map/ppermute | solution.py:61
  51.9 3.1 collective-permute-done.1
  56.5 8.7 %collective-permute-done.5 = bf16[2,80,1376]{2,1,0:T(8,128)(2,1)S(1)} collective-permute-done((bf16[2,80,1376]{2,1,0:T(8,128)(2,1)S(1)}, bf16[2,80,1376]{2,1,0:T(8,128)(2,1)S(1)}, u32[]{:S(2)}, u32[]{:S(2)}) %collective-permute-start.5) | collective-permute-done | bytes 440352 | tf_op jit(solution)/shard_map/ppermute | solution.py:61
  67.9 3.5 collective-permute-done.6
  73.5 2.2 convolution_convert_fusion
  77.6 2.4 collective-permute-done.8
  83.3 2.7 collective-permute-start.11
  87.6 7.6 %collective-permute-done.10 = bf16[80,1024]{1,0:T(8,128)(2,1)S(1)} collective-permute-done((bf16[80,1024]{1,0:T(8,128)(2,1)}, bf16[80,1024]{1,0:T(8,128)(2,1)S(1)}, u32[]{:S(2)}, u32[]{:S(2)}) %collective-permute-start.10) | collective-permute-done | bytes 163872 | tf_op jit(solution)/shard_map/ppermute | solution.py:67
  95.2 5.8 %collective-permute-done.11 = bf16[80,1024]{1,0:T(8,128)(2,1)S(1)} collective-permute-done((bf16[80,1024]{1,0:T(8,128)(2,1)}, bf16[80,1024]{1,0:T(8,128)(2,1)S(1)}, u32[]{:S(2)}, u32[]{:S(2)}) %collective-permute-start.11) | collective-permute-done | bytes 163872 | tf_op jit(solution)/shard_map/ppermute | solution.py:67
  103.5 2.4 collective-permute-start.14
  105.8 3.6 collective-permute-done.12
  109.5 5.5 %collective-permute-done.13 = bf16[80,1024]{1,0:T(8,128)(2,1)S(1)} collective-permute-done((bf16[80,1024]{1,0:T(8,128)(2,1)S(1)}, bf16[80,1024]{1,0:T(8,128)(2,1)S(1)}, u32[]{:S(2)}, u32[]{:S(2)}) %collective-permute-start.13) | collective-permute-done | bytes 163872 | tf_op jit(solution)/shard_map/ppermute | solution.py:67
  115.0 5.0 %collective-permute-done.14 = bf16[80,1024]{1,0:T(8,128)(2,1)S(1)} collective-permute-done((bf16[80,1024]{1,0:T(8,128)(2,1)S(1)}, bf16[80,1024]{1,0:T(8,128)(2,1)S(1)}, u32[]{:S(2)}, u32[]{:S(2)}) %collective-permute-start.14) | collective-permute-done | bytes 163872 | tf_op jit(solution)/shard_map/ppermute | solution.py:67
  120.9 15.1 %collective-permute-done.17 = bf16[2,160,1024]{2,1,0:T(8,128)(2,1)S(1)} collective-permute-done((bf16[2,160,1024]{2,1,0:T(8,128)(2,1)S(1)}, bf16[2,160,1024]{2,1,0:T(8,128)(2,1)S(1)}, u32[]{:S(2)}, u32[]{:S(2)}) %collective-permute-start.17) | collective-permute-done | bytes 655392 | tf_op jit(solution)/shard_map/ppermute | solution.py:61
  138.6 7.7 %collective-permute-done.16 = bf16[160,1024]{1,0:T(8,128)(2,1)S(1)} collective-permute-done((bf16[160,1024]{1,0:T(8,128)(2,1)S(1)}, bf16[160,1024]{1,0:T(8,128)(2,1)S(1)}, u32[]{:S(2)}, u32[]{:S(2)}) %collective-permute-start.16) | collective-permute-done | bytes 327712 | tf_op jit(solution)/shard_map/ppermute | solution.py:61
  149.9 20.9 %head_pre_first.1 = (f32[640,1376]{1,0:T(8,128)}, f32[640,1376]{1,0:T(8,128)}) custom-call(s32[8]{0:T(128)} %copy-done.11, bf16[320,1024]{1,0:T(8,128)(2,1)} %bitcast.285, bf16[320,1024]{1,0:T(8,128)(2,1)} %copy-done.22, bf16[320,1024]{1,0:T(8,128)(2,1)} %bitcast.289, bf16[320,1024]{1,0:T(8,128)(2,1)} %copy-done.23, bf16[320,1024]{1,0:T(8,128)(2,1)} %bitcast.291, ...), custom_call_target="tpu_custom_call" | custom-call | flops 10821304320 | bytes 26476544 | tf_op jit(solution)/shard_map/head_pre_first/pallas_call | solution.py:42
  170.9 2.5 copy-done
  173.4 14.5 %head_hidden_grad.1 = f32[640,1376]{1,0:T(8,128)S(1)} custom-call(s32[8]{0:T(128)S(1)} %copy-done.12, bf16[8,640,512]{2,1,0:T(8,128)(2,1)S(1)} %bitcast.230, bf16[1376,4096]{1,0:T(8,128)(2,1)} %bitcast.292), custom_call_target="tpu_custom_call" | custom-call | flops 7214202880 | bytes 16515072 | tf_op jit(solution)/shard_map/head_hidden_grad/pallas_call | solution.py:42
  189.7 13.1 %head_act.1 = (bf16[640,1376]{1,0:T(8,128)(2,1)}, bf16[640,1376]{1,0:T(8,128)(2,1)}) custom-call(s32[8]{0:T(128)} %copy-done.11, bf16[320,1024]{1,0:T(8,128)(2,1)} %bitcast.49.own, bf16[320,1024]{1,0:T(8,128)(2,1)} %collective-permute-done.19.mate, bf16[1376,4096]{1,0:T(8,128)(2,1)} %bitcast.243, bf16[1376,4096]{1,0:T(8,128)(2,1)} %bitcast.248, ...), custom_call_target="tpu_custom_call" | custom-call | flops 3607101440 | bytes 37945344 | tf_op jit(solution)/shard_map/head_act/pallas_call | solution.py:42
  205.8 7.4 %head_back.5 = (bf16[1,320,1024]{2,1,0:T(8,128)(2,1)S(1)}, bf16[1,320,1024]{2,1,0:T(8,128)(2,1)S(1)}) custom-call(s32[8]{0:T(128)S(1)} %copy-done.13, bf16[640,1376]{1,0:T(8,128)(2,1)S(1)} %copy-done.1, bf16[640,1376]{1,0:T(8,128)(2,1)S(1)} %copy-done.2, bf16[1376,4096]{1,0:T(8,128)(2,1)} %bitcast.244, bf16[1376,4096]{1,0:T(8,128)(2,1)} %bitcast.249, ...), custom_call_target="tpu_custom_call" | custom-call | flops 3607101440 | bytes 31309824 | tf_op jit(solution)/shard_map/head_back/pallas_call | solution.py:42
  213.8 12.6 %head_back.4 = (bf16[2,320,1024]{2,1,0:T(8,128)(2,1)S(1)}, bf16[2,320,1024]{2,1,0:T(8,128)(2,1)S(1)}) custom-call(s32[8]{0:T(128)S(1)} %copy-done.13, bf16[640,1376]{1,0:T(8,128)(2,1)S(1)} %copy-done.1, bf16[640,1376]{1,0:T(8,128)(2,1)} %get-tuple-element.31.dup, bf16[1376,4096]{1,0:T(8,128)(2,1)} %bitcast.245, bf16[1376,4096]{1,0:T(8,128)(2,1)} %bitcast.250, ...), custom_call_target="tpu_custom_call" | custom-call | flops 7214202880 | bytes 31309824 | tf_op jit(solution)/shard_map/head_back/pallas_call | solution.py:42
  227.9 7.4 %head_back.3 = (bf16[1,320,1024]{2,1,0:T(8,128)(2,1)S(1)}, bf16[1,320,1024]{2,1,0:T(8,128)(2,1)S(1)}) custom-call(s32[8]{0:T(128)S(1)} %copy-done.13, bf16[640,1376]{1,0:T(8,128)(2,1)S(1)} %copy-done.1, bf16[640,1376]{1,0:T(8,128)(2,1)S(1)} %copy-done.3, bf16[1376,4096]{1,0:T(8,128)(2,1)} %bitcast.246, bf16[1376,4096]{1,0:T(8,128)(2,1)} %bitcast.251, ...), custom_call_target="tpu_custom_call" | custom-call | flops 3607101440 | bytes 31309824 | tf_op jit(solution)/shard_map/head_back/pallas_call | solution.py:42
  238.2 7.7 %collective-permute-done.28 = bf16[160,1024]{1,0:T(8,128)(2,1)S(1)} collective-permute-done((bf16[160,1024]{1,0:T(8,128)(2,1)S(1)}, bf16[160,1024]{1,0:T(8,128)(2,1)S(1)}, u32[]{:S(2)}, u32[]{:S(2)}) %collective-permute-start.28) | collective-permute-done | bytes 327712 | tf_op jit(solution)/shard_map/ppermute | solution.py:61
  247.6 12.0 %collective-permute-done.27 = bf16[2,160,1024]{2,1,0:T(8,128)(2,1)S(1)} collective-permute-done((bf16[2,160,1024]{2,1,0:T(8,128)(2,1)S(1)}, bf16[2,160,1024]{2,1,0:T(8,128)(2,1)S(1)}, u32[]{:S(2)}, u32[]{:S(2)}) %collective-permute-start.27) | collective-permute-done | bytes 655392 | tf_op jit(solution)/shard_map/ppermute | solution.py:61
  259.5 2.5 collective-permute-done.29
  263.5 2.5 collective-permute-start.32
  266.0 3.7 collective-permute-done.30
  269.7 4.7 %collective-permute-done.31 = bf16[80,1024]{1,0:T(8,128)(2,1)S(1)} collective-permute-done((bf16[80,1024]{1,0:T(8,128)(2,1)S(1)}, bf16[80,1024]{1,0:T(8,128)(2,1)S(1)}, u32[]{:S(2)}, u32[]{:S(2)}) %collective-permute-start.31) | collective-permute-done | bytes 163872 | tf_op jit(solution)/shard_map/ppermute | solution.py:67
  274.3 4.1 %collective-permute-done.32 = bf16[80,1024]{1,0:T(8,128)(2,1)S(1)} collective-permute-done((bf16[80,1024]{1,0:T(8,128)(2,1)S(1)}, bf16[80,1024]{1,0:T(8,128)(2,1)S(1)}, u32[]{:S(2)}, u32[]{:S(2)}) %collective-permute-start.32) | collective-permute-done | bytes 163872 | tf_op jit(solution)/shard_map/ppermute | solution.py:67
  282.2 3.6 collective-permute-done.33
  285.8 5.2 %collective-permute-done.34 = bf16[80,1024]{1,0:T(8,128)(2,1)S(1)} collective-permute-done((bf16[80,1024]{1,0:T(8,128)(2,1)S(1)}, bf16[80,1024]{1,0:T(8,128)(2,1)S(1)}, u32[]{:S(2)}, u32[]{:S(2)}) %collective-permute-start.34) | collective-permute-done | bytes 163872 | tf_op jit(solution)/shard_map/ppermute | solution.py:67
  291.0 4.0 %collective-permute-done.35 = bf16[80,1024]{1,0:T(8,128)(2,1)S(1)} collective-permute-done((bf16[80,1024]{1,0:T(8,128)(2,1)S(1)}, bf16[80,1024]{1,0:T(8,128)(2,1)S(1)}, u32[]{:S(2)}, u32[]{:S(2)}) %collective-permute-start.35) | collective-permute-done | bytes 163872 | tf_op jit(solution)/shard_map/ppermute | solution.py:67
  297.3 2.8 trunk_hidden_grad.1
  301.4 6.4 %collective-permute-done.37 = bf16[80,1376]{1,0:T(8,128)(2,1)S(1)} collective-permute-done((bf16[80,1376]{1,0:T(8,128)(2,1)S(1)}, bf16[80,1376]{1,0:T(8,128)(2,1)S(1)}, u32[]{:S(2)}, u32[]{:S(2)}) %collective-permute-start.37) | collective-permute-done | bytes 220192 | tf_op jit(solution)/shard_map/ppermute | solution.py:61
  310.0 9.6 %collective-permute-done.38 = bf16[2,80,1376]{2,1,0:T(8,128)(2,1)S(1)} collective-permute-done((bf16[2,80,1376]{2,1,0:T(8,128)(2,1)S(1)}, bf16[2,80,1376]{2,1,0:T(8,128)(2,1)S(1)}, u32[]{:S(2)}, u32[]{:S(2)}) %collective-permute-start.38) | collective-permute-done | bytes 440352 | tf_op jit(solution)/shard_map/ppermute | solution.py:61
  323.4 17.8 %collective-permute-done.41 = bf16[2,160,1376]{2,1,0:T(8,128)(2,1)S(1)} collective-permute-done((bf16[2,160,1376]{2,1,0:T(8,128)(2,1)S(1)}, bf16[2,160,1376]{2,1,0:T(8,128)(2,1)S(1)}, u32[]{:S(2)}, u32[]{:S(2)}) %collective-permute-start.41) | collective-permute-done | bytes 880672 | tf_op jit(solution)/shard_map/ppermute | solution.py:61
  344.1 8.1 %collective-permute-done.44 = bf16[160,1376]{1,0:T(8,128)(2,1)S(1)} collective-permute-done((bf16[160,1376]{1,0:T(8,128)(2,1)S(1)}, bf16[160,1376]{1,0:T(8,128)(2,1)S(1)}, u32[]{:S(2)}, u32[]{:S(2)}) %collective-permute-start.44) | collective-permute-done | bytes 440352 | tf_op jit(solution)/shard_map/ppermute | solution.py:61
  352.3 2.2 fusion.31
  354.6 2.4 add_convert_fusion
  357.2 4.9 %fusion.34 = f32[1376,1024]{1,0:T(8,128)} fusion(bf16[640,1376]{1,0:T(8,128)(2,1)S(1)} %bitcast.273, bf16[640,1024]{1,0:T(8,128)(2,1)S(1)} %bitcast.235), kind=kOutput, calls=%fused_computation.114 | convolution fusion | flops 1803550720 | bytes 8708096 | tf_op jit(solution)/shard_map/dot_general | solution.py:21
  362.1 4.9 %fusion.32 = f32[1024,1376]{0,1:T(8,128)} fusion(bf16[640,1024]{1,0:T(8,128)(2,1)S(1)} %bitcast.225, bf16[640,1376]{1,0:T(8,128)(2,1)S(1)} %bitcast.271), kind=kOutput, calls=%fused_computation.112 | convolution fusion | flops 1803550720 | bytes 8708096 | tf_op jit(solution)/shard_map/dot_general | solution.py:21
  370.9 4.9 %fusion.33 = f32[1024,1376]{0,1:T(8,128)} fusion(bf16[640,1024]{1,0:T(8,128)(2,1)S(1)} %bitcast.226, bf16[640,1376]{1,0:T(8,128)(2,1)S(1)} %bitcast.269), kind=kOutput, calls=%fused_computation.113 | convolution fusion | flops 1803550720 | bytes 8708096 | tf_op jit(solution)/shard_map/dot_general | solution.py:21
  375.8 4.7 %collective-permute-done.47 = bf16[80,1024]{1,0:T(8,128)(2,1)S(1)} collective-permute-done((bf16[80,1024]{1,0:T(8,128)(2,1)S(1)}, bf16[80,1024]{1,0:T(8,128)(2,1)S(1)}, u32[]{:S(2)}, u32[]{:S(2)}) %collective-permute-start.47) | collective-permute-done | bytes 163872 | tf_op jit(solution)/shard_map/ppermute | solution.py:67
  380.6 5.2 %collective-permute-done.48 = bf16[80,1024]{1,0:T(8,128)(2,1)S(1)} collective-permute-done((bf16[80,1024]{1,0:T(8,128)(2,1)S(1)}, bf16[80,1024]{1,0:T(8,128)(2,1)S(1)}, u32[]{:S(2)}, u32[]{:S(2)}) %collective-permute-start.48) | collective-permute-done | bytes 163872 | tf_op jit(solution)/shard_map/ppermute | solution.py:67
  (190 shorter events, 66.0 us)
Async XLA Ops:
  7.2 163.7 %all-gather.3.cloned.1.call-start = ((), (), s32[]{:S(2)}) async-start(), calls=%async_computation | async-start | bytes 5898240 | tf_op jit(solution)/shard_map/all_gather | solution.py:316
  15.3 22.1 %collective-permute-start.2 = (bf16[2,160,1376]{2,1,0:T(8,128)(2,1)}, bf16[2,160,1376]{2,1,0:T(8,128)(2,1)}, u32[]{:S(2)}, u32[]{:S(2)}) collective-permute-start(bf16[2,160,1376]{2,1,0:T(8,128)(2,1)} %bitcast.21), channel_id=1, source_target_pairs={{0,16},{8,24},{16,0},{24,8},{1,17},{9,25},{17,1},{25,9},{2,18},{10... | collective-permute-start | bytes 2641928 | tf_op jit(solution)/shard_map/ppermute | solution.py:61
  20.5 23.2 %collective-permute-start = (bf16[2,160,1376]{2,1,0:T(8,128)(2,1)}, bf16[2,160,1376]{2,1,0:T(8,128)(2,1)}, u32[]{:S(2)}, u32[]{:S(2)}) collective-permute-start(bf16[2,160,1376]{2,1,0:T(8,128)(2,1)} %bitcast.17), channel_id=1, source_target_pairs={{0,8},{8,0},{16,24},{24,16},{1,9},{9,1},{17,25},{25,17},{2,10},{10... | collective-permute-start | bytes 2641928 | tf_op jit(solution)/shard_map/ppermute | solution.py:61
  38.7 13.1 %collective-permute-start.3 = (bf16[1,160,1376]{2,1,0:T(8,128)(2,1)S(1)}, bf16[1,160,1376]{2,1,0:T(8,128)(2,1)S(1)}, u32[]{:S(2)}, u32[]{:S(2)}) collective-permute-start(bf16[1,160,1376]{2,1,0:T(8,128)(2,1)S(1)} %slice.254), channel_id=1, source_target_pairs={{0,8},{8,0},{16,24},{24,16},{1,9},{9,1},{17,25},{25,17},{2,10},{10... | collective-permute-start | bytes 1320968 | tf_op jit(solution)/shard_map/ppermute | solution.py:61
  45.1 9.9 %collective-permute-start.1 = (bf16[1,160,1376]{2,1,0:T(8,128)(2,1)S(1)}, bf16[1,160,1376]{2,1,0:T(8,128)(2,1)S(1)}, u32[]{:S(2)}, u32[]{:S(2)}) collective-permute-start(bf16[1,160,1376]{2,1,0:T(8,128)(2,1)S(1)} %slice.255), channel_id=1, source_target_pairs={{0,16},{8,24},{16,0},{24,8},{1,17},{9,25},{17,1},{25,9},{2,18},{10... | collective-permute-start | bytes 1320968 | tf_op jit(solution)/shard_map/ppermute | solution.py:61
  55.4 12.0 %collective-permute-start.4 = (bf16[2,80,1376]{2,1,0:T(8,128)(2,1)S(1)}, bf16[2,80,1376]{2,1,0:T(8,128)(2,1)S(1)}, u32[]{:S(2)}, u32[]{:S(2)}) collective-permute-start(bf16[2,80,1376]{2,1,0:T(8,128)(2,1)S(1)} %multiply_convert_fusion), channel_id=1, source_target_pairs={{0,8},{8,0},{16,24},{24,16},{1,9},{9,1},{17,25},{25,17},{2,10},{10... | collective-permute-start | bytes 1320968 | tf_op jit(solution)/shard_map/ppermute | solution.py:61
  55.6 9.7 %collective-permute-start.5 = (bf16[2,80,1376]{2,1,0:T(8,128)(2,1)S(1)}, bf16[2,80,1376]{2,1,0:T(8,128)(2,1)S(1)}, u32[]{:S(2)}, u32[]{:S(2)}) collective-permute-start(bf16[2,80,1376]{2,1,0:T(8,128)(2,1)S(1)} %multiply_convert_fusion), channel_id=1, source_target_pairs={{0,16},{8,24},{16,0},{24,8},{1,17},{9,25},{17,1},{25,9},{2,18},{10... | collective-permute-start | bytes 1320968 | tf_op jit(solution)/shard_map/ppermute | solution.py:61
  65.2 6.1 %collective-permute-start.6 = (bf16[80,1376]{1,0:T(8,128)(2,1)S(1)}, bf16[80,1376]{1,0:T(8,128)(2,1)S(1)}, u32[]{:S(2)}, u32[]{:S(2)}) collective-permute-start(bf16[80,1376]{1,0:T(8,128)(2,1)S(1)} %slice_bitcast_fusion.16), channel_id=1, source_target_pairs={{0,8},{8,0},{16,24},{24,16},{1,9},{9,1},{17,25},{25,17},{2,10},{10... | collective-permute-start | bytes 660488 | tf_op jit(solution)/shard_map/ppermute | solution.py:61
  67.4 6.0 %collective-permute-start.7 = (bf16[80,1376]{1,0:T(8,128)(2,1)S(1)}, bf16[80,1376]{1,0:T(8,128)(2,1)S(1)}, u32[]{:S(2)}, u32[]{:S(2)}) collective-permute-start(bf16[80,1376]{1,0:T(8,128)(2,1)S(1)} %slice_bitcast_fusion.15), channel_id=1, source_target_pairs={{0,16},{8,24},{16,0},{24,8},{1,17},{9,25},{17,1},{25,9},{2,18},{10... | collective-permute-start | bytes 660488 | tf_op jit(solution)/shard_map/ppermute | solution.py:61
  83.2 12.0 %collective-permute-start.10 = (bf16[80,1024]{1,0:T(8,128)(2,1)}, bf16[80,1024]{1,0:T(8,128)(2,1)S(1)}, u32[]{:S(2)}, u32[]{:S(2)}) collective-permute-start(bf16[80,1024]{1,0:T(8,128)(2,1)} %get-tuple-element.70), channel_id=1, source_target_pairs={{0,4},{1,5},{2,6},{3,7},{4,0},{5,1},{6,2},{7,3},{8,12},{9,13},{10,... | collective-permute-start | bytes 491528 | tf_op jit(solution)/shard_map/ppermute | solution.py:67
  83.3 17.7 %collective-permute-start.11 = (bf16[80,1024]{1,0:T(8,128)(2,1)}, bf16[80,1024]{1,0:T(8,128)(2,1)S(1)}, u32[]{:S(2)}, u32[]{:S(2)}) collective-permute-start(bf16[80,1024]{1,0:T(8,128)(2,1)} %get-tuple-element.69), channel_id=1, source_target_pairs={{0,6},{1,7},{2,4},{3,5},{4,2},{5,3},{6,0},{7,1},{8,14},{9,15},{10,... | collective-permute-start | bytes 491528 | tf_op jit(solution)/shard_map/ppermute | solution.py:67
  86.0 15.0 %collective-permute-start.9 = (bf16[80,1024]{1,0:T(8,128)(2,1)}, bf16[80,1024]{1,0:T(8,128)(2,1)}, u32[]{:S(2)}, u32[]{:S(2)}) collective-permute-start(bf16[80,1024]{1,0:T(8,128)(2,1)} %get-tuple-element.68), channel_id=1, source_target_pairs={{0,2},{1,3},{2,0},{3,1},{4,6},{5,7},{6,4},{7,5},{8,10},{9,11},{10,... | collective-permute-start | bytes 491528 | tf_op jit(solution)/shard_map/ppermute | solution.py:67
  102.3 7.2 %collective-permute-start.12 = (bf16[80,1024]{1,0:T(8,128)(2,1)S(1)}, bf16[80,1024]{1,0:T(8,128)(2,1)S(1)}, u32[]{:S(2)}, u32[]{:S(2)}) collective-permute-start(bf16[80,1024]{1,0:T(8,128)(2,1)S(1)} %get-tuple-element.47), channel_id=1, source_target_pairs={{0,2},{1,3},{2,0},{3,1},{4,6},{5,7},{6,4},{7,5},{8,10},{9,11},{10,... | collective-permute-start | bytes 491528 | tf_op jit(solution)/shard_map/ppermute | solution.py:67
  102.4 12.6 %collective-permute-start.13 = (bf16[80,1024]{1,0:T(8,128)(2,1)S(1)}, bf16[80,1024]{1,0:T(8,128)(2,1)S(1)}, u32[]{:S(2)}, u32[]{:S(2)}) collective-permute-start(bf16[80,1024]{1,0:T(8,128)(2,1)S(1)} %get-tuple-element.47), channel_id=1, source_target_pairs={{0,4},{1,5},{2,6},{3,7},{4,0},{5,1},{6,2},{7,3},{8,12},{9,13},{10,... | collective-permute-start | bytes 491528 | tf_op jit(solution)/shard_map/ppermute | solution.py:67
  103.5 16.6 %collective-permute-start.14 = (bf16[80,1024]{1,0:T(8,128)(2,1)S(1)}, bf16[80,1024]{1,0:T(8,128)(2,1)S(1)}, u32[]{:S(2)}, u32[]{:S(2)}) collective-permute-start(bf16[80,1024]{1,0:T(8,128)(2,1)S(1)} %get-tuple-element.47), channel_id=1, source_target_pairs={{0,6},{1,7},{2,4},{3,5},{4,2},{5,3},{6,0},{7,1},{8,14},{9,15},{10,... | collective-permute-start | bytes 491528 | tf_op jit(solution)/shard_map/ppermute | solution.py:67
  120.0 15.9 %collective-permute-start.17 = (bf16[2,160,1024]{2,1,0:T(8,128)(2,1)S(1)}, bf16[2,160,1024]{2,1,0:T(8,128)(2,1)S(1)}, u32[]{:S(2)}, u32[]{:S(2)}) collective-permute-start(bf16[2,160,1024]{2,1,0:T(8,128)(2,1)S(1)} %bitcast.282), channel_id=1, source_target_pairs={{0,8},{8,0},{16,24},{24,16},{1,9},{9,1},{17,25},{25,17},{2,10},{10... | collective-permute-start | bytes 1966088 | tf_op jit(solution)/shard_map/ppermute | solution.py:61
  120.5 15.6 %collective-permute-start.15 = (bf16[2,160,1024]{2,1,0:T(8,128)(2,1)S(1)}, bf16[2,160,1024]{2,1,0:T(8,128)(2,1)S(1)}, u32[]{:S(2)}, u32[]{:S(2)}) collective-permute-start(bf16[2,160,1024]{2,1,0:T(8,128)(2,1)S(1)} %bitcast.283), channel_id=1, source_target_pairs={{0,16},{8,24},{16,0},{24,8},{1,17},{9,25},{17,1},{25,9},{2,18},{10... | collective-permute-start | bytes 1966088 | tf_op jit(solution)/shard_map/ppermute | solution.py:61
  120.9 27.8 %collective-permute-start.20 = (bf16[320,1024]{1,0:T(8,128)(2,1)S(1)}, bf16[320,1024]{1,0:T(8,128)(2,1)S(1)}, u32[]{:S(2)}, u32[]{:S(2)}) collective-permute-start(bf16[320,1024]{1,0:T(8,128)(2,1)S(1)} %bitcast.284), channel_id=1, source_target_pairs={{0,1},{1,0},{2,3},{3,2},{4,5},{5,4},{6,7},{7,6},{8,9},{9,8},{10,11... | collective-permute-start | bytes 1966088 | tf_op jit(solution)/shard_map/ppermute | solution.py:64
  136.0 12.7 %collective-permute-start.21 = (bf16[320,1024]{1,0:T(8,128)(2,1)S(1)}, bf16[320,1024]{1,0:T(8,128)(2,1)S(1)}, u32[]{:S(2)}, u32[]{:S(2)}) collective-permute-start(bf16[320,1024]{1,0:T(8,128)(2,1)S(1)} %bitcast.288), channel_id=1, source_target_pairs={{0,1},{1,0},{2,3},{3,2},{4,5},{5,4},{6,7},{7,6},{8,9},{9,8},{10,11... | collective-permute-start | bytes 1966088 | tf_op jit(solution)/shard_map/ppermute | solution.py:64
  136.1 12.6 %collective-permute-start.22 = (bf16[320,1024]{1,0:T(8,128)(2,1)S(1)}, bf16[320,1024]{1,0:T(8,128)(2,1)S(1)}, u32[]{:S(2)}, u32[]{:S(2)}) collective-permute-start(bf16[320,1024]{1,0:T(8,128)(2,1)S(1)} %bitcast.290), channel_id=1, source_target_pairs={{0,1},{1,0},{2,3},{3,2},{4,5},{5,4},{6,7},{7,6},{8,9},{9,8},{10,11... | collective-permute-start | bytes 1966088 | tf_op jit(solution)/shard_map/ppermute | solution.py:64
  136.5 9.8 %collective-permute-start.16 = (bf16[160,1024]{1,0:T(8,128)(2,1)S(1)}, bf16[160,1024]{1,0:T(8,128)(2,1)S(1)}, u32[]{:S(2)}, u32[]{:S(2)}) collective-permute-start(bf16[160,1024]{1,0:T(8,128)(2,1)S(1)} %slice_bitcast_fusion.10), channel_id=1, source_target_pairs={{0,8},{8,0},{16,24},{24,16},{1,9},{9,1},{17,25},{25,17},{2,10},{10... | collective-permute-start | bytes 983048 | tf_op jit(solution)/shard_map/ppermute | solution.py:61
  137.8 9.9 %collective-permute-start.18 = (bf16[160,1024]{1,0:T(8,128)(2,1)S(1)}, bf16[160,1024]{1,0:T(8,128)(2,1)S(1)}, u32[]{:S(2)}, u32[]{:S(2)}) collective-permute-start(bf16[160,1024]{1,0:T(8,128)(2,1)S(1)} %slice_bitcast_fusion.9), channel_id=1, source_target_pairs={{0,16},{8,24},{16,0},{24,8},{1,17},{9,25},{17,1},{25,9},{2,18},{10... | collective-permute-start | bytes 983048 | tf_op jit(solution)/shard_map/ppermute | solution.py:61
  148.7 41.0 %collective-permute-start.19 = (bf16[320,1024]{1,0:T(8,128)(2,1)}, bf16[320,1024]{1,0:T(8,128)(2,1)}, u32[]{:S(2)}, u32[]{:S(2)}) collective-permute-start(bf16[320,1024]{1,0:T(8,128)(2,1)} %bitcast.49.own), channel_id=1, source_target_pairs={{0,1},{1,0},{2,3},{3,2},{4,5},{5,4},{6,7},{7,6},{8,9},{9,8},{10,11... | collective-permute-start | bytes 1966088 | tf_op jit(solution)/shard_map/ppermute | solution.py:64
  213.2 13.2 %collective-permute-start.25 = (bf16[1,320,1024]{2,1,0:T(8,128)(2,1)S(1)}, bf16[1,320,1024]{2,1,0:T(8,128)(2,1)S(1)}, u32[]{:S(2)}, u32[]{:S(2)}) collective-permute-start(bf16[1,320,1024]{2,1,0:T(8,128)(2,1)S(1)} %get-tuple-element.37), channel_id=1, source_target_pairs={{0,1},{1,0},{2,3},{3,2},{4,5},{5,4},{6,7},{7,6},{8,9},{9,8},{10,11... | collective-permute-start | bytes 1966088 | tf_op jit(solution)/shard_map/ppermute | solution.py:64
  226.4 9.4 %collective-permute-start.24 = (bf16[2,320,1024]{2,1,0:T(8,128)(2,1)S(1)}, bf16[2,320,1024]{2,1,0:T(8,128)(2,1)S(1)}, u32[]{:S(2)}, u32[]{:S(2)}) collective-permute-start(bf16[2,320,1024]{2,1,0:T(8,128)(2,1)S(1)} %get-tuple-element.35), channel_id=1, source_target_pairs={{0,1},{1,0},{2,3},{3,2},{4,5},{5,4},{6,7},{7,6},{8,9},{9,8},{10,11... | collective-permute-start | bytes 3932168 | tf_op jit(solution)/shard_map/ppermute | solution.py:64
  226.8 10.2 %collective-permute-start.26 = (bf16[160,1024]{1,0:T(8,128)(2,1)S(1)}, bf16[160,1024]{1,0:T(8,128)(2,1)S(1)}, u32[]{:S(2)}, u32[]{:S(2)}) collective-permute-start(bf16[160,1024]{1,0:T(8,128)(2,1)S(1)} %get-tuple-element.66), channel_id=1, source_target_pairs={{0,16},{8,24},{16,0},{24,8},{1,17},{9,25},{17,1},{25,9},{2,18},{10... | collective-permute-start | bytes 983048 | tf_op jit(solution)/shard_map/ppermute | solution.py:61
  235.3 12.0 %collective-permute-start.23 = (bf16[1,320,1024]{2,1,0:T(8,128)(2,1)S(1)}, bf16[1,320,1024]{2,1,0:T(8,128)(2,1)S(1)}, u32[]{:S(2)}, u32[]{:S(2)}) collective-permute-start(bf16[1,320,1024]{2,1,0:T(8,128)(2,1)S(1)} %get-tuple-element.33), channel_id=1, source_target_pairs={{0,1},{1,0},{2,3},{3,2},{4,5},{5,4},{6,7},{7,6},{8,9},{9,8},{10,11... | collective-permute-start | bytes 1966088 | tf_op jit(solution)/shard_map/ppermute | solution.py:64
  235.4 10.6 %collective-permute-start.28 = (bf16[160,1024]{1,0:T(8,128)(2,1)S(1)}, bf16[160,1024]{1,0:T(8,128)(2,1)S(1)}, u32[]{:S(2)}, u32[]{:S(2)}) collective-permute-start(bf16[160,1024]{1,0:T(8,128)(2,1)S(1)} %get-tuple-element.67), channel_id=1, source_target_pairs={{0,8},{8,0},{16,24},{24,16},{1,9},{9,1},{17,25},{25,17},{2,10},{10... | collective-permute-start | bytes 983048 | tf_op jit(solution)/shard_map/ppermute | solution.py:61
  237.1 22.4 %collective-permute-start.27 = (bf16[2,160,1024]{2,1,0:T(8,128)(2,1)S(1)}, bf16[2,160,1024]{2,1,0:T(8,128)(2,1)S(1)}, u32[]{:S(2)}, u32[]{:S(2)}) collective-permute-start(bf16[2,160,1024]{2,1,0:T(8,128)(2,1)S(1)} %pad_maximum_fusion.2), channel_id=1, source_target_pairs={{0,8},{8,0},{16,24},{24,16},{1,9},{9,1},{17,25},{25,17},{2,10},{10... | collective-permute-start | bytes 1966088 | tf_op jit(solution)/shard_map/ppermute | solution.py:61
  246.1 15.9 %collective-permute-start.29 = (bf16[2,160,1024]{2,1,0:T(8,128)(2,1)S(1)}, bf16[2,160,1024]{2,1,0:T(8,128)(2,1)S(1)}, u32[]{:S(2)}, u32[]{:S(2)}) collective-permute-start(bf16[2,160,1024]{2,1,0:T(8,128)(2,1)S(1)} %pad_maximum_fusion.3), channel_id=1, source_target_pairs={{0,16},{8,24},{16,0},{24,8},{1,17},{9,25},{17,1},{25,9},{2,18},{10... | collective-permute-start | bytes 1966088 | tf_op jit(solution)/shard_map/ppermute | solution.py:61
  262.4 7.2 %collective-permute-start.30 = (bf16[80,1024]{1,0:T(8,128)(2,1)S(1)}, bf16[80,1024]{1,0:T(8,128)(2,1)S(1)}, u32[]{:S(2)}, u32[]{:S(2)}) collective-permute-start(bf16[80,1024]{1,0:T(8,128)(2,1)S(1)} %get-tuple-element.63), channel_id=1, source_target_pairs={{0,2},{1,3},{2,0},{3,1},{4,6},{5,7},{6,4},{7,5},{8,10},{9,11},{10,... | collective-permute-start | bytes 491528 | tf_op jit(solution)/shard_map/ppermute | solution.py:67
  262.5 11.8 %collective-permute-start.31 = (bf16[80,1024]{1,0:T(8,128)(2,1)S(1)}, bf16[80,1024]{1,0:T(8,128)(2,1)S(1)}, u32[]{:S(2)}, u32[]{:S(2)}) collective-permute-start(bf16[80,1024]{1,0:T(8,128)(2,1)S(1)} %get-tuple-element.65), channel_id=1, source_target_pairs={{0,4},{1,5},{2,6},{3,7},{4,0},{5,1},{6,2},{7,3},{8,12},{9,13},{10,... | collective-permute-start | bytes 491528 | tf_op jit(solution)/shard_map/ppermute | solution.py:67
  263.5 14.9 %collective-permute-start.32 = (bf16[80,1024]{1,0:T(8,128)(2,1)S(1)}, bf16[80,1024]{1,0:T(8,128)(2,1)S(1)}, u32[]{:S(2)}, u32[]{:S(2)}) collective-permute-start(bf16[80,1024]{1,0:T(8,128)(2,1)S(1)} %get-tuple-element.64), channel_id=1, source_target_pairs={{0,6},{1,7},{2,4},{3,5},{4,2},{5,3},{6,0},{7,1},{8,14},{9,15},{10,... | collective-permute-start | bytes 491528 | tf_op jit(solution)/shard_map/ppermute | solution.py:67
  278.6 7.2 %collective-permute-start.33 = (bf16[80,1024]{1,0:T(8,128)(2,1)S(1)}, bf16[80,1024]{1,0:T(8,128)(2,1)S(1)}, u32[]{:S(2)}, u32[]{:S(2)}) collective-permute-start(bf16[80,1024]{1,0:T(8,128)(2,1)S(1)} %get-tuple-element.45), channel_id=1, source_target_pairs={{0,2},{1,3},{2,0},{3,1},{4,6},{5,7},{6,4},{7,5},{8,10},{9,11},{10,... | collective-permute-start | bytes 491528 | tf_op jit(solution)/shard_map/ppermute | solution.py:67
  278.7 12.3 %collective-permute-start.34 = (bf16[80,1024]{1,0:T(8,128)(2,1)S(1)}, bf16[80,1024]{1,0:T(8,128)(2,1)S(1)}, u32[]{:S(2)}, u32[]{:S(2)}) collective-permute-start(bf16[80,1024]{1,0:T(8,128)(2,1)S(1)} %get-tuple-element.45), channel_id=1, source_target_pairs={{0,4},{1,5},{2,6},{3,7},{4,0},{5,1},{6,2},{7,3},{8,12},{9,13},{10,... | collective-permute-start | bytes 491528 | tf_op jit(solution)/shard_map/ppermute | solution.py:67
  280.3 14.8 %collective-permute-start.35 = (bf16[80,1024]{1,0:T(8,128)(2,1)S(1)}, bf16[80,1024]{1,0:T(8,128)(2,1)S(1)}, u32[]{:S(2)}, u32[]{:S(2)}) collective-permute-start(bf16[80,1024]{1,0:T(8,128)(2,1)S(1)} %get-tuple-element.45), channel_id=1, source_target_pairs={{0,6},{1,7},{2,4},{3,5},{4,2},{5,3},{6,0},{7,1},{8,14},{9,15},{10,... | collective-permute-start | bytes 491528 | tf_op jit(solution)/shard_map/ppermute | solution.py:67
  300.2 7.6 %collective-permute-start.37 = (bf16[80,1376]{1,0:T(8,128)(2,1)S(1)}, bf16[80,1376]{1,0:T(8,128)(2,1)S(1)}, u32[]{:S(2)}, u32[]{:S(2)}) collective-permute-start(bf16[80,1376]{1,0:T(8,128)(2,1)S(1)} %get-tuple-element.71), channel_id=1, source_target_pairs={{0,16},{8,24},{16,0},{24,8},{1,17},{9,25},{17,1},{25,9},{2,18},{10... | collective-permute-start | bytes 660488 | tf_op jit(solution)/shard_map/ppermute | solution.py:61
  300.9 7.5 %collective-permute-start.39 = (bf16[80,1376]{1,0:T(8,128)(2,1)S(1)}, bf16[80,1376]{1,0:T(8,128)(2,1)S(1)}, u32[]{:S(2)}, u32[]{:S(2)}) collective-permute-start(bf16[80,1376]{1,0:T(8,128)(2,1)S(1)} %get-tuple-element.72), channel_id=1, source_target_pairs={{0,8},{8,0},{16,24},{24,16},{1,9},{9,1},{17,25},{25,17},{2,10},{10... | collective-permute-start | bytes 660488 | tf_op jit(solution)/shard_map/ppermute | solution.py:61
  308.0 11.6 %collective-permute-start.38 = (bf16[2,80,1376]{2,1,0:T(8,128)(2,1)S(1)}, bf16[2,80,1376]{2,1,0:T(8,128)(2,1)S(1)}, u32[]{:S(2)}, u32[]{:S(2)}) collective-permute-start(bf16[2,80,1376]{2,1,0:T(8,128)(2,1)S(1)} %pad_maximum_fusion.4), channel_id=1, source_target_pairs={{0,8},{8,0},{16,24},{24,16},{1,9},{9,1},{17,25},{25,17},{2,10},{10... | collective-permute-start | bytes 1320968 | tf_op jit(solution)/shard_map/ppermute | solution.py:61
  308.6 11.3 %collective-permute-start.40 = (bf16[2,80,1376]{2,1,0:T(8,128)(2,1)S(1)}, bf16[2,80,1376]{2,1,0:T(8,128)(2,1)S(1)}, u32[]{:S(2)}, u32[]{:S(2)}) collective-permute-start(bf16[2,80,1376]{2,1,0:T(8,128)(2,1)S(1)} %pad_maximum_fusion.5), channel_id=1, source_target_pairs={{0,16},{8,24},{16,0},{24,8},{1,17},{9,25},{17,1},{25,9},{2,18},{10... | collective-permute-start | bytes 1320968 | tf_op jit(solution)/shard_map/ppermute | solution.py:61
  321.2 20.1 %collective-permute-start.41 = (bf16[2,160,1376]{2,1,0:T(8,128)(2,1)S(1)}, bf16[2,160,1376]{2,1,0:T(8,128)(2,1)S(1)}, u32[]{:S(2)}, u32[]{:S(2)}) collective-permute-start(bf16[2,160,1376]{2,1,0:T(8,128)(2,1)S(1)} %pad_maximum_fusion), channel_id=1, source_target_pairs={{0,8},{8,0},{16,24},{24,16},{1,9},{9,1},{17,25},{25,17},{2,10},{10... | collective-permute-start | bytes 2641928 | tf_op jit(solution)/shard_map/ppermute | solution.py:61
  322.9 21.0 %collective-permute-start.42 = (bf16[2,160,1376]{2,1,0:T(8,128)(2,1)S(1)}, bf16[2,160,1376]{2,1,0:T(8,128)(2,1)S(1)}, u32[]{:S(2)}, u32[]{:S(2)}) collective-permute-start(bf16[2,160,1376]{2,1,0:T(8,128)(2,1)S(1)} %pad_maximum_fusion), channel_id=1, source_target_pairs={{0,16},{8,24},{16,0},{24,8},{1,17},{9,25},{17,1},{25,9},{2,18},{10... | collective-permute-start | bytes 2641928 | tf_op jit(solution)/shard_map/ppermute | solution.py:61
  341.4 10.8 %collective-permute-start.44 = (bf16[160,1376]{1,0:T(8,128)(2,1)S(1)}, bf16[160,1376]{1,0:T(8,128)(2,1)S(1)}, u32[]{:S(2)}, u32[]{:S(2)}) collective-permute-start(bf16[160,1376]{1,0:T(8,128)(2,1)S(1)} %get-tuple-element.54), channel_id=1, source_target_pairs={{0,16},{8,24},{16,0},{24,8},{1,17},{9,25},{17,1},{25,9},{2,18},{10... | collective-permute-start | bytes 1320968 | tf_op jit(solution)/shard_map/ppermute | solution.py:61
  344.0 10.5 %collective-permute-start.43 = (bf16[160,1376]{1,0:T(8,128)(2,1)S(1)}, bf16[160,1376]{1,0:T(8,128)(2,1)S(1)}, u32[]{:S(2)}, u32[]{:S(2)}) collective-permute-start(bf16[160,1376]{1,0:T(8,128)(2,1)S(1)} %get-tuple-element.50), channel_id=1, source_target_pairs={{0,8},{8,0},{16,24},{24,16},{1,9},{9,1},{17,25},{25,17},{2,10},{10... | collective-permute-start | bytes 1320968 | tf_op jit(solution)/shard_map/ppermute | solution.py:61
  357.2 9.9 %collective-permute-start.45 = (bf16[320,1024]{1,0:T(8,128)(2,1)S(1)}, bf16[320,1024]{1,0:T(8,128)(2,1)S(1)}, u32[]{:S(2)}, u32[]{:S(2)}) collective-permute-start(bf16[320,1024]{1,0:T(8,128)(2,1)S(1)} %dynamic-slice_bitcast_fusion), channel_id=1, source_target_pairs={{0,1},{1,0},{2,3},{3,2},{4,5},{5,4},{6,7},{7,6},{8,9},{9,8},{10,11... | collective-permute-start | bytes 1966088 | tf_op jit(solution)/shard_map/ppermute | solution.py:64
  367.4 8.5 %collective-permute-start.46 = (bf16[80,1024]{1,0:T(8,128)(2,1)S(1)}, bf16[80,1024]{1,0:T(8,128)(2,1)S(1)}, u32[]{:S(2)}, u32[]{:S(2)}) collective-permute-start(bf16[80,1024]{1,0:T(8,128)(2,1)S(1)} %get-tuple-element.60), channel_id=1, source_target_pairs={{0,2},{1,3},{2,0},{3,1},{4,6},{5,7},{6,4},{7,5},{8,10},{9,11},{10,... | collective-permute-start | bytes 491528 | tf_op jit(solution)/shard_map/ppermute | solution.py:67
  367.4 13.1 %collective-permute-start.47 = (bf16[80,1024]{1,0:T(8,128)(2,1)S(1)}, bf16[80,1024]{1,0:T(8,128)(2,1)S(1)}, u32[]{:S(2)}, u32[]{:S(2)}) collective-permute-start(bf16[80,1024]{1,0:T(8,128)(2,1)S(1)} %get-tuple-element.62), channel_id=1, source_target_pairs={{0,4},{1,5},{2,6},{3,7},{4,0},{5,1},{6,2},{7,3},{8,12},{9,13},{10,... | collective-permute-start | bytes 491528 | tf_op jit(solution)/shard_map/ppermute | solution.py:67
  369.1 16.7 %collective-permute-start.48 = (bf16[80,1024]{1,0:T(8,128)(2,1)S(1)}, bf16[80,1024]{1,0:T(8,128)(2,1)S(1)}, u32[]{:S(2)}, u32[]{:S(2)}) collective-permute-start(bf16[80,1024]{1,0:T(8,128)(2,1)S(1)} %get-tuple-element.61), channel_id=1, source_target_pairs={{0,6},{1,7},{2,4},{3,5},{4,2},{5,3},{6,0},{7,1},{8,14},{9,15},{10,... | collective-permute-start | bytes 491528 | tf_op jit(solution)/shard_map/ppermute | solution.py:67
  (27 other events, 161.9 us)
Sparse Core Ops, SparseCore 0:
  21.2 54.9 all-gather.2

commit v2 on v1

v2 whole, which is shorter than its diff:
```python
import functools

import jax
import jax.numpy as jnp
from jax import lax
from jax.experimental import pallas as pl
from jax.experimental.pallas import tpu as pltpu
from jax.sharding import PartitionSpec as P

BF = jnp.bfloat16
F32 = jnp.float32
MIB = 1 << 20


def silu_grad(pre_act):
    sig = jax.nn.sigmoid(pre_act)
    return sig * (1.0 + pre_act * (1.0 - sig))


def dot(left, right, dims):
    return lax.dot_general(left, right, (dims, ((), ())), preferred_element_type=F32)


def dot_nt(left, right):
    return dot(left, right, ((1,), (1,)))


def dot_nn(left, right):
    return dot(left, right, ((1,), (0,)))


def row(stack, index):
    return lax.dynamic_index_in_dim(stack, index, 0, keepdims=False)


def whole(shape):
    return pl.BlockSpec(shape, lambda *_: (0,) * len(shape), pipeline_mode=pl.Buffered(1))


def tie(*values):
    return lax.optimization_barrier(values)


def call(kernel, name, grid, index, in_specs, out_specs, out_shape, operands, flops, vmem, scratch=()):
    moved = sum(o.size * o.dtype.itemsize for o in operands)
    return pl.pallas_call(
        kernel,
        grid_spec=pltpu.PrefetchScalarGridSpec(
            num_scalar_prefetch=1, grid=grid, in_specs=in_specs, out_specs=out_specs, scratch_shapes=scratch
        ),
        out_shape=out_shape,
        name=name,
        cost_estimate=pl.CostEstimate(flops=flops, bytes_accessed=moved, transcendentals=0),
        compiler_params=pltpu.CompilerParams(vmem_limit_bytes=vmem * MIB),
    )(index, *operands)


class Plan:
    def __init__(self, mesh):
        self.groups = mesh.shape["group"]
        self.members = mesh.shape["mp"]
        self.places = self.members // 2

    def group_swap(self, value, mask):
        return lax.ppermute(value, "group", [(i, i ^ mask) for i in range(self.groups)])

    def core_swap(self, value):
        return lax.ppermute(value, "mp", [(i, i ^ 1) for i in range(self.members)])

    def place_swap(self, value, mask):
        return lax.ppermute(value, "mp", [(i, i ^ (2 * mask)) for i in range(self.members)])

    def hop_one(self, pair):
        reach = (1, 2) if self.groups == 4 else range(1, self.groups)
        return {0: pair} | {k: self.group_swap(pair, k) for k in reach}

    def hop_two(self, have):
        if self.groups != 4:
            return {}
        return {3: (self.group_swap(have[2][0], 1), self.group_swap(have[1][1], 2))}

    def gather(self, pair, first=None, second=None):
        have = self.hop_one(pair)
        done = first() if first else ()
        have, done = lax.optimization_barrier((have, tuple(done)))
        rest = self.hop_two(have)
        done = second(have, done) if second else done
        rest, done = lax.optimization_barrier((rest, tuple(done)))
        return have | rest, done

    def scatter(self, make, hold):
        if self.groups == 4:
            send, hold = lax.optimization_barrier((make(3, 1, None, hold)[3].astype(BF), hold))
            hops = (self.group_swap(send[0], 1), self.group_swap(send[1], 2))
            parts, hops = make(1, 2, hops, hold)
            to_x = jnp.stack([parts[1][0].astype(F32), parts[1][1].astype(F32) + hops[1].astype(F32)]).astype(BF)
            to_y = jnp.stack([parts[2][0].astype(F32) + hops[0].astype(F32), parts[2][1].astype(F32)]).astype(BF)
            to_x, to_y, hold = lax.optimization_barrier((to_x, to_y, hold))
            came_x = self.group_swap(to_x, 1)
            came_y = self.group_swap(to_y, 2)
            parts = make(0, 1, None, hold)
            return parts[0].astype(F32) + (came_x.astype(F32) + came_y.astype(F32))
        parts = make(0, self.groups, None, hold)
        total = parts[0].astype(F32)
        for k in range(1, self.groups):
            total = total + self.group_swap(parts[k].astype(BF), k).astype(F32)
        return total

    def halving(self, keep, send, first):
        current = keep.astype(F32) + self.group_swap(send, first).astype(F32)
        keys = [k for k in range(self.groups) if not k & first]
        current = {k: current[i] for i, k in enumerate(keys)}
        mask = 1
        while mask < self.groups:
            if mask != first:
                keys = [k for k in current if not k & mask]
                came = self.group_swap(jnp.stack([current[k | mask] for k in keys]).astype(BF), mask)
                current = {k: current[k] + came[i].astype(F32) for i, k in enumerate(keys)}
            mask *= 2
        return current[0]

    def place_sum(self, parts, me, beside=()):
        total = row(parts, me).astype(F32)
        came = [self.place_swap(row(parts, me ^ mask).astype(BF), mask) for mask in range(1, self.places)]
        came = tie(*came, *beside)
        for piece in came[: self.places - 1]:
            total = total + piece.astype(F32)
        return total, came[self.places - 1 :]

    def place_gather(self, piece, me, beside=()):
        came = [self.place_swap(piece, mask) for mask in range(1, self.places)]
        came, beside = lax.optimization_barrier((came, beside))
        out = jnp.zeros((self.places,) + piece.shape, piece.dtype)
        out = lax.dynamic_update_index_in_dim(out, piece, me, 0)
        for mask in range(1, self.places):
            out = lax.dynamic_update_index_in_dim(out, came[mask - 1], me ^ mask, 0)
        return out, beside


def chunks_kernel(index, *refs):
    value = jnp.concatenate([ref[...] for ref in refs[:-2]], 0)
    refs[-1][...] = dot_nt(value, refs[-2][...]).astype(BF)


def chunks_product(index, value, weight_t, order, groups, name):
    n = len(order)
    rows, depth = value.shape
    units = weight_t.shape[0]
    share = rows // groups
    specs = [pl.BlockSpec((share, depth), lambda i, index, k=k: (index[k], 0)) for k in order]
    shape = (n * share, units)
    out = call(
        chunks_kernel,
        name,
        (1,),
        index,
        specs + [whole(weight_t.shape)],
        whole(shape),
        jax.ShapeDtypeStruct(shape, BF),
        [value] * n + [weight_t],
        2 * n * share * depth * units,
        32,
    )
    return out.reshape(n, share, units)


def ghid_kernel(index, cot, weight, out):
    product = dot_nt(cot[0], weight[...])

    @pl.when(pl.program_id(0) == 0)
    def _():
        out[...] = product

    @pl.when(pl.program_id(0) > 0)
    def _():
        out[...] += product


def ghid_product(index, half_at, cot, weight):
    parts, rows, depth = cot.shape
    units = weight.shape[0]
    half = rows // 2
    return call(
        ghid_kernel,
        "head_hidden_grad",
        (parts,),
        index,
        [
            pl.BlockSpec((1, half, depth), lambda i, index: (i, index[half_at], 0)),
            pl.BlockSpec((units, depth), lambda i, index: (0, i)),
        ],
        whole((half, units)),
        jax.ShapeDtypeStruct((half, units), F32),
        [cot, weight],
        2 * half * units * depth * parts,
        40,
    )


def pre_kernel(n, begun, index, *refs):
    pieces, (gate_w, up_w), refs = refs[:n], refs[n : n + 2], refs[n + 2 :]
    start, (pre, lin) = refs[:begun], refs[begun:]
    for j in range(n // 2):

        @pl.when(pl.program_id(0) == j)
        def _(j=j):
            value = jnp.concatenate([p[...] for p in pieces[2 * j : 2 * j + 2]], 0)
            a, b = dot_nt(value, gate_w[...]), dot_nt(value, up_w[...])
            if j == 0 and begun:
                pre[...] = start[0][...] + a
                lin[...] = start[1][...] + b
            elif j == 0:
                pre[...] = a
                lin[...] = b
            else:
                pre[...] += a
                lin[...] += b


def pre_product(index, offset, pieces, gate_t, up_t, start=()):
    flat = [piece for pair in pieces for piece in pair]
    half, depth = flat[0].shape
    units = gate_t.shape[0]
    weight = pl.BlockSpec((units, depth), lambda i, index: (0, index[offset + i]))
    shape = jax.ShapeDtypeStruct((2 * half, units), F32)
    both = [whole((2 * half, units))] * 2
    return call(
        functools.partial(pre_kernel, len(flat), len(start)),
        "head_pre",
        (len(pieces),),
        index,
        [whole((half, depth))] * len(flat) + [weight] * 2 + both[: len(start)],
        both,
        [shape] * 2,
        flat + [gate_t, up_t, *start],
        8 * half * depth * units * len(pieces),
        60,
    )


def back_rows(places, place, product, cot, own, mate):
    half, depth = product.shape[0] // 2, product.shape[1]
    mate[0] = product[half:].astype(BF)
    extra = jnp.concatenate([cot[j, 0] for j in range(cot.shape[0])], 1).astype(F32)
    rows = product[:half].reshape(places, half // places, depth)
    at = lax.broadcasted_iota(jnp.int32, rows.shape, 0)
    rows = rows + jnp.where(at == place, extra[None], 0.0)
    own[0] = rows.reshape(half, depth).astype(BF)


def act_kernel(n, places, place_at, index, *refs):
    pieces, (gate_w, up_w, pre, lin, ghid_own, ghid_mate, cot, dgate, dup, own, mate) = refs[:n], refs[n : n + 11]
    sums = refs[n + 11 :]
    half = pieces[0].shape[0]
    for j in range(n // 2):

        @pl.when(pl.program_id(0) == j)
        def _(j=j):
            for side, ghid in enumerate((ghid_own, ghid_mate)):
                rows = slice(side * half, side * half + half)
                value = pieces[2 * j + side][...]
                before = (pre, lin) if j == 0 else sums
                gate = before[0][rows] + dot_nt(value, gate_w[...])
                up = before[1][rows] + dot_nt(value, up_w[...])
                if j < n // 2 - 1:
                    sums[0][rows] = gate
                    sums[1][rows] = up
                else:
                    h, sig = ghid[...], jax.nn.sigmoid(gate)
                    dgate[rows] = (h * up * (sig * (1.0 + gate * (1.0 - sig)))).astype(BF)
                    dup[rows] = (h * (gate * sig)).astype(BF)
            if j == n // 2 - 1:
                product = dot_nn(dgate[...], gate_w[...]) + dot_nn(dup[...], up_w[...])
                back_rows(places, index[place_at], product, cot, own, mate)


def cot_blocks(cot, places, groups):
    parts, rows, width = cot.shape
    return cot.reshape(parts, 2 * places, rows // (2 * places), width), (parts // groups, 1, rows // (2 * places), width)


def act_product(index, offset, pieces, gate_t, up_t, pre, lin, ghids, cot, places, core_at):
    flat = [piece for pair in pieces for piece in pair]
    half, depth = flat[0].shape
    units = gate_t.shape[0]
    last = offset + len(pieces) - 1
    weight = pl.BlockSpec((units, depth), lambda i, index: (0, index[offset + i]))
    cot, block = cot_blocks(cot, places, core_at)
    cot_spec = pl.BlockSpec(block, lambda i, index: (index[last], index[core_at + 2], 0, 0))
    return call(
        functools.partial(act_kernel, len(flat), places, core_at + 3),
        "head_act",
        (len(pieces),),
        index,
        [whole((half, depth))] * len(flat)
        + [weight] * 2
        + [whole((2 * half, units))] * 2
        + [whole((half, units))] * 2
        + [cot_spec],
        [whole((2 * half, units))] * 2 + [whole((1, half, depth))] * 2,
        [jax.ShapeDtypeStruct((2 * half, units), BF)] * 2 + [jax.ShapeDtypeStruct((1, half, depth), BF)] * 2,
        [*flat, gate_t, up_t, pre, lin, *ghids, cot],
        8 * half * depth * units * (len(pieces) + 1),
        60,
        [pltpu.VMEM((2 * half, units), F32)] * 2,
    )


def back_kernel(places, place_at, index, dgate, dup, gate_w, up_w, cot, own, mate):
    product = dot_nn(dgate[...], gate_w[...]) + dot_nn(dup[...], up_w[...])
    back_rows(places, index[place_at], product, cot, own, mate)


def back_product(index, offset, count, dgate, dup, gate_t, up_t, cot, places, core_at):
    rows, units = dgate.shape
    depth = gate_t.shape[1] // core_at
    half = rows // 2
    cot, block = cot_blocks(cot, places, core_at)
    weight = pl.BlockSpec((units, depth), lambda i, index: (0, index[offset + i]))
    cot_spec = pl.BlockSpec(block, lambda i, index: (index[offset + i], index[core_at + 2], 0, 0))
    out = pl.BlockSpec((1, half, depth), lambda i, index: (i, 0, 0))
    return call(
        functools.partial(back_kernel, places, core_at + 3),
        "head_back",
        (count,),
        index,
        [whole((rows, units))] * 2 + [weight] * 2 + [cot_spec],
        [out] * 2,
        [jax.ShapeDtypeStruct((count, half, depth), BF)] * 2,
        [dgate, dup, gate_t, up_t, cot],
        4 * rows * units * depth * count,
        48,
    )


def trunk_act_kernel(groups, core_at, index, *refs):
    ghids, gates, ups = refs[: 2 * groups], refs[2 * groups : 3 * groups], refs[3 * groups : 4 * groups]
    gate_w, up_w, dgate, dup, own, mate = refs[4 * groups :]
    for k in range(groups):
        share = gates[k].shape[0]
        ghid = jnp.concatenate([ghids[2 * k][...], ghids[2 * k + 1][...]], 0).astype(F32)
        gate, up = gates[k][...].astype(F32), ups[k][...].astype(F32)
        sig = jax.nn.sigmoid(gate)
        rows = pl.ds(pl.multiple_of(index[k] * share, share), share)
        dgate[rows] = (ghid * up * (sig * (1.0 + gate * (1.0 - sig)))).astype(BF)
        dup[rows] = (ghid * (gate * sig)).astype(BF)
    half = own.shape[0]
    for side, out in enumerate((own, mate)):
        rows = pl.ds(pl.multiple_of(index[core_at + side] * half, half), half)
        product = dot_nn(dgate[rows], gate_w[...]) + dot_nn(dup[rows], up_w[...])
        out[...] = product.astype(BF)


def trunk_act(index, ghids, gates, ups, gate_t, up_t):
    groups = len(gates)
    share, units = gates[0].shape
    rows, width = share * groups, gate_t.shape[1]
    flat = [half for pair in ghids for half in pair]
    shapes = [(rows, units)] * 2 + [(rows // 2, width)] * 2
    return call(
        functools.partial(trunk_act_kernel, groups, groups),
        "trunk_act",
        (1,),
        index,
        [whole(v.shape) for v in [*flat, *gates, *ups, gate_t, up_t]],
        [whole(shape) for shape in shapes],
        [jax.ShapeDtypeStruct(shape, BF) for shape in shapes],
        [*flat, *gates, *ups, gate_t, up_t],
        4 * rows * units * width,
        36,
    )


def grads_kernel(index, dgate, dup, toks, gate, up):
    gate[...] = dot(dgate[...], toks[...], ((0,), (0,)))
    up[...] = dot(dup[...], toks[...], ((0,), (0,)))


def grads_product(index, dgate, dup, toks):
    rows, units = dgate.shape
    width = toks.shape[1]
    tile = width // 2
    out = pl.BlockSpec((units, tile), lambda i, index: (0, i))
    return call(
        grads_kernel,
        "trunk_weight_grads",
        (2,),
        index,
        [whole((rows, units))] * 2 + [pl.BlockSpec((rows, tile), lambda i, index: (0, i))],
        [out] * 2,
        [jax.ShapeDtypeStruct((units, width), F32)] * 2,
        [dgate, dup, toks],
        4 * rows * units * width,
        48,
    )


def make_body(plan):
    groups, places = plan.groups, plan.places

    def body(tokens, trunk_gate, trunk_up, trunk_down, head_gate, head_up, head_down, head_grads):
        g = lax.axis_index("group")
        m = lax.axis_index("mp")
        z, c = m // 2, m % 2
        total_rows, width = tokens.shape
        rows = total_rows // plan.members
        units = trunk_gate.shape[1]
        half_rows = places * rows
        share = total_rows // groups
        offsets = [g ^ k for k in range(groups)]
        index = jnp.stack(offsets + [c, 1 - c, c * places + z, z]).astype(jnp.int32)

        toks = tokens.reshape(places, 2, rows, width).transpose(1, 0, 2, 3)
        own_tok = row(row(toks, c), z)
        toks = toks.reshape(total_rows, width)
        cot_width = head_grads.shape[2]
        cot_own = head_grads[0].reshape(places, 2, rows, cot_width).transpose(1, 0, 2, 3)
        cot_own, toks = lax.optimization_barrier((cot_own.reshape(total_rows, cot_width), toks))
        cot = lax.all_gather(cot_own, "mp", axis=0, tiled=False)

        def in_order(pieces):
            out = jnp.zeros((groups, 2, share // 2, units), BF)
            for k, pair in pieces.items():
                if isinstance(pair, tuple):
                    for side in range(2):
                        out = lax.dynamic_update_slice(out, pair[side][None, None], (g ^ k, side, 0, 0))
                else:
                    out = lax.dynamic_update_slice(out, pair[None], (g ^ k, 0, 0, 0))
            return out.reshape(total_rows, units)

        def sums(weight, first, name):
            keep = [k for k in range(groups) if not k & first]
            send = [k for k in range(groups) if k & first]
            sent = chunks_product(index, toks, weight.T, send, groups, name)
            return sent, lambda: chunks_product(index, toks, weight.T, keep, groups, name)

        gate_send, gate_keep = sums(trunk_gate, 1, "trunk_gate")
        up_send, up_keep = sums(trunk_up, 2, "trunk_up")
        gate_r = plan.halving(gate_keep(), gate_send, 1)
        up_r = plan.halving(up_keep(), up_send, 2)
        hid_r = (jax.nn.silu(gate_r) * up_r).astype(BF)
        hidden = in_order(plan.gather(hid_r.reshape(2, share // 2, units))[0])
        sides = hidden.reshape(2, half_rows, units)
        came = plan.core_swap(dot_nn(row(sides, 1 - c), trunk_down).astype(BF))
        part = (dot_nn(row(sides, c), trunk_down) + came.astype(F32)).astype(BF)
        part, cot, pair = tie(part, cot, jnp.stack([gate_r, up_r]).astype(BF))
        have = plan.hop_one(pair)
        ghid_own = ghid_product(index, groups, cot, head_down[0])
        beside = (ghid_own, *(have[k] for k in sorted(have)))
        summed, (ghid_own, *got) = plan.place_sum(part.reshape(places, rows, width), z, beside)
        have = dict(zip(sorted(have), got))
        shard = (own_tok.astype(F32) + summed).astype(BF)
        shard, have, cot = lax.optimization_barrier((shard, have, cot))
        rest = plan.hop_two(have)
        ghid_mate = ghid_product(index, groups + 1, cot, head_down[0])
        block, (ghid_mate, rest) = plan.place_gather(shard, z, (ghid_mate, rest))
        have = have | rest
        gates, ups = ([have[k][i] for k in range(groups)] for i in range(2))
        block = block.reshape(2, half_rows // 2, width)

        gate_t, up_t = head_gate[0].T, head_up[0].T
        def both_cores(pair):
            own = (jnp.stack(pair) if isinstance(pair, tuple) else pair).reshape(half_rows, width)
            return own, plan.core_swap(own)

        def first_product():
            return pre_product(index, 0, [both_cores(block)], gate_t, up_t)

        def second_product(have, begun):
            return pre_product(index, 1, [both_cores(have[1])], gate_t, up_t, begun)

        wide, (pre, lin) = plan.gather(block, first_product, second_product)
        pieces = [both_cores(wide[k]) for k in range(2, groups)]
        dgate, dup, *last_block = act_product(
            index, 2, pieces, gate_t, up_t, pre, lin, (ghid_own, ghid_mate), cot, places, groups
        )

        def make(offset, count, hops, hold):
            if groups == 4 and offset == groups - 1:
                own, mate = last_block
            else:
                own, mate = back_product(index, offset, count, *hold, gate_t, up_t, cot, places, groups)
            if hops is not None:
                own, mate, hops = lax.optimization_barrier((own, mate, hops))
            total = own.astype(F32) + plan.core_swap(mate).astype(F32)
            parts = {offset + i: total[i].reshape(2, half_rows // 2, width) for i in range(count)}
            return parts if hops is None else (parts, hops)

        cols = plan.scatter(make, (dgate, dup))
        dshard = plan.place_sum(cols.astype(BF).reshape(places, rows, width), z)[0].astype(BF)
        dhalf = plan.place_gather(dshard, z)[0].reshape(half_rows, width)
        dmate = plan.core_swap(dhalf)
        grad_mid = jnp.zeros((2, half_rows, width), BF)
        grad_mid = lax.dynamic_update_index_in_dim(grad_mid, dhalf, c, 0)
        grad_mid = lax.dynamic_update_index_in_dim(grad_mid, dmate, 1 - c, 0).reshape(total_rows, width)

        back = chunks_product(index, grad_mid, trunk_down, list(range(groups)), groups, "trunk_hidden_grad")
        back = back.reshape(groups, 2, share // 2, units)

        def chunks(offset, count, hops, hold):
            parts = {offset + i: back[offset + i] for i in range(count)}
            return parts if hops is None else (parts, hops)

        ghid_t = plan.scatter(chunks, ()).astype(BF)
        wide, (grad_down,) = plan.gather(ghid_t, lambda: (dot(hidden, grad_mid, ((0,), (0,))),))
        ghids = [wide[k] for k in range(groups)]
        dgate_t, dup_t, own, mate = trunk_act(index, ghids, gates, ups, trunk_gate.T, trunk_up.T)
        part = (own.astype(F32) + plan.core_swap(mate).astype(F32)).astype(BF)
        part, dgate_t, dup_t = tie(part, dgate_t, dup_t)
        grads = grads_product(index, dgate_t, dup_t, toks)
        summed, (grad_gate, grad_up) = plan.place_sum(part.reshape(places, rows, width), z, grads)
        grad_x = (dshard.astype(F32) + summed).astype(BF)
        grad_gate, grad_up = grad_gate.T, grad_up.T
        return (grad_x, grad_gate, grad_up, grad_down)

    return body


def solution(mesh):
    return jax.shard_map(
        make_body(Plan(mesh)),
        mesh=mesh,
        in_specs=(
            P(None, "group"),
            P("group", "mp"),
            P("group", "mp"),
            P("mp", "group"),
            P("group", None, "mp"),
            P("group", None, "mp"),
            P("group", "mp", None),
            P("group", None, "mp"),
        ),
        out_specs=(P("mp", "group"), P("group", "mp"), P("group", "mp"), P("mp", "group")),
        check_vma=False,
    )
```

time: 401 us -> 360 us (0.90)
  waiting for transfers between devices: 202 us -> 129 us
  Pallas kernels: 86.1 us -> 112 us
  starting transfers between devices: 38.7 us -> 54.9 us
  matrix products: 21.6 us -> 10.9 us
  local copies, waits for them, and re-layouts: 18.8 us -> 24 us
    ppermute x24 -> x28, waiting for transfers between devices: 135 us -> 80.1 us  [group_swap(): lax.ppermute(value, 'group', [(i, i ^ mask) for i in range(self.groups)])]
    ppermute x15, waiting for transfers between devices: 62.8 us -> 34.2 us  [place_swap(): lax.ppermute(value, 'mp', [(i, i ^ 2 * mask) for i in range(self.members)])]
    pallas_call x9 -> x14, Pallas kernels: 86.1 us -> 112 us  [call(): pl.pallas_call(kernel, grid_spec=pltpu.PrefetchScalarGridSpec(num_scalar_...]
    ppermute x24 -> x28, starting transfers between devices: 18.8 us -> 34.2 us  [group_swap(): lax.ppermute(value, 'group', [(i, i ^ mask) for i in range(self.groups)])]
    dot_general x6 -> x3, matrix products: 21.6 us -> 10.9 us  [dot(): lax.dot_general(left, right, (dims, ((), ())), preferred_element_type=F32)]
    ppermute x10, waiting for transfers between devices: 4.31 us -> 14.3 us  [core_swap(): return lax.ppermute(value, 'mp', [(i, i ^ 1) for i in range(self.members)])]
    squeeze x6 -> x9, local copies, waits for them, and re-layouts: 0.26 us -> 5.92 us  [the longest x4 4.41 us: hop_two(): return {3: (self.group_swap(have[2][0], 1), self.group_swap(have[1][1], 2))}]
    unnamed x50 -> x46, local copies, waits for them, and re-layouts: 12.6 us -> 8.63 us
  transfers between devices with their start and end apart: 50 -> 54, of which waited for: 36 -> 36; matrix products, arithmetic and copies ran while one was open for 8% -> 7% of each run, Pallas kernels for 15% -> 20%
where the time goes in v2:
time: 360 us; the launch traced here: 353 us
  waiting for transfers between devices  129 us (36%)
  Pallas kernels  112 us (31%)
  starting transfers between devices  54.9 us (15%)
  local copies, waits for them, and re-layouts  24 us (7%)
  between operations  15.2 us (4%)
  matrix products  10.9 us (3%)
  other arithmetic  7.5 us (2%)
    pallas_call x14, Pallas kernels, call(): pl.pallas_call(kernel, grid_spec=pltpu.PrefetchScalarGridSpec(num_scalar_...  112 us
    ppermute x28, waiting for transfers between devices, group_swap(): lax.ppermute(value, 'group', [(i, i ^ mask) for i in range(self.groups)])  80.1 us
    ppermute x15, waiting for transfers between devices, place_swap(): lax.ppermute(value, 'mp', [(i, i ^ 2 * mask) for i in range(self.members)])  34.2 us
    ppermute x28, starting transfers between devices, group_swap(): lax.ppermute(value, 'group', [(i, i ^ mask) for i in range(self.groups)])  34.2 us
    ppermute x15, starting transfers between devices, place_swap(): lax.ppermute(value, 'mp', [(i, i ^ 2 * mask) for i in range(self.members)])  19.3 us
    ppermute x10, waiting for transfers between devices, core_swap(): return lax.ppermute(value, 'mp', [(i, i ^ 1) for i in range(self.members)])  14.3 us
    dot_general x3, matrix products, dot(): lax.dot_general(left, right, (dims, ((), ())), preferred_element_type=F32)  10.9 us
    unnamed x46, local copies, waits for them, and re-layouts  8.63 us
  transfers between devices with their start and end apart: 54, of which 36 were waited for; matrix products, arithmetic and copies ran while one was open for 7% of the time, Pallas kernels for 20%

profile of v2, /device:TPU:18, one launch (start us, length us, event | category | flops | bytes accessed | tf_op | source)
XLA Modules:
  0.0 353.2 jit_solution(10832020876151225248)
XLA Ops:
  9.7 1.8 copy-done.3
  11.5 1.7 trunk_gate.3
  13.9 1.8 trunk_up.3
  17.2 1.8 trunk_gate.2
  19.0 1.8 trunk_up.2
  20.8 14.3 %collective-permute-done = bf16[2,160,1376]{2,1,0:T(8,128)(2,1)S(1)} collective-permute-done((bf16[2,160,1376]{2,1,0:T(8,128)(2,1)S(1)}, bf16[2,160,1376]{2,1,0:T(8,128)(2,1)S(1)}, u32[]{:S(2)}, u32[]{:S(2)}) %collective-permute-start) | collective-permute-done | bytes 880672 | tf_op jit(solution)/shard_map/ppermute | solution.py:65
  37.6 2.5 collective-permute-start.3
  40.1 6.7 %collective-permute-done.1 = bf16[1,160,1376]{2,1,0:T(8,128)(2,1)S(1)} collective-permute-done((bf16[1,160,1376]{2,1,0:T(8,128)(2,1)S(1)}, bf16[1,160,1376]{2,1,0:T(8,128)(2,1)S(1)}, u32[]{:S(2)}, u32[]{:S(2)}) %collective-permute-start.1) | collective-permute-done | bytes 440352 | tf_op jit(solution)/shard_map/ppermute | solution.py:65
  51.9 6.6 %collective-permute-done.4 = bf16[2,80,1376]{2,1,0:T(8,128)(2,1)S(1)} collective-permute-done((bf16[2,80,1376]{2,1,0:T(8,128)(2,1)S(1)}, bf16[2,80,1376]{2,1,0:T(8,128)(2,1)S(1)}, u32[]{:S(2)}, u32[]{:S(2)}) %collective-permute-start.4) | collective-permute-done | bytes 440352 | tf_op jit(solution)/shard_map/ppermute | solution.py:65
  64.5 2.5 collective-permute-done.6
  67.6 2.0 convolution_convert_fusion
  69.7 2.3 collective-permute-done.8
  72.0 4.0 %add_convert_fusion.3 = bf16[320,1024]{1,0:T(8,128)(2,1)} fusion(bf16[320,1024]{1,0:T(8,128)(2,1)} %collective-permute-done.8, bf16[1376,1024]{1,0:T(8,128)(2,1)} %refs_4_.1, bf16[2,320,1376]{2,1,0:T(8,128)(2,1)S(1)} %bitcast.255, s32[]{:T(128)S(6)} %select_n.75), kind=kOutput, calls=%fused_computation.8 | convolution fusion | flops 902758400 | bytes 5029892 | tf_op jit(solution)/shard_map/dot_general | solution.py:21
  80.9 2.7 collective-permute-start.11
  84.8 2.5 copy-done
  87.3 11.1 %head_hidden_grad.2.refs_8_ = f32[320,1376]{1,0:T(8,128)S(1)} custom-call(s32[8]{0:T(128)S(1)} %stack.84.index, bf16[8,640,512]{2,1,0:T(8,128)(2,1)S(1)} %bitcast.201, bf16[1376,4096]{1,0:T(8,128)(2,1)} %bitcast.237), custom_call_target="tpu_custom_call" | custom-call | flops 3607101440 | bytes 16515072 | tf_op jit(solution)/shard_map/head_hidden_grad/pallas_call | solution.py:46
  100.7 1.8 collective-permute-start.14
  107.8 10.6 %head_hidden_grad.3.refs_9_ = f32[320,1376]{1,0:T(8,128)S(1)} custom-call(s32[8]{0:T(128)S(1)} %stack.84.index, bf16[8,640,512]{2,1,0:T(8,128)(2,1)S(1)} %bitcast.202, bf16[1376,4096]{1,0:T(8,128)(2,1)} %bitcast.238), custom_call_target="tpu_custom_call" | custom-call | flops 3607101440 | bytes 16515072 | tf_op jit(solution)/shard_map/head_hidden_grad/pallas_call | solution.py:46
  125.7 9.8 %head_pre.2 = (f32[640,1376]{1,0:T(8,128)}, f32[640,1376]{1,0:T(8,128)}) custom-call(s32[8]{0:T(128)} %copy-done.11, bf16[320,1024]{1,0:T(8,128)(2,1)} %bitcast.47.refs_0_, bf16[320,1024]{1,0:T(8,128)(2,1)} %collective-permute-done.21.refs_1_, bf16[1376,4096]{1,0:T(8,128)(2,1)} %bitcast.227, bf16[1376,4096]{1,0:T(8,128)(2,1)} %bitcast.232), custom_call_target="tpu_custom_call" | custom-call | flops 3607101440 | bytes 23855104 | tf_op jit(solution)/shard_map/head_pre/pallas_call | solution.py:46
  135.6 5.2 %collective-permute-done.19 = bf16[2,160,1024]{2,1,0:T(8,128)(2,1)} collective-permute-done((bf16[2,160,1024]{2,1,0:T(8,128)(2,1)}, bf16[2,160,1024]{2,1,0:T(8,128)(2,1)}, u32[]{:S(2)}, u32[]{:S(2)}) %collective-permute-start.19) | collective-permute-done | bytes 655392 | tf_op jit(solution)/shard_map/ppermute | solution.py:65
  146.5 11.9 %head_pre.3 = (f32[640,1376]{1,0:T(8,128)}, f32[640,1376]{1,0:T(8,128)}) custom-call(s32[8]{0:T(128)} %copy-done.11, bf16[320,1024]{1,0:T(8,128)(2,1)} %bitcast.55.refs_0_, bf16[320,1024]{1,0:T(8,128)(2,1)} %collective-permute-done.25.refs_1_, bf16[1376,4096]{1,0:T(8,128)(2,1)} %bitcast.228, bf16[1376,4096]{1,0:T(8,128)(2,1)} %bitcast.233, ...), custom_call_target="tpu_custom_call" | custom-call | flops 3607101440 | bytes 30900224 | tf_op jit(solution)/shard_map/head_pre/pallas_call | solution.py:46
  163.5 23.2 %head_act.1 = (bf16[640,1376]{1,0:T(8,128)(2,1)}, bf16[640,1376]{1,0:T(8,128)(2,1)}, bf16[1,320,1024]{2,1,0:T(8,128)(2,1)}, bf16[1,320,1024]{2,1,0:T(8,128)(2,1)}) custom-call(s32[8]{0:T(128)} %copy-done.11, bf16[320,1024]{1,0:T(8,128)(2,1)} %bitcast.52.refs_0_, bf16[320,1024]{1,0:T(8,128)(2,1)} %collective-permute-done.22.refs_1_, ...), custom_call_target="tpu_custom_call" | custom-call | flops 10821304320 | bytes 40976384 | tf_op jit(solution)/shard_map/head_act/pallas_call | solution.py:46
  187.1 1.9 collective-permute-done.27
  193.5 12.6 %head_back.2 = (bf16[2,320,1024]{2,1,0:T(8,128)(2,1)S(1)}, bf16[2,320,1024]{2,1,0:T(8,128)(2,1)S(1)}) custom-call(s32[8]{0:T(128)S(1)} %copy-done.12, bf16[640,1376]{1,0:T(8,128)(2,1)S(1)} %copy-done.7, bf16[640,1376]{1,0:T(8,128)(2,1)} %get-tuple-element.143.dup, bf16[1376,4096]{1,0:T(8,128)(2,1)} %bitcast.230, bf16[1376,4096]{1,0:T(8,128)(2,1)} %bitcast.235, ...), custom_call_target="tpu_custom_call" | custom-call | flops 7214202880 | bytes 31309824 | tf_op jit(solution)/shard_map/head_back/pallas_call | solution.py:46
  206.2 3.0 collective-permute-done.30
  211.7 7.5 %head_back.3 = (bf16[1,320,1024]{2,1,0:T(8,128)(2,1)S(1)}, bf16[1,320,1024]{2,1,0:T(8,128)(2,1)S(1)}) custom-call(s32[8]{0:T(128)S(1)} %copy-done.12, bf16[640,1376]{1,0:T(8,128)(2,1)S(1)} %copy-done.7, bf16[640,1376]{1,0:T(8,128)(2,1)S(1)} %copy-done.8, bf16[1376,4096]{1,0:T(8,128)(2,1)} %bitcast.231, bf16[1376,4096]{1,0:T(8,128)(2,1)} %bitcast.236, ...), custom_call_target="tpu_custom_call" | custom-call | flops 3607101440 | bytes 31309824 | tf_op jit(solution)/shard_map/head_back/pallas_call | solution.py:46
  221.5 14.8 %collective-permute-done.32 = bf16[2,160,1024]{2,1,0:T(8,128)(2,1)S(1)} collective-permute-done((bf16[2,160,1024]{2,1,0:T(8,128)(2,1)S(1)}, bf16[2,160,1024]{2,1,0:T(8,128)(2,1)S(1)}, u32[]{:S(2)}, u32[]{:S(2)}) %collective-permute-start.32) | collective-permute-done | bytes 655392 | tf_op jit(solution)/shard_map/ppermute | solution.py:65
  236.9 2.6 collective-permute-start.34
  241.1 3.6 %collective-permute-done.34 = bf16[80,1024]{1,0:T(8,128)(2,1)S(1)} collective-permute-done((bf16[80,1024]{1,0:T(8,128)(2,1)S(1)}, bf16[80,1024]{1,0:T(8,128)(2,1)S(1)}, u32[]{:S(2)}, u32[]{:S(2)}) %collective-permute-start.34) | collective-permute-done | bytes 163872 | tf_op jit(solution)/shard_map/ppermute | solution.py:71
  244.7 6.6 %collective-permute-done.35 = bf16[80,1024]{1,0:T(8,128)(2,1)S(1)} collective-permute-done((bf16[80,1024]{1,0:T(8,128)(2,1)S(1)}, bf16[80,1024]{1,0:T(8,128)(2,1)S(1)}, u32[]{:S(2)}, u32[]{:S(2)}) %collective-permute-start.35) | collective-permute-done | bytes 163872 | tf_op jit(solution)/shard_map/ppermute | solution.py:71
  251.3 3.9 %collective-permute-done.36 = bf16[80,1024]{1,0:T(8,128)(2,1)S(1)} collective-permute-done((bf16[80,1024]{1,0:T(8,128)(2,1)S(1)}, bf16[80,1024]{1,0:T(8,128)(2,1)S(1)}, u32[]{:S(2)}, u32[]{:S(2)}) %collective-permute-start.36) | collective-permute-done | bytes 163872 | tf_op jit(solution)/shard_map/ppermute | solution.py:71
  255.4 1.9 collective-permute-start.38
  258.8 3.6 %collective-permute-done.37 = bf16[80,1024]{1,0:T(8,128)(2,1)S(1)} collective-permute-done((bf16[80,1024]{1,0:T(8,128)(2,1)S(1)}, bf16[80,1024]{1,0:T(8,128)(2,1)S(1)}, u32[]{:S(2)}, u32[]{:S(2)}) %collective-permute-start.37) | collective-permute-done | bytes 163872 | tf_op jit(solution)/shard_map/ppermute | solution.py:71
  262.5 5.4 %collective-permute-done.38 = bf16[80,1024]{1,0:T(8,128)(2,1)S(1)} collective-permute-done((bf16[80,1024]{1,0:T(8,128)(2,1)S(1)}, bf16[80,1024]{1,0:T(8,128)(2,1)S(1)}, u32[]{:S(2)}, u32[]{:S(2)}) %collective-permute-start.38) | collective-permute-done | bytes 163872 | tf_op jit(solution)/shard_map/ppermute | solution.py:71
  267.9 3.9 %collective-permute-done.39 = bf16[80,1024]{1,0:T(8,128)(2,1)S(1)} collective-permute-done((bf16[80,1024]{1,0:T(8,128)(2,1)S(1)}, bf16[80,1024]{1,0:T(8,128)(2,1)S(1)}, u32[]{:S(2)}, u32[]{:S(2)}) %collective-permute-start.39) | collective-permute-done | bytes 163872 | tf_op jit(solution)/shard_map/ppermute | solution.py:71
  272.3 1.8 collective-permute-done.40
  274.2 2.8 trunk_hidden_grad.1
  279.2 5.5 %collective-permute-done.41 = bf16[80,1376]{1,0:T(8,128)(2,1)S(1)} collective-permute-done((bf16[80,1376]{1,0:T(8,128)(2,1)S(1)}, bf16[80,1376]{1,0:T(8,128)(2,1)S(1)}, u32[]{:S(2)}, u32[]{:S(2)}) %collective-permute-start.41) | collective-permute-done | bytes 220192 | tf_op jit(solution)/shard_map/ppermute | solution.py:65
  288.3 8.3 %collective-permute-done.43 = bf16[2,80,1376]{2,1,0:T(8,128)(2,1)S(1)} collective-permute-done((bf16[2,80,1376]{2,1,0:T(8,128)(2,1)S(1)}, bf16[2,80,1376]{2,1,0:T(8,128)(2,1)S(1)}, u32[]{:S(2)}, u32[]{:S(2)}) %collective-permute-start.43) | collective-permute-done | bytes 440352 | tf_op jit(solution)/shard_map/ppermute | solution.py:65
  300.0 4.9 %fusion.35 = f32[1376,1024]{1,0:T(8,128)} fusion(bf16[640,1376]{1,0:T(8,128)(2,1)S(1)} %bitcast.256, bf16[640,1024]{1,0:T(8,128)(2,1)S(1)} %bitcast.216), kind=kOutput, calls=%fused_computation.106 | convolution fusion | flops 1803550720 | bytes 8708096 | tf_op jit(solution)/shard_map/dot_general | solution.py:21
  304.9 3.5 collective-permute-done.45
  311.7 2.8 collective-permute-done.47.refs_6_
  316.2 8.4 %trunk_act.1 = (bf16[640,1376]{1,0:T(8,128)(2,1)S(1)}, bf16[640,1376]{1,0:T(8,128)(2,1)S(1)}, bf16[320,1024]{1,0:T(8,128)(2,1)S(1)}, bf16[320,1024]{1,0:T(8,128)(2,1)S(1)}) custom-call(s32[8]{0:T(128)S(1)} %copy-done.12, bf16[80,1376]{1,0:T(8,128)(2,1)S(1)} %get-tuple-element.220.refs_0_, bf16[80,1376]{1,0:T(8,128)(2,1)S(1)} %get-tuple-element.219.refs_1_, ...), custom_call_target="tpu_custom_call" | custom-call | flops 3607101440 | bytes 10919936 | tf_op jit(solution)/shard_map/trunk_act/pallas_call | solution.py:46
  324.7 2.1 collective-permute-done.49
  328.7 1.9 collective-permute-start.52
  330.6 7.3 %trunk_weight_grads.1 = (f32[1376,1024]{1,0:T(8,128)}, f32[1376,1024]{1,0:T(8,128)}) custom-call(s32[8]{0:T(128)S(1)} %copy-done.12, bf16[640,1376]{1,0:T(8,128)(2,1)S(1)} %get-tuple-element.170.dgate, bf16[640,1376]{1,0:T(8,128)(2,1)S(1)} %get-tuple-element.171.dup, bf16[640,1024]{1,0:T(8,128)(2,1)S(1)} %bitcast.211), custom_call_target="tpu_custom_call" | custom-call | flops 3607101440 | bytes 4833280 | tf_op jit(solution)/shard_map/trunk_weight_grads/pallas_call | solution.py:46
  338.0 2.4 collective-permute-done.51
  340.3 4.8 %collective-permute-done.52 = bf16[80,1024]{1,0:T(8,128)(2,1)S(1)} collective-permute-done((bf16[80,1024]{1,0:T(8,128)(2,1)S(1)}, bf16[80,1024]{1,0:T(8,128)(2,1)S(1)}, u32[]{:S(2)}, u32[]{:S(2)}) %collective-permute-start.52) | collective-permute-done | bytes 163872 | tf_op jit(solution)/shard_map/ppermute | solution.py:71
  (186 shorter events, 81.5 us)
Async XLA Ops:
  7.2 68.9 %all-gather.3.cloned.1.call-start = ((), (), s32[]{:S(2)}) async-start(), calls=%async_computation | async-start | bytes 5898240 | tf_op jit(solution)/shard_map/all_gather | solution.py:419
  13.3 21.8 %collective-permute-start = (bf16[2,160,1376]{2,1,0:T(8,128)(2,1)S(1)}, bf16[2,160,1376]{2,1,0:T(8,128)(2,1)S(1)}, u32[]{:S(2)}, u32[]{:S(2)}) collective-permute-start(bf16[2,160,1376]{2,1,0:T(8,128)(2,1)S(1)} %bitcast.226), channel_id=1, source_target_pairs={{0,8},{8,0},{16,24},{24,16},{1,9},{9,1},{17,25},{25,17},{2,10},{10... | collective-permute-start | bytes 2641928 | tf_op jit(solution)/shard_map/ppermute | solution.py:65
  15.7 21.7 %collective-permute-start.2 = (bf16[2,160,1376]{2,1,0:T(8,128)(2,1)S(1)}, bf16[2,160,1376]{2,1,0:T(8,128)(2,1)S(1)}, u32[]{:S(2)}, u32[]{:S(2)}) collective-permute-start(bf16[2,160,1376]{2,1,0:T(8,128)(2,1)S(1)} %bitcast.225), channel_id=1, source_target_pairs={{0,16},{8,24},{16,0},{24,8},{1,17},{9,25},{17,1},{25,9},{2,18},{10... | collective-permute-start | bytes 2641928 | tf_op jit(solution)/shard_map/ppermute | solution.py:65
  35.3 11.5 %collective-permute-start.1 = (bf16[1,160,1376]{2,1,0:T(8,128)(2,1)S(1)}, bf16[1,160,1376]{2,1,0:T(8,128)(2,1)S(1)}, u32[]{:S(2)}, u32[]{:S(2)}) collective-permute-start(bf16[1,160,1376]{2,1,0:T(8,128)(2,1)S(1)} %slice.197), channel_id=1, source_target_pairs={{0,16},{8,24},{16,0},{24,8},{1,17},{9,25},{17,1},{25,9},{2,18},{10... | collective-permute-start | bytes 1320968 | tf_op jit(solution)/shard_map/ppermute | solution.py:65
  37.6 10.9 %collective-permute-start.3 = (bf16[1,160,1376]{2,1,0:T(8,128)(2,1)S(1)}, bf16[1,160,1376]{2,1,0:T(8,128)(2,1)S(1)}, u32[]{:S(2)}, u32[]{:S(2)}) collective-permute-start(bf16[1,160,1376]{2,1,0:T(8,128)(2,1)S(1)} %slice.196), channel_id=1, source_target_pairs={{0,8},{8,0},{16,24},{24,16},{1,9},{9,1},{17,25},{25,17},{2,10},{10... | collective-permute-start | bytes 1320968 | tf_op jit(solution)/shard_map/ppermute | solution.py:65
  48.8 9.7 %collective-permute-start.4 = (bf16[2,80,1376]{2,1,0:T(8,128)(2,1)S(1)}, bf16[2,80,1376]{2,1,0:T(8,128)(2,1)S(1)}, u32[]{:S(2)}, u32[]{:S(2)}) collective-permute-start(bf16[2,80,1376]{2,1,0:T(8,128)(2,1)S(1)} %multiply_convert_fusion), channel_id=1, source_target_pairs={{0,8},{8,0},{16,24},{24,16},{1,9},{9,1},{17,25},{25,17},{2,10},{10... | collective-permute-start | bytes 1320968 | tf_op jit(solution)/shard_map/ppermute | solution.py:65
  50.4 9.7 %collective-permute-start.5 = (bf16[2,80,1376]{2,1,0:T(8,128)(2,1)S(1)}, bf16[2,80,1376]{2,1,0:T(8,128)(2,1)}, u32[]{:S(2)}, u32[]{:S(2)}) collective-permute-start(bf16[2,80,1376]{2,1,0:T(8,128)(2,1)S(1)} %multiply_convert_fusion), channel_id=1, source_target_pairs={{0,16},{8,24},{16,0},{24,8},{1,17},{9,25},{17,1},{25,9},{2,18},{10... | collective-permute-start | bytes 1320968 | tf_op jit(solution)/shard_map/ppermute | solution.py:65
  61.0 6.0 %collective-permute-start.6 = (bf16[80,1376]{1,0:T(8,128)(2,1)S(1)}, bf16[80,1376]{1,0:T(8,128)(2,1)S(1)}, u32[]{:S(2)}, u32[]{:S(2)}) collective-permute-start(bf16[80,1376]{1,0:T(8,128)(2,1)S(1)} %slice_bitcast_fusion.23), channel_id=1, source_target_pairs={{0,8},{8,0},{16,24},{24,16},{1,9},{9,1},{17,25},{25,17},{2,10},{10... | collective-permute-start | bytes 660488 | tf_op jit(solution)/shard_map/ppermute | solution.py:65
  61.4 6.0 %collective-permute-start.7 = (bf16[80,1376]{1,0:T(8,128)(2,1)S(1)}, bf16[80,1376]{1,0:T(8,128)(2,1)S(1)}, u32[]{:S(2)}, u32[]{:S(2)}) collective-permute-start(bf16[80,1376]{1,0:T(8,128)(2,1)S(1)} %slice_bitcast_fusion.22), channel_id=1, source_target_pairs={{0,16},{8,24},{16,0},{24,8},{1,17},{9,25},{17,1},{25,9},{2,18},{10... | collective-permute-start | bytes 660488 | tf_op jit(solution)/shard_map/ppermute | solution.py:65
  69.6 2.4 collective-permute-start.8
  76.1 22.4 %collective-permute-start.12 = (bf16[2,160,1376]{2,1,0:T(8,128)(2,1)S(1)}, bf16[2,160,1376]{2,1,0:T(8,128)(2,1)S(1)}, u32[]{:S(2)}, u32[]{:S(2)}) collective-permute-start(bf16[2,160,1376]{2,1,0:T(8,128)(2,1)S(1)} %pad_maximum_fusion), channel_id=1, source_target_pairs={{0,8},{8,0},{16,24},{24,16},{1,9},{9,1},{17,25},{25,17},{2,10},{10... | collective-permute-start | bytes 2641928 | tf_op jit(solution)/shard_map/ppermute | solution.py:65
  77.7 21.9 %collective-permute-start.13 = (bf16[2,160,1376]{2,1,0:T(8,128)(2,1)S(1)}, bf16[2,160,1376]{2,1,0:T(8,128)(2,1)}, u32[]{:S(2)}, u32[]{:S(2)}) collective-permute-start(bf16[2,160,1376]{2,1,0:T(8,128)(2,1)S(1)} %pad_maximum_fusion), channel_id=1, source_target_pairs={{0,16},{8,24},{16,0},{24,8},{1,17},{9,25},{17,1},{25,9},{2,18},{10... | collective-permute-start | bytes 2641928 | tf_op jit(solution)/shard_map/ppermute | solution.py:65
  80.4 18.0 %collective-permute-start.10 = (bf16[80,1024]{1,0:T(8,128)(2,1)S(1)}, bf16[80,1024]{1,0:T(8,128)(2,1)S(1)}, u32[]{:S(2)}, u32[]{:S(2)}) collective-permute-start(bf16[80,1024]{1,0:T(8,128)(2,1)S(1)} %get-tuple-element.213), channel_id=1, source_target_pairs={{0,4},{1,5},{2,6},{3,7},{4,0},{5,1},{6,2},{7,3},{8,12},{9,13},{10,... | collective-permute-start | bytes 491528 | tf_op jit(solution)/shard_map/ppermute | solution.py:71
  80.9 17.5 %collective-permute-start.11 = (bf16[80,1024]{1,0:T(8,128)(2,1)S(1)}, bf16[80,1024]{1,0:T(8,128)(2,1)S(1)}, u32[]{:S(2)}, u32[]{:S(2)}) collective-permute-start(bf16[80,1024]{1,0:T(8,128)(2,1)S(1)} %get-tuple-element.212), channel_id=1, source_target_pairs={{0,6},{1,7},{2,4},{3,5},{4,2},{5,3},{6,0},{7,1},{8,14},{9,15},{10,... | collective-permute-start | bytes 491528 | tf_op jit(solution)/shard_map/ppermute | solution.py:71
  83.6 14.8 %collective-permute-start.9 = (bf16[80,1024]{1,0:T(8,128)(2,1)S(1)}, bf16[80,1024]{1,0:T(8,128)(2,1)S(1)}, u32[]{:S(2)}, u32[]{:S(2)}) collective-permute-start(bf16[80,1024]{1,0:T(8,128)(2,1)S(1)} %get-tuple-element.214), channel_id=1, source_target_pairs={{0,2},{1,3},{2,0},{3,1},{4,6},{5,7},{6,4},{7,5},{8,10},{9,11},{10,... | collective-permute-start | bytes 491528 | tf_op jit(solution)/shard_map/ppermute | solution.py:71
  100.7 20.5 %collective-permute-start.14 = (bf16[80,1024]{1,0:T(8,128)(2,1)S(1)}, bf16[80,1024]{1,0:T(8,128)(2,1)S(1)}, u32[]{:S(2)}, u32[]{:S(2)}) collective-permute-start(bf16[80,1024]{1,0:T(8,128)(2,1)S(1)} %fusion.24), channel_id=1, source_target_pairs={{0,2},{1,3},{2,0},{3,1},{4,6},{5,7},{6,4},{7,5},{8,10},{9,11},{10,... | collective-permute-start | bytes 491528 | tf_op jit(solution)/shard_map/ppermute | solution.py:71
  102.5 18.8 %collective-permute-start.15 = (bf16[80,1024]{1,0:T(8,128)(2,1)S(1)}, bf16[80,1024]{1,0:T(8,128)(2,1)S(1)}, u32[]{:S(2)}, u32[]{:S(2)}) collective-permute-start(bf16[80,1024]{1,0:T(8,128)(2,1)S(1)} %fusion.24), channel_id=1, source_target_pairs={{0,4},{1,5},{2,6},{3,7},{4,0},{5,1},{6,2},{7,3},{8,12},{9,13},{10,... | collective-permute-start | bytes 491528 | tf_op jit(solution)/shard_map/ppermute | solution.py:71
  102.7 18.5 %collective-permute-start.16 = (bf16[80,1024]{1,0:T(8,128)(2,1)S(1)}, bf16[80,1024]{1,0:T(8,128)(2,1)S(1)}, u32[]{:S(2)}, u32[]{:S(2)}) collective-permute-start(bf16[80,1024]{1,0:T(8,128)(2,1)S(1)} %fusion.24), channel_id=1, source_target_pairs={{0,6},{1,7},{2,4},{3,5},{4,2},{5,3},{6,0},{7,1},{8,14},{9,15},{10,... | collective-permute-start | bytes 491528 | tf_op jit(solution)/shard_map/ppermute | solution.py:71
  105.6 15.7 %collective-permute-start.17 = (bf16[160,1376]{1,0:T(8,128)(2,1)S(1)}, bf16[160,1376]{1,0:T(8,128)(2,1)S(1)}, u32[]{:S(2)}, u32[]{:S(2)}) collective-permute-start(bf16[160,1376]{1,0:T(8,128)(2,1)S(1)} %get-tuple-element.199.refs_10_), channel_id=1, source_target_pairs={{0,8},{8,0},{16,24},{24,16},{1,9},{9,1},{17,25},{25,17},{2,10},{10... | collective-permute-start | bytes 1320968 | tf_op jit(solution)/shard_map/ppermute | solution.py:65
  106.2 15.0 %collective-permute-start.18 = (bf16[160,1376]{1,0:T(8,128)(2,1)S(1)}, bf16[160,1376]{1,0:T(8,128)(2,1)S(1)}, u32[]{:S(2)}, u32[]{:S(2)}) collective-permute-start(bf16[160,1376]{1,0:T(8,128)(2,1)S(1)} %get-tuple-element.203.refs_13_), channel_id=1, source_target_pairs={{0,16},{8,24},{16,0},{24,8},{1,17},{9,25},{17,1},{25,9},{2,18},{10... | collective-permute-start | bytes 1320968 | tf_op jit(solution)/shard_map/ppermute | solution.py:65
  123.3 17.5 %collective-permute-start.19 = (bf16[2,160,1024]{2,1,0:T(8,128)(2,1)}, bf16[2,160,1024]{2,1,0:T(8,128)(2,1)}, u32[]{:S(2)}, u32[]{:S(2)}) collective-permute-start(bf16[2,160,1024]{2,1,0:T(8,128)(2,1)} %bitcast.46), channel_id=1, source_target_pairs={{0,8},{8,0},{16,24},{24,16},{1,9},{9,1},{17,25},{25,17},{2,10},{10... | collective-permute-start | bytes 1966088 | tf_op jit(solution)/shard_map/ppermute | solution.py:65
  124.8 17.2 %collective-permute-start.20 = (bf16[2,160,1024]{2,1,0:T(8,128)(2,1)}, bf16[2,160,1024]{2,1,0:T(8,128)(2,1)}, u32[]{:S(2)}, u32[]{:S(2)}) collective-permute-start(bf16[2,160,1024]{2,1,0:T(8,128)(2,1)} %bitcast.46), channel_id=1, source_target_pairs={{0,16},{8,24},{16,0},{24,8},{1,17},{9,25},{17,1},{25,9},{2,18},{10... | collective-permute-start | bytes 1966088 | tf_op jit(solution)/shard_map/ppermute | solution.py:65
  142.0 4.4 %collective-permute-start.25 = (bf16[320,1024]{1,0:T(8,128)(2,1)}, bf16[320,1024]{1,0:T(8,128)(2,1)}, u32[]{:S(2)}, u32[]{:S(2)}) collective-permute-start(bf16[320,1024]{1,0:T(8,128)(2,1)} %bitcast.55.refs_0_), channel_id=1, source_target_pairs={{0,1},{1,0},{2,3},{3,2},{4,5},{5,4},{6,7},{7,6},{8,9},{9,8},{10,11... | collective-permute-start | bytes 1966088 | tf_op jit(solution)/shard_map/ppermute | solution.py:68
  143.7 14.6 %collective-permute-start.23 = (bf16[160,1024]{1,0:T(8,128)(2,1)}, bf16[160,1024]{1,0:T(8,128)(2,1)}, u32[]{:S(2)}, u32[]{:S(2)}) collective-permute-start(bf16[160,1024]{1,0:T(8,128)(2,1)} %slice_bitcast_fusion.11), channel_id=1, source_target_pairs={{0,8},{8,0},{16,24},{24,16},{1,9},{9,1},{17,25},{25,17},{2,10},{10... | collective-permute-start | bytes 983048 | tf_op jit(solution)/shard_map/ppermute | solution.py:65
  146.0 12.4 %collective-permute-start.24 = (bf16[160,1024]{1,0:T(8,128)(2,1)}, bf16[160,1024]{1,0:T(8,128)(2,1)}, u32[]{:S(2)}, u32[]{:S(2)}) collective-permute-start(bf16[160,1024]{1,0:T(8,128)(2,1)} %slice_bitcast_fusion.10), channel_id=1, source_target_pairs={{0,16},{8,24},{16,0},{24,8},{1,17},{9,25},{17,1},{25,9},{2,18},{10... | collective-permute-start | bytes 983048 | tf_op jit(solution)/shard_map/ppermute | solution.py:65
  146.5 14.5 %collective-permute-start.22 = (bf16[320,1024]{1,0:T(8,128)(2,1)}, bf16[320,1024]{1,0:T(8,128)(2,1)}, u32[]{:S(2)}, u32[]{:S(2)}) collective-permute-start(bf16[320,1024]{1,0:T(8,128)(2,1)} %bitcast.52.refs_0_), channel_id=1, source_target_pairs={{0,1},{1,0},{2,3},{3,2},{4,5},{5,4},{6,7},{7,6},{8,9},{9,8},{10,11... | collective-permute-start | bytes 1966088 | tf_op jit(solution)/shard_map/ppermute | solution.py:68
  190.4 15.7 %collective-permute-start.28 = (bf16[160,1024]{1,0:T(8,128)(2,1)S(1)}, bf16[160,1024]{1,0:T(8,128)(2,1)S(1)}, u32[]{:S(2)}, u32[]{:S(2)}) collective-permute-start(bf16[160,1024]{1,0:T(8,128)(2,1)S(1)} %get-tuple-element.211), channel_id=1, source_target_pairs={{0,8},{8,0},{16,24},{24,16},{1,9},{9,1},{17,25},{25,17},{2,10},{10... | collective-permute-start | bytes 983048 | tf_op jit(solution)/shard_map/ppermute | solution.py:65
  192.0 14.2 %collective-permute-start.29 = (bf16[160,1024]{1,0:T(8,128)(2,1)S(1)}, bf16[160,1024]{1,0:T(8,128)(2,1)S(1)}, u32[]{:S(2)}, u32[]{:S(2)}) collective-permute-start(bf16[160,1024]{1,0:T(8,128)(2,1)S(1)} %get-tuple-element.210), channel_id=1, source_target_pairs={{0,16},{8,24},{16,0},{24,8},{1,17},{9,25},{17,1},{25,9},{2,18},{10... | collective-permute-start | bytes 983048 | tf_op jit(solution)/shard_map/ppermute | solution.py:65
  206.2 3.1 collective-permute-start.30
  219.3 17.0 %collective-permute-start.32 = (bf16[2,160,1024]{2,1,0:T(8,128)(2,1)S(1)}, bf16[2,160,1024]{2,1,0:T(8,128)(2,1)S(1)}, u32[]{:S(2)}, u32[]{:S(2)}) collective-permute-start(bf16[2,160,1024]{2,1,0:T(8,128)(2,1)S(1)} %get-tuple-element.146), channel_id=1, source_target_pairs={{0,8},{8,0},{16,24},{24,16},{1,9},{9,1},{17,25},{25,17},{2,10},{10... | collective-permute-start | bytes 1966088 | tf_op jit(solution)/shard_map/ppermute | solution.py:65
  219.9 16.7 %collective-permute-start.33 = (bf16[2,160,1024]{2,1,0:T(8,128)(2,1)S(1)}, bf16[2,160,1024]{2,1,0:T(8,128)(2,1)S(1)}, u32[]{:S(2)}, u32[]{:S(2)}) collective-permute-start(bf16[2,160,1024]{2,1,0:T(8,128)(2,1)S(1)} %get-tuple-element.147), channel_id=1, source_target_pairs={{0,16},{8,24},{16,0},{24,8},{1,17},{9,25},{17,1},{25,9},{2,18},{10... | collective-permute-start | bytes 1966088 | tf_op jit(solution)/shard_map/ppermute | solution.py:65
  236.9 7.7 %collective-permute-start.34 = (bf16[80,1024]{1,0:T(8,128)(2,1)S(1)}, bf16[80,1024]{1,0:T(8,128)(2,1)S(1)}, u32[]{:S(2)}, u32[]{:S(2)}) collective-permute-start(bf16[80,1024]{1,0:T(8,128)(2,1)S(1)} %get-tuple-element.209), channel_id=1, source_target_pairs={{0,2},{1,3},{2,0},{3,1},{4,6},{5,7},{6,4},{7,5},{8,10},{9,11},{10,... | collective-permute-start | bytes 491528 | tf_op jit(solution)/shard_map/ppermute | solution.py:71
  239.6 11.7 %collective-permute-start.35 = (bf16[80,1024]{1,0:T(8,128)(2,1)S(1)}, bf16[80,1024]{1,0:T(8,128)(2,1)S(1)}, u32[]{:S(2)}, u32[]{:S(2)}) collective-permute-start(bf16[80,1024]{1,0:T(8,128)(2,1)S(1)} %get-tuple-element.208), channel_id=1, source_target_pairs={{0,4},{1,5},{2,6},{3,7},{4,0},{5,1},{6,2},{7,3},{8,12},{9,13},{10,... | collective-permute-start | bytes 491528 | tf_op jit(solution)/shard_map/ppermute | solution.py:71
  239.6 15.5 %collective-permute-start.36 = (bf16[80,1024]{1,0:T(8,128)(2,1)S(1)}, bf16[80,1024]{1,0:T(8,128)(2,1)S(1)}, u32[]{:S(2)}, u32[]{:S(2)}) collective-permute-start(bf16[80,1024]{1,0:T(8,128)(2,1)S(1)} %get-tuple-element.207), channel_id=1, source_target_pairs={{0,6},{1,7},{2,4},{3,5},{4,2},{5,3},{6,0},{7,1},{8,14},{9,15},{10,... | collective-permute-start | bytes 491528 | tf_op jit(solution)/shard_map/ppermute | solution.py:71
  255.3 7.2 %collective-permute-start.37 = (bf16[80,1024]{1,0:T(8,128)(2,1)S(1)}, bf16[80,1024]{1,0:T(8,128)(2,1)S(1)}, u32[]{:S(2)}, u32[]{:S(2)}) collective-permute-start(bf16[80,1024]{1,0:T(8,128)(2,1)S(1)} %get-tuple-element.181), channel_id=1, source_target_pairs={{0,2},{1,3},{2,0},{3,1},{4,6},{5,7},{6,4},{7,5},{8,10},{9,11},{10,... | collective-permute-start | bytes 491528 | tf_op jit(solution)/shard_map/ppermute | solution.py:71
  255.4 12.6 %collective-permute-start.38 = (bf16[80,1024]{1,0:T(8,128)(2,1)S(1)}, bf16[80,1024]{1,0:T(8,128)(2,1)S(1)}, u32[]{:S(2)}, u32[]{:S(2)}) collective-permute-start(bf16[80,1024]{1,0:T(8,128)(2,1)S(1)} %get-tuple-element.181), channel_id=1, source_target_pairs={{0,4},{1,5},{2,6},{3,7},{4,0},{5,1},{6,2},{7,3},{8,12},{9,13},{10,... | collective-permute-start | bytes 491528 | tf_op jit(solution)/shard_map/ppermute | solution.py:71
  257.3 14.6 %collective-permute-start.39 = (bf16[80,1024]{1,0:T(8,128)(2,1)S(1)}, bf16[80,1024]{1,0:T(8,128)(2,1)S(1)}, u32[]{:S(2)}, u32[]{:S(2)}) collective-permute-start(bf16[80,1024]{1,0:T(8,128)(2,1)S(1)} %get-tuple-element.181), channel_id=1, source_target_pairs={{0,6},{1,7},{2,4},{3,5},{4,2},{5,3},{6,0},{7,1},{8,14},{9,15},{10,... | collective-permute-start | bytes 491528 | tf_op jit(solution)/shard_map/ppermute | solution.py:71
  277.1 7.6 %collective-permute-start.41 = (bf16[80,1376]{1,0:T(8,128)(2,1)S(1)}, bf16[80,1376]{1,0:T(8,128)(2,1)S(1)}, u32[]{:S(2)}, u32[]{:S(2)}) collective-permute-start(bf16[80,1376]{1,0:T(8,128)(2,1)S(1)} %get-tuple-element.222), channel_id=1, source_target_pairs={{0,16},{8,24},{16,0},{24,8},{1,17},{9,25},{17,1},{25,9},{2,18},{10... | collective-permute-start | bytes 660488 | tf_op jit(solution)/shard_map/ppermute | solution.py:65
  277.7 7.3 %collective-permute-start.42 = (bf16[80,1376]{1,0:T(8,128)(2,1)S(1)}, bf16[80,1376]{1,0:T(8,128)(2,1)S(1)}, u32[]{:S(2)}, u32[]{:S(2)}) collective-permute-start(bf16[80,1376]{1,0:T(8,128)(2,1)S(1)} %get-tuple-element.221), channel_id=1, source_target_pairs={{0,8},{8,0},{16,24},{24,16},{1,9},{9,1},{17,25},{25,17},{2,10},{10... | collective-permute-start | bytes 660488 | tf_op jit(solution)/shard_map/ppermute | solution.py:65
  285.2 11.4 %collective-permute-start.43 = (bf16[2,80,1376]{2,1,0:T(8,128)(2,1)S(1)}, bf16[2,80,1376]{2,1,0:T(8,128)(2,1)S(1)}, u32[]{:S(2)}, u32[]{:S(2)}) collective-permute-start(bf16[2,80,1376]{2,1,0:T(8,128)(2,1)S(1)} %pad_maximum_fusion.4), channel_id=1, source_target_pairs={{0,8},{8,0},{16,24},{24,16},{1,9},{9,1},{17,25},{25,17},{2,10},{10... | collective-permute-start | bytes 1320968 | tf_op jit(solution)/shard_map/ppermute | solution.py:65
  286.7 11.0 %collective-permute-start.44 = (bf16[2,80,1376]{2,1,0:T(8,128)(2,1)S(1)}, bf16[2,80,1376]{2,1,0:T(8,128)(2,1)S(1)}, u32[]{:S(2)}, u32[]{:S(2)}) collective-permute-start(bf16[2,80,1376]{2,1,0:T(8,128)(2,1)S(1)} %pad_maximum_fusion.5), channel_id=1, source_target_pairs={{0,16},{8,24},{16,0},{24,8},{1,17},{9,25},{17,1},{25,9},{2,18},{10... | collective-permute-start | bytes 1320968 | tf_op jit(solution)/shard_map/ppermute | solution.py:65
  297.9 10.5 %collective-permute-start.45 = (bf16[2,80,1376]{2,1,0:T(8,128)(2,1)S(1)}, bf16[2,80,1376]{2,1,0:T(8,128)(2,1)S(1)}, u32[]{:S(2)}, u32[]{:S(2)}) collective-permute-start(bf16[2,80,1376]{2,1,0:T(8,128)(2,1)S(1)} %fusion), channel_id=1, source_target_pairs={{0,8},{8,0},{16,24},{24,16},{1,9},{9,1},{17,25},{25,17},{2,10},{10... | collective-permute-start | bytes 1320968 | tf_op jit(solution)/shard_map/ppermute | solution.py:65
  298.6 9.8 %collective-permute-start.46 = (bf16[2,80,1376]{2,1,0:T(8,128)(2,1)S(1)}, bf16[2,80,1376]{2,1,0:T(8,128)(2,1)S(1)}, u32[]{:S(2)}, u32[]{:S(2)}) collective-permute-start(bf16[2,80,1376]{2,1,0:T(8,128)(2,1)S(1)} %fusion), channel_id=1, source_target_pairs={{0,16},{8,24},{16,0},{24,8},{1,17},{9,25},{17,1},{25,9},{2,18},{10... | collective-permute-start | bytes 1320968 | tf_op jit(solution)/shard_map/ppermute | solution.py:65
  308.4 6.0 %collective-permute-start.47 = (bf16[80,1376]{1,0:T(8,128)(2,1)S(1)}, bf16[80,1376]{1,0:T(8,128)(2,1)S(1)}, u32[]{:S(2)}, u32[]{:S(2)}) collective-permute-start(bf16[80,1376]{1,0:T(8,128)(2,1)S(1)} %get-tuple-element.216.refs_4_), channel_id=1, source_target_pairs={{0,8},{8,0},{16,24},{24,16},{1,9},{9,1},{17,25},{25,17},{2,10},{10... | collective-permute-start | bytes 660488 | tf_op jit(solution)/shard_map/ppermute | solution.py:65
  310.2 6.0 %collective-permute-start.48 = (bf16[80,1376]{1,0:T(8,128)(2,1)S(1)}, bf16[80,1376]{1,0:T(8,128)(2,1)S(1)}, u32[]{:S(2)}, u32[]{:S(2)}) collective-permute-start(bf16[80,1376]{1,0:T(8,128)(2,1)S(1)} %get-tuple-element.217.refs_3_), channel_id=1, source_target_pairs={{0,16},{8,24},{16,0},{24,8},{1,17},{9,25},{17,1},{25,9},{2,18},{10... | collective-permute-start | bytes 660488 | tf_op jit(solution)/shard_map/ppermute | solution.py:65
  327.1 10.9 %collective-permute-start.50 = (bf16[80,1024]{1,0:T(8,128)(2,1)S(1)}, bf16[80,1024]{1,0:T(8,128)(2,1)S(1)}, u32[]{:S(2)}, u32[]{:S(2)}) collective-permute-start(bf16[80,1024]{1,0:T(8,128)(2,1)S(1)} %get-tuple-element.206), channel_id=1, source_target_pairs={{0,2},{1,3},{2,0},{3,1},{4,6},{5,7},{6,4},{7,5},{8,10},{9,11},{10,... | collective-permute-start | bytes 491528 | tf_op jit(solution)/shard_map/ppermute | solution.py:71
  327.2 13.2 %collective-permute-start.51 = (bf16[80,1024]{1,0:T(8,128)(2,1)S(1)}, bf16[80,1024]{1,0:T(8,128)(2,1)S(1)}, u32[]{:S(2)}, u32[]{:S(2)}) collective-permute-start(bf16[80,1024]{1,0:T(8,128)(2,1)S(1)} %get-tuple-element.205), channel_id=1, source_target_pairs={{0,4},{1,5},{2,6},{3,7},{4,0},{5,1},{6,2},{7,3},{8,12},{9,13},{10,... | collective-permute-start | bytes 491528 | tf_op jit(solution)/shard_map/ppermute | solution.py:71
  328.7 16.4 %collective-permute-start.52 = (bf16[80,1024]{1,0:T(8,128)(2,1)S(1)}, bf16[80,1024]{1,0:T(8,128)(2,1)S(1)}, u32[]{:S(2)}, u32[]{:S(2)}) collective-permute-start(bf16[80,1024]{1,0:T(8,128)(2,1)S(1)} %get-tuple-element.204), channel_id=1, source_target_pairs={{0,6},{1,7},{2,4},{3,5},{4,2},{5,3},{6,0},{7,1},{8,14},{9,15},{10,... | collective-permute-start | bytes 491528 | tf_op jit(solution)/shard_map/ppermute | solution.py:71
  (29 other events, 227.3 us)
Sparse Core Ops, SparseCore 0:
  10.2 55.8 all-gather.2

commit v3 on v2

v3 whole, which is shorter than its diff:
```python
import functools

import jax
import jax.numpy as jnp
from jax import lax
from jax.experimental import pallas as pl
from jax.experimental.pallas import tpu as pltpu
from jax.sharding import PartitionSpec as P

BF = jnp.bfloat16
F32 = jnp.float32
MIB = 1 << 20


def silu_grad(pre_act):
    sig = jax.nn.sigmoid(pre_act)
    return sig * (1.0 + pre_act * (1.0 - sig))


def dot(left, right, dims):
    return lax.dot_general(left, right, (dims, ((), ())), preferred_element_type=F32)


def dot_nt(left, right):
    return dot(left, right, ((1,), (1,)))


def dot_nn(left, right):
    return dot(left, right, ((1,), (0,)))


def row(stack, index):
    return lax.dynamic_index_in_dim(stack, index, 0, keepdims=False)


def whole(shape):
    return pl.BlockSpec(shape, lambda *_: (0,) * len(shape), pipeline_mode=pl.Buffered(1))


def tie(*values):
    return lax.optimization_barrier(values)


def call(kernel, name, grid, index, in_specs, out_specs, out_shape, operands, flops, vmem, scratch=()):
    moved = sum(o.size * o.dtype.itemsize for o in operands)
    return pl.pallas_call(
        kernel,
        grid_spec=pltpu.PrefetchScalarGridSpec(
            num_scalar_prefetch=1, grid=grid, in_specs=in_specs, out_specs=out_specs, scratch_shapes=scratch
        ),
        out_shape=out_shape,
        name=name,
        cost_estimate=pl.CostEstimate(flops=flops, bytes_accessed=moved, transcendentals=0),
        compiler_params=pltpu.CompilerParams(vmem_limit_bytes=vmem * MIB),
    )(index, *operands)


class Plan:
    def __init__(self, mesh):
        self.groups = mesh.shape["group"]
        self.members = mesh.shape["mp"]
        self.places = self.members // 2

    def group_swap(self, value, mask):
        return lax.ppermute(value, "group", [(i, i ^ mask) for i in range(self.groups)])

    def core_swap(self, value):
        return lax.ppermute(value, "mp", [(i, i ^ 1) for i in range(self.members)])

    def place_swap(self, value, mask):
        return lax.ppermute(value, "mp", [(i, i ^ (2 * mask)) for i in range(self.members)])

    def hop_one(self, pair):
        reach = (1, 2) if self.groups == 4 else range(1, self.groups)
        return {0: pair} | {k: self.group_swap(pair, k) for k in reach}

    def hop_two(self, have):
        if self.groups != 4:
            return {}
        return {3: (self.group_swap(have[2][0], 1), self.group_swap(have[1][1], 2))}

    def gather(self, pair, first=None, second=None):
        have = self.hop_one(pair)
        done = first() if first else ()
        have, done = lax.optimization_barrier((have, tuple(done)))
        rest = self.hop_two(have)
        done = second(have, done) if second else done
        rest, done = lax.optimization_barrier((rest, tuple(done)))
        return have | rest, done

    def scatter(self, make, hold):
        if self.groups == 4:
            send, hold = lax.optimization_barrier((make(3, 1, None, hold)[3].astype(BF), hold))
            hops = (self.group_swap(send[0], 1), self.group_swap(send[1], 2))
            parts, hops = make(1, 2, hops, hold)
            to_x = jnp.stack([parts[1][0].astype(F32), parts[1][1].astype(F32) + hops[1].astype(F32)]).astype(BF)
            to_y = jnp.stack([parts[2][0].astype(F32) + hops[0].astype(F32), parts[2][1].astype(F32)]).astype(BF)
            to_x, to_y, hold = lax.optimization_barrier((to_x, to_y, hold))
            came_x = self.group_swap(to_x, 1)
            came_y = self.group_swap(to_y, 2)
            parts, (came_x, came_y) = make(0, 1, (came_x, came_y), hold)
            return parts[0].astype(F32) + (came_x.astype(F32) + came_y.astype(F32))
        parts = make(0, self.groups, None, hold)
        total = parts[0].astype(F32)
        for k in range(1, self.groups):
            total = total + self.group_swap(parts[k].astype(BF), k).astype(F32)
        return total

    def halving(self, keep, came, first):
        current = keep.astype(F32) + came.astype(F32)
        keys = [k for k in range(self.groups) if not k & first]
        current = {k: current[i] for i, k in enumerate(keys)}
        mask = 1
        while mask < self.groups:
            if mask != first:
                keys = [k for k in current if not k & mask]
                came = self.group_swap(jnp.stack([current[k | mask] for k in keys]).astype(BF), mask)
                current = {k: current[k] + came[i].astype(F32) for i, k in enumerate(keys)}
            mask *= 2
        return current[0]

    def place_sum(self, parts, beside=()):
        came = [self.place_swap(parts[k].astype(BF), k) for k in range(1, self.places)]
        came, beside = lax.optimization_barrier((came, beside))
        total = parts[0].astype(F32)
        for piece in came:
            total = total + piece.astype(F32)
        return total, beside

    def place_gather(self, piece, beside=()):
        came = [self.place_swap(piece, k) for k in range(1, self.places)]
        came, beside = lax.optimization_barrier((came, beside))
        return jnp.concatenate([piece, *came], 0), beside


def chunks_kernel(index, *refs):
    value = jnp.concatenate([ref[...] for ref in refs[:-2]], 0)
    refs[-1][...] = dot_nt(value, refs[-2][...]).astype(BF)


def chunks_product(index, value, weight_t, order, groups, name, rows_at=None):
    n = len(order)
    rows, depth = value.shape if rows_at is None else value[0].shape
    units = weight_t.shape[0]
    share = rows // groups
    specs = [pl.BlockSpec((share, depth), lambda i, index, k=k: (index[k], 0)) for k in order]
    if rows_at is not None:
        value, rows_each = value
        per = share // rows_each
        specs = [
            pl.BlockSpec((rows_each, depth), lambda i, index, k=k, b=b: (index[rows_at + per * index[k] + b], 0))
            for k in order
            for b in range(per)
        ]
    shape = (n * share, units)
    out = call(
        chunks_kernel,
        name,
        (1,),
        index,
        specs + [whole(weight_t.shape)],
        whole(shape),
        jax.ShapeDtypeStruct(shape, BF),
        [value] * len(specs) + [weight_t],
        2 * n * share * depth * units,
        32,
    )
    return out.reshape(n, share, units)


def ghid_kernel(n, begun, index, *refs):
    cots, weight, start, out = refs[:n], refs[n], refs[n + 1 : n + 1 + begun], refs[n + 1 + begun]
    for j in range(n):

        @pl.when(pl.program_id(0) == j)
        def _(j=j):
            product = dot_nt(cots[j][...], weight[...])
            if j == 0 and begun:
                out[...] = start[0][...] + product
            elif j == 0:
                out[...] = product
            else:
                out[...] += product


def ghid_product(index, members_at, cots, weight, start=()):
    keys = sorted(cots)
    n = len(keys)
    rows, depth = cots[keys[0]].shape
    units = weight.shape[0]

    def column(i, index):
        at = index[members_at + keys[0]]
        for j in range(1, n):
            at = jnp.where(i == j, index[members_at + keys[j]], at)
        return 0, at

    return call(
        functools.partial(ghid_kernel, n, len(start)),
        "head_hidden_grad",
        (n,),
        index,
        [whole((rows, depth))] * n + [pl.BlockSpec((units, depth), column)] + [whole((rows, units))] * len(start),
        whole((rows, units)),
        jax.ShapeDtypeStruct((rows, units), F32),
        [cots[k] for k in keys] + [weight, *start],
        2 * rows * units * depth * n,
        48,
    )


def down_kernel(n, index, value, weight, *refs):
    product = dot_nn(value[0], weight[...])
    if n:
        product = product + refs[0][...].astype(F32)
    refs[n][...] = product.astype(BF)


def down_product(index, side, value, weight, came=()):
    rows, units = value.shape
    half, width = rows // 2, weight.shape[1]
    return call(
        functools.partial(down_kernel, len(came)),
        "trunk_down",
        (1,),
        index,
        [
            pl.BlockSpec((1, half, units), lambda i, index: (side, 0, 0)),
            whole((units, width)),
            *[whole((half, width))] * len(came),
        ],
        whole((half, width)),
        jax.ShapeDtypeStruct((half, width), BF),
        [value.reshape(2, half, units), weight, *came],
        2 * half * units * width,
        24,
    )


def rows_kernel(index, value, out):
    out[...] = value[...]


def rows_in_order(index, rows_at, value, rows_each):
    rows, width = value.shape
    return call(
        rows_kernel,
        "rows_in_order",
        (rows // rows_each,),
        index,
        [pl.BlockSpec((rows_each, width), lambda i, index: (index[rows_at + i], 0))],
        pl.BlockSpec((rows_each, width), lambda i, index: (i, 0)),
        jax.ShapeDtypeStruct(value.shape, value.dtype),
        [value],
        rows * width,
        16,
    )


def cot_kernel(index, *refs):
    for j, ref in enumerate(refs[:-1]):

        @pl.when(pl.program_id(0) == j)
        def _(ref=ref):
            refs[-1][...] = ref[0]


def cot_columns(index, members_at, place_at, cots, rows):
    n = len(cots)
    width = cots[0].shape[1]
    mine = pl.BlockSpec((1, rows, width), lambda i, index: (index[place_at], 0, 0))
    return call(
        cot_kernel,
        "head_output_grad_rows",
        (n,),
        index,
        [mine] * n,
        pl.BlockSpec((rows, width), lambda i, index: (0, index[members_at + i])),
        jax.ShapeDtypeStruct((rows, n * width), BF),
        [cots[k].reshape(-1, rows, width) for k in range(n)],
        rows * n * width,
        32,
    )


def pre_kernel(n, begun, index, *refs):
    pieces, (gate_w, up_w), refs = refs[:n], refs[n : n + 2], refs[n + 2 :]
    start, (pre, lin) = refs[:begun], refs[begun:]
    value = jnp.concatenate([piece[...] for piece in pieces], 0)
    for i, (weight, out) in enumerate(((gate_w, pre), (up_w, lin))):
        product = dot_nt(value, weight[...])
        out[...] = start[i][...] + product if begun else product


def pre_product(index, offset, parts, gate_t, up_t, start=()):
    rows, depth = sum(part.shape[0] for part in parts), parts[0].shape[1]
    units = gate_t.shape[0]
    weight = pl.BlockSpec((units, depth), lambda i, index: (0, index[offset]), pipeline_mode=pl.Buffered(1))
    both = [whole((rows, units))] * 2
    return call(
        functools.partial(pre_kernel, len(parts), len(start)),
        "head_pre",
        (1,),
        index,
        [whole(part.shape) for part in parts] + [weight] * 2 + both[: len(start)],
        both,
        [jax.ShapeDtypeStruct((rows, units), F32)] * 2,
        [*parts, gate_t, up_t, *start],
        4 * rows * depth * units,
        48,
    )


def back_rows(product, cot, own, mate):
    half = product.shape[0] // 2
    mate[0] = product[half:].astype(BF)
    mine = cot.shape[0]
    first = product[:mine] + cot[...].astype(F32)
    own[0] = jnp.concatenate([first, product[mine:half]], 0).astype(BF)


def act_kernel(counts, places, blocks_at, index, *refs):
    n = sum(counts)
    parts, (gate_w, up_w, pre, lin, ghid, cot, dgate, dup, own, mate) = refs[:n], refs[n : n + 10]
    pre_held, lin_held, ghid_held, sems = refs[n + 10 :]
    half = own.shape[1]
    held = (pre_held, lin_held)
    copies = [pltpu.make_async_copy(pre, pre_held, sems.at[0]), pltpu.make_async_copy(lin, lin_held, sems.at[1])]
    rows_each = half // places
    for block in range(2 * places):
        into = ghid_held.at[pl.ds(block * rows_each, rows_each)]
        copies.append(pltpu.make_async_copy(ghid.at[index[blocks_at + block]], into, sems.at[2 + block]))
    for j, count in enumerate(counts):

        @pl.when(pl.program_id(0) == j)
        def _(j=j, count=count):
            if j == 0:
                for copy in copies:
                    copy.start()
            last = j == len(counts) - 1
            begin = sum(counts[:j])
            value = jnp.concatenate([part[...] for part in parts[begin : begin + count]], 0)
            products = [dot_nt(value, gate_w[...]), dot_nt(value, up_w[...])]
            if j == 0:
                for copy in copies:
                    copy.wait()
            if not last:
                for sums, product in zip(held, products):
                    sums[...] += product
            else:
                for side in range(2):
                    rows = slice(side * half, side * half + half)
                    gate = pre_held[rows] + products[0][rows]
                    up = lin_held[rows] + products[1][rows]
                    h, sig = ghid_held[rows], jax.nn.sigmoid(gate)
                    dgate[rows] = (h * up * (sig * (1.0 + gate * (1.0 - sig)))).astype(BF)
                    dup[rows] = (h * (gate * sig)).astype(BF)
                product = dot_nn(dgate[...], gate_w[...]) + dot_nn(dup[...], up_w[...])
                back_rows(product, cot, own, mate)


def act_product(index, offset, pieces, gate_t, up_t, pre, lin, ghid, cot, places, blocks_at):
    flat = [part for piece in pieces for part in piece]
    depth = flat[0].shape[1]
    rows, units = pre.shape
    half = rows // 2
    last = offset + len(pieces) - 1
    weight = pl.BlockSpec((units, depth), lambda i, index: (0, index[offset + i]))
    hbm = pl.BlockSpec(memory_space=pl.ANY)
    return call(
        functools.partial(act_kernel, [len(piece) for piece in pieces], places, blocks_at),
        "head_act",
        (len(pieces),),
        index,
        [whole(part.shape) for part in flat]
        + [weight] * 2
        + [hbm] * 3
        + [pl.BlockSpec((cot.shape[0], depth), lambda i, index: (0, index[last]))],
        [whole((rows, units))] * 2 + [whole((1, half, depth))] * 2,
        [jax.ShapeDtypeStruct((rows, units), BF)] * 2 + [jax.ShapeDtypeStruct((1, half, depth), BF)] * 2,
        [*flat, gate_t, up_t, pre, lin, ghid.reshape(2 * places, half // places, units), cot],
        4 * rows * depth * units * (len(pieces) + 1),
        60,
        [pltpu.VMEM((rows, units), F32)] * 3 + [pltpu.SemaphoreType.DMA((2 + 2 * places,))],
    )


def back_kernel(index, dgate, dup, gate_w, up_w, cot, own, mate):
    product = dot_nn(dgate[...], gate_w[...]) + dot_nn(dup[...], up_w[...])
    back_rows(product, cot, own, mate)


def back_product(index, offset, count, dgate, dup, gate_t, up_t, cot, groups):
    rows, units = dgate.shape
    depth = gate_t.shape[1] // groups
    half = rows // 2
    weight = pl.BlockSpec((units, depth), lambda i, index: (0, index[offset + i]))
    cot_spec = pl.BlockSpec((cot.shape[0], depth), lambda i, index: (0, index[offset + i]))
    out = pl.BlockSpec((1, half, depth), lambda i, index: (i, 0, 0))
    return call(
        back_kernel,
        "head_back",
        (count,),
        index,
        [whole((rows, units))] * 2 + [weight] * 2 + [cot_spec],
        [out] * 2,
        [jax.ShapeDtypeStruct((count, half, depth), BF)] * 2,
        [dgate, dup, gate_t, up_t, cot],
        4 * rows * units * depth * count,
        48,
    )


def trunk_act_kernel(groups, index, *refs):
    ghids, gates, ups = refs[: 2 * groups], refs[2 * groups : 3 * groups], refs[3 * groups : 4 * groups]
    gate_w, up_w, dgate, dup, own, mate = refs[4 * groups :]
    for k in range(groups):
        share = gates[k].shape[0]
        ghid = jnp.concatenate([ghids[2 * k][...], ghids[2 * k + 1][...]], 0).astype(F32)
        gate, up = gates[k][...].astype(F32), ups[k][...].astype(F32)
        sig = jax.nn.sigmoid(gate)
        rows = pl.ds(pl.multiple_of(index[k] * share, share), share)
        dgate[rows] = (ghid * up * (sig * (1.0 + gate * (1.0 - sig)))).astype(BF)
        dup[rows] = (ghid * (gate * sig)).astype(BF)
    half = own.shape[0]
    for side, out in enumerate((own, mate)):
        rows = slice(side * half, side * half + half)
        product = dot_nn(dgate[rows], gate_w[...]) + dot_nn(dup[rows], up_w[...])
        out[...] = product.astype(BF)


def trunk_act(index, ghids, gates, ups, gate_t, up_t):
    groups = len(gates)
    share, units = gates[0].shape
    rows, width = share * groups, gate_t.shape[1]
    flat = [half for pair in ghids for half in pair]
    shapes = [(rows, units)] * 2 + [(rows // 2, width)] * 2
    return call(
        functools.partial(trunk_act_kernel, groups),
        "trunk_act",
        (1,),
        index,
        [whole(v.shape) for v in [*flat, *gates, *ups, gate_t, up_t]],
        [whole(shape) for shape in shapes],
        [jax.ShapeDtypeStruct(shape, BF) for shape in shapes],
        [*flat, *gates, *ups, gate_t, up_t],
        4 * rows * units * width,
        36,
    )


def grads_kernel(index, dgate, dup, toks, gate, up):
    gate[...] = dot(dgate[...], toks[...], ((0,), (0,)))
    up[...] = dot(dup[...], toks[...], ((0,), (0,)))


def grads_product(index, dgate, dup, toks):
    rows, units = dgate.shape
    width = toks.shape[1]
    tile = width // 2
    out = pl.BlockSpec((units, tile), lambda i, index: (0, i))
    return call(
        grads_kernel,
        "trunk_weight_grads",
        (2,),
        index,
        [whole((rows, units))] * 2 + [pl.BlockSpec((rows, tile), lambda i, index: (0, i))],
        [out] * 2,
        [jax.ShapeDtypeStruct((units, width), F32)] * 2,
        [dgate, dup, toks],
        4 * rows * units * width,
        48,
    )


def make_body(plan):
    groups, places = plan.groups, plan.places

    def body(tokens, trunk_gate, trunk_up, trunk_down, head_gate, head_up, head_down, head_grads):
        g = lax.axis_index("group")
        m = lax.axis_index("mp")
        z, c = m // 2, m % 2
        total_rows, width = tokens.shape
        rows = total_rows // plan.members
        units = trunk_gate.shape[1]
        half_rows = places * rows
        share = total_rows // groups
        offsets = [g ^ k for k in range(groups)]
        both = [(k, side) for side in range(2) for k in range(places)]
        blocks = [(c ^ side) * places + (z ^ k) for k, side in both]
        members = [2 * (z ^ k) + (c ^ side) for k in range(places) for side in range(2)]
        blocks_at, members_at = groups, groups + plan.members
        rows_at = members_at + plan.members
        index = jnp.stack(offsets + blocks + members + [2 * (z ^ k) + (c ^ side) for k, side in both]).astype(jnp.int32)

        own_tok = row(tokens.reshape(plan.members, rows, width), m)
        cot_width = head_grads.shape[2]
        cot_own = head_grads[0].reshape(places, 2, rows, cot_width).transpose(1, 0, 2, 3)
        cot_own = cot_own.reshape(total_rows, cot_width)

        def in_order(pieces):
            out = jnp.zeros((groups, 2, share // 2, units), BF)
            for k, pair in pieces.items():
                if isinstance(pair, tuple):
                    for side in range(2):
                        out = lax.dynamic_update_slice(out, pair[side][None, None], (g ^ k, side, 0, 0))
                else:
                    out = lax.dynamic_update_slice(out, pair[None], (g ^ k, 0, 0, 0))
            return out.reshape(total_rows, units)

        def sums(weight, first, name):
            keep = [k for k in range(groups) if not k & first]
            send = [k for k in range(groups) if k & first]
            sent = chunks_product(index, (tokens, rows), weight.T, send, groups, name, rows_at)
            return sent, lambda: chunks_product(index, (tokens, rows), weight.T, keep, groups, name, rows_at)

        gate_send, gate_keep = sums(trunk_gate, 1, "trunk_gate")
        up_send, up_keep = sums(trunk_up, 2, "trunk_up")
        gate_came, up_came = plan.group_swap(gate_send, 1), plan.group_swap(up_send, 2)
        gate_kept, up_kept = gate_keep(), up_keep()
        near = [k for k in range(1, places) if not k & (k - 1)][::-1]
        far = [k for k in range(1, places) if k & (k - 1)]
        crossed = {k: plan.place_swap(cot_own, k) for k in near}
        cots = {0: cot_own, 1: plan.core_swap(cot_own)}
        ghid = ghid_product(index, members_at, cots, head_down[0])
        toks = rows_in_order(index, rows_at, tokens, rows)
        gate_came, up_came, ghid, toks = tie(gate_came, up_came, ghid, toks)
        gate_r = plan.halving(gate_kept, gate_came, 1)
        up_r = plan.halving(up_kept, up_came, 2)
        gate_r, up_r, crossed = lax.optimization_barrier((gate_r, up_r, crossed))

        def both_members(which):
            pairs = [((2 * k, crossed[k]), (2 * k + 1, plan.core_swap(crossed[k]))) for k in which]
            return dict(sum(pairs, ()))

        came_first, came_next = both_members(near[:1]), both_members(near[1:])
        for k in far:
            crossed[k] = plan.place_swap(crossed[k & (k - 1)], k & -k)
        hid_r = (jax.nn.silu(gate_r) * up_r).astype(BF)
        wide, (ghid, came_next, got) = plan.gather(
            hid_r.reshape(2, share // 2, units),
            second=lambda have, done: (
                ghid_product(index, members_at, came_first, head_down[0], (ghid,)),
                came_next,
                [crossed[k] for k in far],
            ),
        )
        crossed |= dict(zip(far, got))
        hidden = in_order(wide)
        pair = jnp.stack([gate_r, up_r]).astype(BF)
        hidden, pair = tie(hidden, pair)
        have = plan.hop_one(pair)
        came = plan.core_swap(down_product(index, 1, hidden, trunk_down))
        part = down_product(index, 0, hidden, trunk_down, (came,))
        came_last = came_next | both_members(far)
        part, came_last = lax.optimization_barrier((part, came_last))
        ghid = ghid_product(index, members_at, came_last, head_down[0], (ghid,))
        beside = (ghid, have)
        summed, (ghid, have) = plan.place_sum(part.reshape(places, rows, width), beside)
        cots |= came_first | came_last
        shard = (own_tok.astype(F32) + summed).astype(BF)
        shard, have, cots = lax.optimization_barrier((shard, have, cots))
        gate_t, up_t = head_gate[0].T, head_up[0].T
        cot_rows = cot_columns(index, members_at, blocks_at, cots, rows)
        came = {k: plan.place_swap(shard, k) for k in range(1, places)}
        inner = places // 2
        near, have = lax.optimization_barrier(({k: came[k] for k in range(1, inner)}, have))
        top = jnp.concatenate([shard] + [near[k] for k in range(1, inner)], 0)
        wide = [plan.hop_one(top), None]
        rest = plan.hop_two(have)
        far, wide[0], cot_rows = lax.optimization_barrier(
            ({k: came[k] for k in range(inner, places)}, wide[0], cot_rows)
        )
        low = jnp.concatenate([far[k] for k in range(inner, places)], 0)
        wide[1] = plan.hop_one(low)
        relayed = [plan.group_swap(wide[0][2], 1)] if groups == 4 else []

        def both_cores(parts):
            return parts + [plan.core_swap(part) for part in parts]

        pre, lin = pre_product(index, 0, both_cores([top, low]), gate_t, up_t)
        wide, rest, pre, lin = lax.optimization_barrier((wide, rest, pre, lin))
        have = have | rest
        gates, ups = ([have[k][i] for k in range(groups)] for i in range(2))
        relayed += [plan.group_swap(wide[1][1], 2)] if groups == 4 else []
        pieces = [both_cores([half[k] for half in wide]) for k in range(2, groups) if k in wide[0]]
        pre, lin = pre_product(index, 1, both_cores([half[1] for half in wide]), gate_t, up_t, (pre, lin))
        relayed, pieces, pre, lin = lax.optimization_barrier((relayed, pieces, pre, lin))
        pieces += [both_cores(relayed)] if groups == 4 else []
        dgate, dup, *last_block = act_product(
            index, 2, pieces, gate_t, up_t, pre, lin, ghid, cot_rows, places, blocks_at
        )

        def make(offset, count, hops, hold):
            if groups == 4 and offset == groups - 1:
                own, mate = last_block
            else:
                own, mate = back_product(index, offset, count, *hold, gate_t, up_t, cot_rows, groups)
            if hops is not None:
                own, mate, hops = lax.optimization_barrier((own, mate, hops))
            total = own.astype(F32) + plan.core_swap(mate).astype(F32)
            parts = {offset + i: total[i].reshape(2, half_rows // 2, width) for i in range(count)}
            return parts if hops is None else (parts, hops)

        cols = plan.scatter(make, (dgate, dup))
        dshard = plan.place_sum(cols.astype(BF).reshape(places, rows, width))[0].astype(BF)
        dhalf = plan.place_gather(dshard)[0]
        grad_mid = jnp.concatenate([dhalf, plan.core_swap(dhalf)], 0)

        back = chunks_product(index, grad_mid, trunk_down, list(range(groups)), groups, "trunk_hidden_grad")
        back = back.reshape(groups, 2, share // 2, units)

        def chunks(offset, count, hops, hold):
            parts = {offset + i: back[offset + i] for i in range(count)}
            return parts if hops is None else (parts, hops)

        ghid_t = plan.scatter(chunks, ()).astype(BF)
        wide, (grad_down,) = plan.gather(ghid_t, lambda: (dot(hidden, grad_mid, ((0,), (0,))),))
        ghids = [wide[k] for k in range(groups)]
        dgate_t, dup_t, own, mate = trunk_act(index, ghids, gates, ups, trunk_gate.T, trunk_up.T)
        part = (own.astype(F32) + plan.core_swap(mate).astype(F32)).astype(BF)
        part, dgate_t, dup_t = tie(part, dgate_t, dup_t)
        grads = grads_product(index, dgate_t, dup_t, toks)
        summed, (grad_gate, grad_up) = plan.place_sum(part.reshape(places, rows, width), grads)
        grad_x = (dshard.astype(F32) + summed).astype(BF)
        grad_gate, grad_up = grad_gate.T, grad_up.T
        return (grad_x, grad_gate, grad_up, grad_down)

    return body


def solution(mesh):
    return jax.shard_map(
        make_body(Plan(mesh)),
        mesh=mesh,
        in_specs=(
            P(None, "group"),
            P("group", "mp"),
            P("group", "mp"),
            P("mp", "group"),
            P("group", None, "mp"),
            P("group", None, "mp"),
            P("group", "mp", None),
            P("group", None, "mp"),
        ),
        out_specs=(P("mp", "group"), P("group", "mp"), P("group", "mp"), P("mp", "group")),
        check_vma=False,
    )
```

time: 360 us -> 330 us (0.917)
  between operations: 15.2 us -> 1.88 us
  waiting for transfers between devices: 129 us -> 119 us
  local copies, waits for them, and re-layouts: 24 us -> 16.1 us
  Pallas kernels: 112 us -> 118 us
  matrix products: 10.9 us -> 4.91 us
    ppermute x28 -> x30, waiting for transfers between devices: 80.1 us -> 62.4 us  [group_swap(): lax.ppermute(value, 'group', [(i, i ^ mask) for i in range(self.groups)])]
    ppermute x15 -> x18, waiting for transfers between devices: 34.2 us -> 43.9 us  [place_swap(): lax.ppermute(value, 'mp', [(i, i ^ 2 * mask) for i in range(self.members)])]
    dot_general x3 -> x1, matrix products: 10.9 us -> 4.91 us  [dot(): lax.dot_general(left, right, (dims, ((), ())), preferred_element_type=F32)]
    pallas_call x14 -> x19, Pallas kernels: 112 us -> 118 us  [call(): pl.pallas_call(kernel, grid_spec=pltpu.PrefetchScalarGridSpec(num_scalar_...]
    squeeze x4 -> x2, local copies, waits for them, and re-layouts: 4.41 us -> 0.03 us  [hop_two(): return {3: (self.group_swap(have[2][0], 1), self.group_swap(have[1][1], 2))}]
    ppermute x15 -> x18, starting transfers between devices: 19.3 us -> 21.8 us  [place_swap(): lax.ppermute(value, 'mp', [(i, i ^ 2 * mask) for i in range(self.members)])]
    unnamed x46 -> x93, local copies, waits for them, and re-layouts: 8.63 us -> 10.6 us
    ppermute x10 -> x18, waiting for transfers between devices: 14.3 us -> 13 us  [core_swap(): return lax.ppermute(value, 'mp', [(i, i ^ 1) for i in range(self.members)])]
  transfers between devices with their start and end apart: 54 -> 66, of which waited for: 36 -> 36; matrix products, arithmetic and copies ran while one was open for 7% -> 4% of each run, Pallas kernels for 20% -> 25%
where the time goes in v3:
time: 330 us; the launch traced here: 325 us
  waiting for transfers between devices  119 us (36%)
  Pallas kernels  118 us (36%)
  starting transfers between devices  57.7 us (17%)
  local copies, waits for them, and re-layouts  16.1 us (5%)
  other arithmetic  7.28 us (2%)
  matrix products  4.91 us (1%)
    pallas_call x19, Pallas kernels, call(): pl.pallas_call(kernel, grid_spec=pltpu.PrefetchScalarGridSpec(num_scalar_...  118 us
    ppermute x30, waiting for transfers between devices, group_swap(): lax.ppermute(value, 'group', [(i, i ^ mask) for i in range(self.groups)])  62.4 us
    ppermute x18, waiting for transfers between devices, place_swap(): lax.ppermute(value, 'mp', [(i, i ^ 2 * mask) for i in range(self.members)])  43.9 us
    ppermute x30, starting transfers between devices, group_swap(): lax.ppermute(value, 'group', [(i, i ^ mask) for i in range(self.groups)])  33 us
    ppermute x18, starting transfers between devices, place_swap(): lax.ppermute(value, 'mp', [(i, i ^ 2 * mask) for i in range(self.members)])  21.8 us
    ppermute x18, waiting for transfers between devices, core_swap(): return lax.ppermute(value, 'mp', [(i, i ^ 1) for i in range(self.members)])  13 us
    unnamed x93, local copies, waits for them, and re-layouts  10.6 us
  transfers between devices with their start and end apart: 66, of which 36 were waited for; matrix products, arithmetic and copies ran while one was open for 4% of the time, Pallas kernels for 25%

profile of v3, /device:TPU:18, one launch (start us, length us, event | category | flops | bytes accessed | tf_op | source)
XLA Modules:
  0.0 325.2 jit_solution(15278538946035187298)
XLA Ops:
  16.8 4.4 %head_hidden_grad.3.refs_3_ = f32[640,1376]{1,0:T(8,128)S(1)} custom-call(s32[28]{0:T(128)S(1)} %stack.137.index, bf16[640,512]{1,0:T(8,128)(2,1)S(1)} %bitcast.172, bf16[640,512]{1,0:T(8,128)(2,1)S(1)} %collective-permute-done.2.refs_1_, bf16[1376,4096]{1,0:T(8,128)(2,1)} %bitcast.191), custom_call_target="tpu_custom_call" | custom-call | flops 1803550720 | bytes 12582912 | tf_op jit(solution)/shard_map/head_hidden_grad/pallas_call | solution.py:46
  21.2 6.3 %collective-permute-done = bf16[2,160,1376]{2,1,0:T(8,128)(2,1)S(1)} collective-permute-done((bf16[2,160,1376]{2,1,0:T(8,128)(2,1)S(1)}, bf16[2,160,1376]{2,1,0:T(8,128)(2,1)S(1)}, u32[]{:S(2)}, u32[]{:S(2)}) %collective-permute-start) | collective-permute-done | bytes 880672 | tf_op jit(solution)/shard_map/ppermute | solution.py:65
  27.5 2.1 collective-permute-done.1
  33.2 7.7 %collective-permute-done.4 = bf16[1,160,1376]{2,1,0:T(8,128)(2,1)S(1)} collective-permute-done((bf16[1,160,1376]{2,1,0:T(8,128)(2,1)S(1)}, bf16[1,160,1376]{2,1,0:T(8,128)(2,1)S(1)}, u32[]{:S(2)}, u32[]{:S(2)}) %collective-permute-start.4) | collective-permute-done | bytes 440352 | tf_op jit(solution)/shard_map/ppermute | solution.py:65
  47.7 5.5 %collective-permute-done.7 = bf16[2,80,1376]{2,1,0:T(8,128)(2,1)S(1)} collective-permute-done((bf16[2,80,1376]{2,1,0:T(8,128)(2,1)S(1)}, bf16[2,80,1376]{2,1,0:T(8,128)(2,1)S(1)}, u32[]{:S(2)}, u32[]{:S(2)}) %collective-permute-start.7) | collective-permute-done | bytes 440352 | tf_op jit(solution)/shard_map/ppermute | solution.py:65
  56.5 6.2 %head_hidden_grad.4.refs_5_ = f32[640,1376]{1,0:T(8,128)S(1)} custom-call(s32[28]{0:T(128)S(1)} %stack.137.index, bf16[640,512]{1,0:T(8,128)(2,1)} %collective-permute-done.6.refs_0_, bf16[640,512]{1,0:T(8,128)(2,1)S(1)} %collective-permute-done.11.refs_1_, bf16[1376,4096]{1,0:T(8,128)(2,1)} %bitcast.192, f32[640,1376]{1,0:T(8,128)} %copy-done.5), custom_call_target="tpu_custom_call" | custom-call | flops 1803550720 | bytes 16105472 | tf_op jit(solution)/shard_map/head_hidden_grad/pallas_call | solution.py:46
  62.9 2.6 trunk_down.2
  70.1 2.8 trunk_down.3
  73.0 2.5 collective-permute-start.16
  77.1 11.0 %head_hidden_grad.5 = f32[640,1376]{1,0:T(8,128)} custom-call(s32[28]{0:T(128)S(1)} %stack.137.index, bf16[640,512]{1,0:T(8,128)(2,1)} %collective-permute-done.5.refs_0_, bf16[640,512]{1,0:T(8,128)(2,1)S(1)} %copy-done.22, bf16[640,512]{1,0:T(8,128)(2,1)} %collective-permute-done.13.refs_2_, bf16[640,512]{1,0:T(8,128)(2,1)} %collective-permute-done.15.refs_3_, ...), custom_call_target="tpu_custom_call" | custom-call | flops 3607101440 | bytes 17416192 | tf_op jit(solution)/shard_map/head_hidden_grad/pallas_call | solution.py:46
  88.1 3.1 collective-permute-done.18
  92.7 1.9 collective-permute-start.21
  95.8 2.2 head_output_grad_rows.1.refs_13_.cot
  103.3 1.9 collective-permute-done.21
  106.7 2.3 collective-permute-done.22
  109.1 2.0 slice_bitcast_fusion.4
  114.5 9.3 %head_pre.2 = (f32[640,1376]{1,0:T(8,128)S(1)}, f32[640,1376]{1,0:T(8,128)}) custom-call(s32[28]{0:T(128)S(1)} %stack.137.index, bf16[160,1024]{1,0:T(8,128)(2,1)S(1)} %constant_dynamic-update-slice_fusion.refs_0_, bf16[160,1024]{1,0:T(8,128)(2,1)S(1)} %constant_dynamic-update-slice_fusion.2.refs_1_, bf16[160,1024]{1,0:T(8,128)(2,1)S(1)} %collective-permute-done.31.refs_2_, ...), custom_call_target="tpu_custom_call" | custom-call | flops 3607101440 | bytes 23855104 | tf_op jit(solution)/shard_map/head_pre/pallas_call | solution.py:46
  123.8 1.8 copy-done.16
  125.7 5.2 %collective-permute-done.28.refs_1_ = bf16[160,1024]{1,0:T(8,128)(2,1)S(1)} collective-permute-done((bf16[160,1024]{1,0:T(8,128)(2,1)S(1)}, bf16[160,1024]{1,0:T(8,128)(2,1)S(1)}, u32[]{:S(2)}, u32[]{:S(2)}) %collective-permute-start.28) | collective-permute-done | bytes 327712 | tf_op jit(solution)/shard_map/ppermute | solution.py:65
  135.0 11.4 %head_pre.3 = (f32[640,1376]{1,0:T(8,128)S(1)}, f32[640,1376]{1,0:T(8,128)}) custom-call(s32[28]{0:T(128)S(1)} %stack.137.index, bf16[160,1024]{1,0:T(8,128)(2,1)S(1)} %collective-permute-done.24.refs_0_, bf16[160,1024]{1,0:T(8,128)(2,1)S(1)} %collective-permute-done.27.refs_1_, bf16[160,1024]{1,0:T(8,128)(2,1)S(1)} %collective-permute-done.36.refs_2_, ...), custom_call_target="tpu_custom_call" | custom-call | flops 3607101440 | bytes 30900224 | tf_op jit(solution)/shard_map/head_pre/pallas_call | solution.py:46
  152.0 21.5 %head_act.1 = (bf16[640,1376]{1,0:T(8,128)(2,1)}, bf16[640,1376]{1,0:T(8,128)(2,1)}, bf16[1,320,1024]{2,1,0:T(8,128)(2,1)}, bf16[1,320,1024]{2,1,0:T(8,128)(2,1)}) custom-call(s32[28]{0:T(128)} %copy-done.28, bf16[160,1024]{1,0:T(8,128)(2,1)} %copy-done.36, bf16[160,1024]{1,0:T(8,128)(2,1)} %copy-done.37, bf16[160,1024]{1,0:T(8,128)(2,1)} %copy-done.40, ...), custom_call_target="tpu_custom_call" | custom-call | flops 10821304320 | bytes 36388864 | tf_op jit(solution)/shard_map/head_act/pallas_call | solution.py:46
  173.8 2.2 collective-permute-done.40
  178.5 12.5 %head_back.2 = (bf16[2,320,1024]{2,1,0:T(8,128)(2,1)S(1)}, bf16[2,320,1024]{2,1,0:T(8,128)(2,1)S(1)}) custom-call(s32[28]{0:T(128)S(1)} %copy-done.29, bf16[640,1376]{1,0:T(8,128)(2,1)S(1)} %copy-done.12, bf16[640,1376]{1,0:T(8,128)(2,1)} %get-tuple-element.210.dup, bf16[1376,4096]{1,0:T(8,128)(2,1)} %bitcast.184, bf16[1376,4096]{1,0:T(8,128)(2,1)} %bitcast.189, ...), custom_call_target="tpu_custom_call" | custom-call | flops 7214202880 | bytes 26722304 | tf_op jit(solution)/shard_map/head_back/pallas_call | solution.py:46
  191.2 3.0 collective-permute-done.43
  198.2 7.4 %head_back.3 = (bf16[1,320,1024]{2,1,0:T(8,128)(2,1)S(1)}, bf16[1,320,1024]{2,1,0:T(8,128)(2,1)S(1)}) custom-call(s32[28]{0:T(128)S(1)} %copy-done.29, bf16[640,1376]{1,0:T(8,128)(2,1)S(1)} %copy-done.12, bf16[640,1376]{1,0:T(8,128)(2,1)S(1)} %copy-done.13, bf16[1376,4096]{1,0:T(8,128)(2,1)} %bitcast.185, bf16[1376,4096]{1,0:T(8,128)(2,1)} %bitcast.190, ...), custom_call_target="tpu_custom_call" | custom-call | flops 3607101440 | bytes 26722304 | tf_op jit(solution)/shard_map/head_back/pallas_call | solution.py:46
  205.7 6.4 %collective-permute-done.44 = bf16[2,160,1024]{2,1,0:T(8,128)(2,1)S(1)} collective-permute-done((bf16[2,160,1024]{2,1,0:T(8,128)(2,1)S(1)}, bf16[2,160,1024]{2,1,0:T(8,128)(2,1)S(1)}, u32[]{:S(2)}, u32[]{:S(2)}) %collective-permute-start.44) | collective-permute-done | bytes 655392 | tf_op jit(solution)/shard_map/ppermute | solution.py:65
  213.2 2.1 collective-permute-done.46
  215.9 2.0 collective-permute-start.48
  219.4 3.6 %collective-permute-done.47 = bf16[80,1024]{1,0:T(8,128)(2,1)S(1)} collective-permute-done((bf16[80,1024]{1,0:T(8,128)(2,1)S(1)}, bf16[80,1024]{1,0:T(8,128)(2,1)S(1)}, u32[]{:S(2)}, u32[]{:S(2)}) %collective-permute-start.47) | collective-permute-done | bytes 163872 | tf_op jit(solution)/shard_map/ppermute | solution.py:71
  223.0 6.6 %collective-permute-done.48 = bf16[80,1024]{1,0:T(8,128)(2,1)S(1)} collective-permute-done((bf16[80,1024]{1,0:T(8,128)(2,1)S(1)}, bf16[80,1024]{1,0:T(8,128)(2,1)S(1)}, u32[]{:S(2)}, u32[]{:S(2)}) %collective-permute-start.48) | collective-permute-done | bytes 163872 | tf_op jit(solution)/shard_map/ppermute | solution.py:71
  229.6 4.3 %collective-permute-done.49 = bf16[80,1024]{1,0:T(8,128)(2,1)S(1)} collective-permute-done((bf16[80,1024]{1,0:T(8,128)(2,1)S(1)}, bf16[80,1024]{1,0:T(8,128)(2,1)S(1)}, u32[]{:S(2)}, u32[]{:S(2)}) %collective-permute-start.49) | collective-permute-done | bytes 163872 | tf_op jit(solution)/shard_map/ppermute | solution.py:71
  234.1 2.0 collective-permute-start.51
  237.6 3.6 %collective-permute-done.50 = bf16[80,1024]{1,0:T(8,128)(2,1)S(1)} collective-permute-done((bf16[80,1024]{1,0:T(8,128)(2,1)S(1)}, bf16[80,1024]{1,0:T(8,128)(2,1)S(1)}, u32[]{:S(2)}, u32[]{:S(2)}) %collective-permute-start.50) | collective-permute-done | bytes 163872 | tf_op jit(solution)/shard_map/ppermute | solution.py:71
  241.3 6.1 %collective-permute-done.51 = bf16[80,1024]{1,0:T(8,128)(2,1)S(1)} collective-permute-done((bf16[80,1024]{1,0:T(8,128)(2,1)S(1)}, bf16[80,1024]{1,0:T(8,128)(2,1)S(1)}, u32[]{:S(2)}, u32[]{:S(2)}) %collective-permute-start.51) | collective-permute-done | bytes 163872 | tf_op jit(solution)/shard_map/ppermute | solution.py:71
  247.3 3.6 %collective-permute-done.52 = bf16[80,1024]{1,0:T(8,128)(2,1)S(1)} collective-permute-done((bf16[80,1024]{1,0:T(8,128)(2,1)S(1)}, bf16[80,1024]{1,0:T(8,128)(2,1)S(1)}, u32[]{:S(2)}, u32[]{:S(2)}) %collective-permute-start.52) | collective-permute-done | bytes 163872 | tf_op jit(solution)/shard_map/ppermute | solution.py:71
  251.2 2.0 collective-permute-done.53
  253.2 2.8 trunk_hidden_grad.1
  258.2 5.6 %collective-permute-done.54 = bf16[80,1376]{1,0:T(8,128)(2,1)S(1)} collective-permute-done((bf16[80,1376]{1,0:T(8,128)(2,1)S(1)}, bf16[80,1376]{1,0:T(8,128)(2,1)S(1)}, u32[]{:S(2)}, u32[]{:S(2)}) %collective-permute-start.54) | collective-permute-done | bytes 220192 | tf_op jit(solution)/shard_map/ppermute | solution.py:65
  267.7 8.9 %collective-permute-done.56 = bf16[2,80,1376]{2,1,0:T(8,128)(2,1)S(1)} collective-permute-done((bf16[2,80,1376]{2,1,0:T(8,128)(2,1)S(1)}, bf16[2,80,1376]{2,1,0:T(8,128)(2,1)S(1)}, u32[]{:S(2)}, u32[]{:S(2)}) %collective-permute-start.56) | collective-permute-done | bytes 440352 | tf_op jit(solution)/shard_map/ppermute | solution.py:65
  279.2 4.9 %fusion.21 = f32[1376,1024]{1,0:T(8,128)} fusion(bf16[640,1376]{1,0:T(8,128)(2,1)S(1)} %bitcast.162, bf16[640,1024]{1,0:T(8,128)(2,1)S(1)} %constant_dynamic-update-slice_fusion.4.refs_0_.refs_1_.refs_2_.refs_3_), kind=kOutput, calls=%fused_computation.86 | convolution fusion | flops 1803550720 | bytes 8708096 | tf_op jit(solution)/shard_map/dot_general | solution.py:21
  284.1 3.0 collective-permute-done.58
  289.9 4.7 %collective-permute-done.60.refs_6_ = bf16[80,1376]{1,0:T(8,128)(2,1)S(1)} collective-permute-done((bf16[80,1376]{1,0:T(8,128)(2,1)S(1)}, bf16[80,1376]{1,0:T(8,128)(2,1)S(1)}, u32[]{:S(2)}, u32[]{:S(2)}) %collective-permute-start.60) | collective-permute-done | bytes 220192 | tf_op jit(solution)/shard_map/ppermute | solution.py:65
  295.1 8.5 %trunk_act.1 = (bf16[640,1376]{1,0:T(8,128)(2,1)S(1)}, bf16[640,1376]{1,0:T(8,128)(2,1)S(1)}, bf16[320,1024]{1,0:T(8,128)(2,1)S(1)}, bf16[320,1024]{1,0:T(8,128)(2,1)S(1)}) custom-call(s32[28]{0:T(128)S(1)} %copy-done.29, bf16[80,1376]{1,0:T(8,128)(2,1)S(1)} %get-tuple-element.291.refs_0_, bf16[80,1376]{1,0:T(8,128)(2,1)S(1)} %get-tuple-element.290.refs_1_, ...), custom_call_target="tpu_custom_call" | custom-call | flops 3607101440 | bytes 10919936 | tf_op jit(solution)/shard_map/trunk_act/pallas_call | solution.py:46
  303.7 2.1 collective-permute-done.62
  306.2 2.1 collective-permute-start.64
  309.7 7.3 %trunk_weight_grads.1 = (f32[1376,1024]{1,0:T(8,128)}, f32[1376,1024]{1,0:T(8,128)}) custom-call(s32[28]{0:T(128)S(1)} %copy-done.29, bf16[640,1376]{1,0:T(8,128)(2,1)S(1)} %get-tuple-element.241.dgate, bf16[640,1376]{1,0:T(8,128)(2,1)S(1)} %get-tuple-element.242.dup, bf16[640,1024]{1,0:T(8,128)(2,1)S(1)} %copy-done.24), custom_call_target="tpu_custom_call" | custom-call | flops 3607101440 | bytes 4833280 | tf_op jit(solution)/shard_map/trunk_weight_grads/pallas_call | solution.py:46
  316.9 3.0 collective-permute-done.64
  319.9 4.2 %collective-permute-done.65 = bf16[80,1024]{1,0:T(8,128)(2,1)S(1)} collective-permute-done((bf16[80,1024]{1,0:T(8,128)(2,1)S(1)}, bf16[80,1024]{1,0:T(8,128)(2,1)S(1)}, u32[]{:S(2)}, u32[]{:S(2)}) %collective-permute-start.65) | collective-permute-done | bytes 163872 | tf_op jit(solution)/shard_map/ppermute | solution.py:71
  (247 shorter events, 84.7 us)
Async XLA Ops:
  5.7 21.8 %collective-permute-start = (bf16[2,160,1376]{2,1,0:T(8,128)(2,1)S(1)}, bf16[2,160,1376]{2,1,0:T(8,128)(2,1)S(1)}, u32[]{:S(2)}, u32[]{:S(2)}) collective-permute-start(bf16[2,160,1376]{2,1,0:T(8,128)(2,1)S(1)} %bitcast.179), channel_id=1, source_target_pairs={{0,8},{8,0},{16,24},{24,16},{1,9},{9,1},{17,25},{25,17},{2,10},{10... | collective-permute-start | bytes 2641928 | tf_op jit(solution)/shard_map/ppermute | solution.py:65
  8.0 21.5 %collective-permute-start.1 = (bf16[2,160,1376]{2,1,0:T(8,128)(2,1)S(1)}, bf16[2,160,1376]{2,1,0:T(8,128)(2,1)S(1)}, u32[]{:S(2)}, u32[]{:S(2)}) collective-permute-start(bf16[2,160,1376]{2,1,0:T(8,128)(2,1)S(1)} %bitcast.180), channel_id=1, source_target_pairs={{0,16},{8,24},{16,0},{24,8},{1,17},{9,25},{17,1},{25,9},{2,18},{10... | collective-permute-start | bytes 2641928 | tf_op jit(solution)/shard_map/ppermute | solution.py:65
  9.8 32.7 %collective-permute-start.5 = (bf16[640,512]{1,0:T(8,128)(2,1)S(1)}, bf16[640,512]{1,0:T(8,128)(2,1)}, u32[]{:S(2)}, u32[]{:S(2)}) collective-permute-start(bf16[640,512]{1,0:T(8,128)(2,1)S(1)} %bitcast.170), channel_id=1, source_target_pairs={{0,2},{1,3},{2,0},{3,1},{4,6},{5,7},{6,4},{7,5},{8,10},{9,11},{10,... | collective-permute-start | bytes 1966088 | tf_op jit(solution)/shard_map/ppermute | solution.py:71
  11.4 31.1 %collective-permute-start.6 = (bf16[640,512]{1,0:T(8,128)(2,1)S(1)}, bf16[640,512]{1,0:T(8,128)(2,1)}, u32[]{:S(2)}, u32[]{:S(2)}) collective-permute-start(bf16[640,512]{1,0:T(8,128)(2,1)S(1)} %bitcast.171), channel_id=1, source_target_pairs={{0,4},{1,5},{2,6},{3,7},{4,0},{5,1},{6,2},{7,3},{8,12},{9,13},{10,... | collective-permute-start | bytes 1966088 | tf_op jit(solution)/shard_map/ppermute | solution.py:71
  29.8 11.1 %collective-permute-start.4 = (bf16[1,160,1376]{2,1,0:T(8,128)(2,1)S(1)}, bf16[1,160,1376]{2,1,0:T(8,128)(2,1)S(1)}, u32[]{:S(2)}, u32[]{:S(2)}) collective-permute-start(bf16[1,160,1376]{2,1,0:T(8,128)(2,1)S(1)} %slice.258), channel_id=1, source_target_pairs={{0,8},{8,0},{16,24},{24,16},{1,9},{9,1},{17,25},{25,17},{2,10},{10... | collective-permute-start | bytes 1320968 | tf_op jit(solution)/shard_map/ppermute | solution.py:65
  31.6 10.8 %collective-permute-start.3 = (bf16[1,160,1376]{2,1,0:T(8,128)(2,1)S(1)}, bf16[1,160,1376]{2,1,0:T(8,128)(2,1)S(1)}, u32[]{:S(2)}, u32[]{:S(2)}) collective-permute-start(bf16[1,160,1376]{2,1,0:T(8,128)(2,1)S(1)} %slice.259), channel_id=1, source_target_pairs={{0,16},{8,24},{16,0},{24,8},{1,17},{9,25},{17,1},{25,9},{2,18},{10... | collective-permute-start | bytes 1320968 | tf_op jit(solution)/shard_map/ppermute | solution.py:65
  42.8 10.5 %collective-permute-start.7 = (bf16[2,80,1376]{2,1,0:T(8,128)(2,1)S(1)}, bf16[2,80,1376]{2,1,0:T(8,128)(2,1)S(1)}, u32[]{:S(2)}, u32[]{:S(2)}) collective-permute-start(bf16[2,80,1376]{2,1,0:T(8,128)(2,1)S(1)} %bitcast.201), channel_id=1, source_target_pairs={{0,8},{8,0},{16,24},{24,16},{1,9},{9,1},{17,25},{25,17},{2,10},{10... | collective-permute-start | bytes 1320968 | tf_op jit(solution)/shard_map/ppermute | solution.py:65
  43.4 11.1 %collective-permute-start.8 = (bf16[2,80,1376]{2,1,0:T(8,128)(2,1)S(1)}, bf16[2,80,1376]{2,1,0:T(8,128)(2,1)S(1)}, u32[]{:S(2)}, u32[]{:S(2)}) collective-permute-start(bf16[2,80,1376]{2,1,0:T(8,128)(2,1)S(1)} %bitcast.202), channel_id=1, source_target_pairs={{0,16},{8,24},{16,0},{24,8},{1,17},{9,25},{17,1},{25,9},{2,18},{10... | collective-permute-start | bytes 1320968 | tf_op jit(solution)/shard_map/ppermute | solution.py:65
  44.9 11.6 %collective-permute-start.11 = (bf16[640,512]{1,0:T(8,128)(2,1)}, bf16[640,512]{1,0:T(8,128)(2,1)S(1)}, u32[]{:S(2)}, u32[]{:S(2)}) collective-permute-start(bf16[640,512]{1,0:T(8,128)(2,1)} %collective-permute-done.6.refs_0_), channel_id=1, source_target_pairs={{0,1},{1,0},{2,3},{3,2},{4,5},{5,4},{6,7},{7,6},{8,9},{9,8},{10,11... | collective-permute-start | bytes 1966088 | tf_op jit(solution)/shard_map/ppermute | solution.py:68
  44.9 17.9 %collective-permute-start.13 = (bf16[640,512]{1,0:T(8,128)(2,1)}, bf16[640,512]{1,0:T(8,128)(2,1)}, u32[]{:S(2)}, u32[]{:S(2)}) collective-permute-start(bf16[640,512]{1,0:T(8,128)(2,1)} %collective-permute-done.6.refs_0_), channel_id=1, source_target_pairs={{0,2},{1,3},{2,0},{3,1},{4,6},{5,7},{6,4},{7,5},{8,10},{9,11},{10,... | collective-permute-start | bytes 1966088 | tf_op jit(solution)/shard_map/ppermute | solution.py:71
  46.5 16.3 %collective-permute-start.12 = (bf16[640,512]{1,0:T(8,128)(2,1)}, bf16[640,512]{1,0:T(8,128)(2,1)S(1)}, u32[]{:S(2)}, u32[]{:S(2)}) collective-permute-start(bf16[640,512]{1,0:T(8,128)(2,1)} %collective-permute-done.5.refs_0_), channel_id=1, source_target_pairs={{0,1},{1,0},{2,3},{3,2},{4,5},{5,4},{6,7},{7,6},{8,9},{9,8},{10,11... | collective-permute-start | bytes 1966088 | tf_op jit(solution)/shard_map/ppermute | solution.py:68
  54.5 8.4 %collective-permute-start.10 = (bf16[80,1376]{1,0:T(8,128)(2,1)S(1)}, bf16[80,1376]{1,0:T(8,128)(2,1)S(1)}, u32[]{:S(2)}, u32[]{:S(2)}) collective-permute-start(bf16[80,1376]{1,0:T(8,128)(2,1)S(1)} %slice_bitcast_fusion.20), channel_id=1, source_target_pairs={{0,16},{8,24},{16,0},{24,8},{1,17},{9,25},{17,1},{25,9},{2,18},{10... | collective-permute-start | bytes 660488 | tf_op jit(solution)/shard_map/ppermute | solution.py:65
  55.1 7.8 %collective-permute-start.9 = (bf16[80,1376]{1,0:T(8,128)(2,1)S(1)}, bf16[80,1376]{1,0:T(8,128)(2,1)S(1)}, u32[]{:S(2)}, u32[]{:S(2)}) collective-permute-start(bf16[80,1376]{1,0:T(8,128)(2,1)S(1)} %slice_bitcast_fusion.21), channel_id=1, source_target_pairs={{0,8},{8,0},{16,24},{24,16},{1,9},{9,1},{17,25},{25,17},{2,10},{10... | collective-permute-start | bytes 660488 | tf_op jit(solution)/shard_map/ppermute | solution.py:65
  65.6 7.3 %collective-permute-start.15 = (bf16[640,512]{1,0:T(8,128)(2,1)}, bf16[640,512]{1,0:T(8,128)(2,1)}, u32[]{:S(2)}, u32[]{:S(2)}) collective-permute-start(bf16[640,512]{1,0:T(8,128)(2,1)} %collective-permute-done.13.refs_2_), channel_id=1, source_target_pairs={{0,1},{1,0},{2,3},{3,2},{4,5},{5,4},{6,7},{7,6},{8,9},{9,8},{10,11... | collective-permute-start | bytes 1966088 | tf_op jit(solution)/shard_map/ppermute | solution.py:68
  66.1 25.1 %collective-permute-start.19 = (bf16[2,160,1376]{2,1,0:T(8,128)(2,1)}, bf16[2,160,1376]{2,1,0:T(8,128)(2,1)}, u32[]{:S(2)}, u32[]{:S(2)}) collective-permute-start(bf16[2,160,1376]{2,1,0:T(8,128)(2,1)} %pad_maximum_fusion), channel_id=1, source_target_pairs={{0,8},{8,0},{16,24},{24,16},{1,9},{9,1},{17,25},{25,17},{2,10},{10... | collective-permute-start | bytes 2641928 | tf_op jit(solution)/shard_map/ppermute | solution.py:65
  67.1 24.1 %collective-permute-start.20 = (bf16[2,160,1376]{2,1,0:T(8,128)(2,1)}, bf16[2,160,1376]{2,1,0:T(8,128)(2,1)}, u32[]{:S(2)}, u32[]{:S(2)}) collective-permute-start(bf16[2,160,1376]{2,1,0:T(8,128)(2,1)} %pad_maximum_fusion), channel_id=1, source_target_pairs={{0,16},{8,24},{16,0},{24,8},{1,17},{9,25},{17,1},{25,9},{2,18},{10... | collective-permute-start | bytes 2641928 | tf_op jit(solution)/shard_map/ppermute | solution.py:65
  73.0 15.1 %collective-permute-start.16 = (bf16[80,1024]{1,0:T(8,128)(2,1)S(1)}, bf16[80,1024]{1,0:T(8,128)(2,1)S(1)}, u32[]{:S(2)}, u32[]{:S(2)}) collective-permute-start(bf16[80,1024]{1,0:T(8,128)(2,1)S(1)} %get-tuple-element.285), channel_id=1, source_target_pairs={{0,2},{1,3},{2,0},{3,1},{4,6},{5,7},{6,4},{7,5},{8,10},{9,11},{10,... | collective-permute-start | bytes 491528 | tf_op jit(solution)/shard_map/ppermute | solution.py:71
  75.5 12.6 %collective-permute-start.17 = (bf16[80,1024]{1,0:T(8,128)(2,1)S(1)}, bf16[80,1024]{1,0:T(8,128)(2,1)S(1)}, u32[]{:S(2)}, u32[]{:S(2)}) collective-permute-start(bf16[80,1024]{1,0:T(8,128)(2,1)S(1)} %get-tuple-element.284), channel_id=1, source_target_pairs={{0,4},{1,5},{2,6},{3,7},{4,0},{5,1},{6,2},{7,3},{8,12},{9,13},{10,... | collective-permute-start | bytes 491528 | tf_op jit(solution)/shard_map/ppermute | solution.py:71
  76.1 15.1 %collective-permute-start.18 = (bf16[80,1024]{1,0:T(8,128)(2,1)S(1)}, bf16[80,1024]{1,0:T(8,128)(2,1)S(1)}, u32[]{:S(2)}, u32[]{:S(2)}) collective-permute-start(bf16[80,1024]{1,0:T(8,128)(2,1)S(1)} %get-tuple-element.283), channel_id=1, source_target_pairs={{0,6},{1,7},{2,4},{3,5},{4,2},{5,3},{6,0},{7,1},{8,14},{9,15},{10,... | collective-permute-start | bytes 491528 | tf_op jit(solution)/shard_map/ppermute | solution.py:71
  92.7 12.6 %collective-permute-start.21 = (bf16[80,1024]{1,0:T(8,128)(2,1)S(1)}, bf16[80,1024]{1,0:T(8,128)(2,1)S(1)}, u32[]{:S(2)}, u32[]{:S(2)}) collective-permute-start(bf16[80,1024]{1,0:T(8,128)(2,1)S(1)} %fusion.12), channel_id=1, source_target_pairs={{0,4},{1,5},{2,6},{3,7},{4,0},{5,1},{6,2},{7,3},{8,12},{9,13},{10,... | collective-permute-start | bytes 491528 | tf_op jit(solution)/shard_map/ppermute | solution.py:71
  94.6 14.4 %collective-permute-start.22 = (bf16[80,1024]{1,0:T(8,128)(2,1)S(1)}, bf16[80,1024]{1,0:T(8,128)(2,1)S(1)}, u32[]{:S(2)}, u32[]{:S(2)}) collective-permute-start(bf16[80,1024]{1,0:T(8,128)(2,1)S(1)} %fusion.12), channel_id=1, source_target_pairs={{0,6},{1,7},{2,4},{3,5},{4,2},{5,3},{6,0},{7,1},{8,14},{9,15},{10,... | collective-permute-start | bytes 491528 | tf_op jit(solution)/shard_map/ppermute | solution.py:71
  99.5 9.5 %collective-permute-start.24 = (bf16[160,1024]{1,0:T(8,128)(2,1)S(1)}, bf16[160,1024]{1,0:T(8,128)(2,1)S(1)}, u32[]{:S(2)}, u32[]{:S(2)}) collective-permute-start(bf16[160,1024]{1,0:T(8,128)(2,1)S(1)} %constant_dynamic-update-slice_fusion.refs_0_), channel_id=1, source_target_pairs={{0,8},{8,0},{16,24},{24,16},{1,9},{9,1},{17,25},{25,17},{2,10},{10... | collective-permute-start | bytes 983048 | tf_op jit(solution)/shard_map/ppermute | solution.py:65
  100.6 8.4 %collective-permute-start.25 = (bf16[160,1024]{1,0:T(8,128)(2,1)S(1)}, bf16[160,1024]{1,0:T(8,128)(2,1)S(1)}, u32[]{:S(2)}, u32[]{:S(2)}) collective-permute-start(bf16[160,1024]{1,0:T(8,128)(2,1)S(1)} %constant_dynamic-update-slice_fusion.refs_0_), channel_id=1, source_target_pairs={{0,16},{8,24},{16,0},{24,8},{1,17},{9,25},{17,1},{25,9},{2,18},{10... | collective-permute-start | bytes 983048 | tf_op jit(solution)/shard_map/ppermute | solution.py:65
  102.1 12.1 %collective-permute-start.31 = (bf16[160,1024]{1,0:T(8,128)(2,1)S(1)}, bf16[160,1024]{1,0:T(8,128)(2,1)S(1)}, u32[]{:S(2)}, u32[]{:S(2)}) collective-permute-start(bf16[160,1024]{1,0:T(8,128)(2,1)S(1)} %constant_dynamic-update-slice_fusion.refs_0_), channel_id=1, source_target_pairs={{0,1},{1,0},{2,3},{3,2},{4,5},{5,4},{6,7},{7,6},{8,9},{9,8},{10,11... | collective-permute-start | bytes 983048 | tf_op jit(solution)/shard_map/ppermute | solution.py:68
  105.3 20.4 %collective-permute-start.29 = (bf16[160,1376]{1,0:T(8,128)(2,1)S(1)}, bf16[160,1376]{1,0:T(8,128)(2,1)S(1)}, u32[]{:S(2)}, u32[]{:S(2)}) collective-permute-start(bf16[160,1376]{1,0:T(8,128)(2,1)S(1)} %get-tuple-element.267.refs_10_), channel_id=1, source_target_pairs={{0,8},{8,0},{16,24},{24,16},{1,9},{9,1},{17,25},{25,17},{2,10},{10... | collective-permute-start | bytes 1320968 | tf_op jit(solution)/shard_map/ppermute | solution.py:65
  111.1 14.5 %collective-permute-start.30 = (bf16[160,1376]{1,0:T(8,128)(2,1)S(1)}, bf16[160,1376]{1,0:T(8,128)(2,1)S(1)}, u32[]{:S(2)}, u32[]{:S(2)}) collective-permute-start(bf16[160,1376]{1,0:T(8,128)(2,1)S(1)} %get-tuple-element.271.refs_13_), channel_id=1, source_target_pairs={{0,16},{8,24},{16,0},{24,8},{1,17},{9,25},{17,1},{25,9},{2,18},{10... | collective-permute-start | bytes 1320968 | tf_op jit(solution)/shard_map/ppermute | solution.py:65
  112.6 13.1 %collective-permute-start.27 = (bf16[160,1024]{1,0:T(8,128)(2,1)S(1)}, bf16[160,1024]{1,0:T(8,128)(2,1)S(1)}, u32[]{:S(2)}, u32[]{:S(2)}) collective-permute-start(bf16[160,1024]{1,0:T(8,128)(2,1)S(1)} %constant_dynamic-update-slice_fusion.2.refs_1_), channel_id=1, source_target_pairs={{0,8},{8,0},{16,24},{24,16},{1,9},{9,1},{17,25},{25,17},{2,10},{10... | collective-permute-start | bytes 983048 | tf_op jit(solution)/shard_map/ppermute | solution.py:65
  114.2 16.7 %collective-permute-start.28 = (bf16[160,1024]{1,0:T(8,128)(2,1)S(1)}, bf16[160,1024]{1,0:T(8,128)(2,1)S(1)}, u32[]{:S(2)}, u32[]{:S(2)}) collective-permute-start(bf16[160,1024]{1,0:T(8,128)(2,1)S(1)} %constant_dynamic-update-slice_fusion.2.refs_1_), channel_id=1, source_target_pairs={{0,16},{8,24},{16,0},{24,8},{1,17},{9,25},{17,1},{25,9},{2,18},{10... | collective-permute-start | bytes 983048 | tf_op jit(solution)/shard_map/ppermute | solution.py:65
  131.4 16.8 %collective-permute-start.26 = (bf16[160,1024]{1,0:T(8,128)(2,1)S(1)}, bf16[160,1024]{1,0:T(8,128)(2,1)S(1)}, u32[]{:S(2)}, u32[]{:S(2)}) collective-permute-start(bf16[160,1024]{1,0:T(8,128)(2,1)S(1)} %collective-permute-done.25.refs_0_), channel_id=1, source_target_pairs={{0,8},{8,0},{16,24},{24,16},{1,9},{9,1},{17,25},{25,17},{2,10},{10... | collective-permute-start | bytes 983048 | tf_op jit(solution)/shard_map/ppermute | solution.py:65
  132.8 15.4 %collective-permute-start.33 = (bf16[160,1024]{1,0:T(8,128)(2,1)S(1)}, bf16[160,1024]{1,0:T(8,128)(2,1)S(1)}, u32[]{:S(2)}, u32[]{:S(2)}) collective-permute-start(bf16[160,1024]{1,0:T(8,128)(2,1)S(1)} %collective-permute-done.27.refs_1_), channel_id=1, source_target_pairs={{0,16},{8,24},{16,0},{24,8},{1,17},{9,25},{17,1},{25,9},{2,18},{10... | collective-permute-start | bytes 983048 | tf_op jit(solution)/shard_map/ppermute | solution.py:65
  134.4 13.8 %collective-permute-start.34 = (bf16[160,1024]{1,0:T(8,128)(2,1)S(1)}, bf16[160,1024]{1,0:T(8,128)(2,1)S(1)}, u32[]{:S(2)}, u32[]{:S(2)}) collective-permute-start(bf16[160,1024]{1,0:T(8,128)(2,1)S(1)} %collective-permute-done.25.refs_0_), channel_id=1, source_target_pairs={{0,1},{1,0},{2,3},{3,2},{4,5},{5,4},{6,7},{7,6},{8,9},{9,8},{10,11... | collective-permute-start | bytes 983048 | tf_op jit(solution)/shard_map/ppermute | solution.py:68
  134.4 13.8 %collective-permute-start.35 = (bf16[160,1024]{1,0:T(8,128)(2,1)S(1)}, bf16[160,1024]{1,0:T(8,128)(2,1)S(1)}, u32[]{:S(2)}, u32[]{:S(2)}) collective-permute-start(bf16[160,1024]{1,0:T(8,128)(2,1)S(1)} %collective-permute-done.28.refs_1_), channel_id=1, source_target_pairs={{0,1},{1,0},{2,3},{3,2},{4,5},{5,4},{6,7},{7,6},{8,9},{9,8},{10,11... | collective-permute-start | bytes 983048 | tf_op jit(solution)/shard_map/ppermute | solution.py:68
  177.3 13.8 %collective-permute-start.41 = (bf16[160,1024]{1,0:T(8,128)(2,1)S(1)}, bf16[160,1024]{1,0:T(8,128)(2,1)S(1)}, u32[]{:S(2)}, u32[]{:S(2)}) collective-permute-start(bf16[160,1024]{1,0:T(8,128)(2,1)S(1)} %get-tuple-element.282), channel_id=1, source_target_pairs={{0,8},{8,0},{16,24},{24,16},{1,9},{9,1},{17,25},{25,17},{2,10},{10... | collective-permute-start | bytes 983048 | tf_op jit(solution)/shard_map/ppermute | solution.py:65
  177.8 13.3 %collective-permute-start.42 = (bf16[160,1024]{1,0:T(8,128)(2,1)S(1)}, bf16[160,1024]{1,0:T(8,128)(2,1)S(1)}, u32[]{:S(2)}, u32[]{:S(2)}) collective-permute-start(bf16[160,1024]{1,0:T(8,128)(2,1)S(1)} %get-tuple-element.281), channel_id=1, source_target_pairs={{0,16},{8,24},{16,0},{24,8},{1,17},{9,25},{17,1},{25,9},{2,18},{10... | collective-permute-start | bytes 983048 | tf_op jit(solution)/shard_map/ppermute | solution.py:65
  195.2 16.8 %collective-permute-start.44 = (bf16[2,160,1024]{2,1,0:T(8,128)(2,1)S(1)}, bf16[2,160,1024]{2,1,0:T(8,128)(2,1)S(1)}, u32[]{:S(2)}, u32[]{:S(2)}) collective-permute-start(bf16[2,160,1024]{2,1,0:T(8,128)(2,1)S(1)} %get-tuple-element.213), channel_id=1, source_target_pairs={{0,8},{8,0},{16,24},{24,16},{1,9},{9,1},{17,25},{25,17},{2,10},{10... | collective-permute-start | bytes 1966088 | tf_op jit(solution)/shard_map/ppermute | solution.py:65
  196.7 16.5 %collective-permute-start.45 = (bf16[2,160,1024]{2,1,0:T(8,128)(2,1)S(1)}, bf16[2,160,1024]{2,1,0:T(8,128)(2,1)S(1)}, u32[]{:S(2)}, u32[]{:S(2)}) collective-permute-start(bf16[2,160,1024]{2,1,0:T(8,128)(2,1)S(1)} %get-tuple-element.214), channel_id=1, source_target_pairs={{0,16},{8,24},{16,0},{24,8},{1,17},{9,25},{17,1},{25,9},{2,18},{10... | collective-permute-start | bytes 1966088 | tf_op jit(solution)/shard_map/ppermute | solution.py:65
  215.9 13.6 %collective-permute-start.48 = (bf16[80,1024]{1,0:T(8,128)(2,1)S(1)}, bf16[80,1024]{1,0:T(8,128)(2,1)S(1)}, u32[]{:S(2)}, u32[]{:S(2)}) collective-permute-start(bf16[80,1024]{1,0:T(8,128)(2,1)S(1)} %get-tuple-element.279), channel_id=1, source_target_pairs={{0,4},{1,5},{2,6},{3,7},{4,0},{5,1},{6,2},{7,3},{8,12},{9,13},{10,... | collective-permute-start | bytes 491528 | tf_op jit(solution)/shard_map/ppermute | solution.py:71
  218.0 16.0 %collective-permute-start.49 = (bf16[80,1024]{1,0:T(8,128)(2,1)S(1)}, bf16[80,1024]{1,0:T(8,128)(2,1)S(1)}, u32[]{:S(2)}, u32[]{:S(2)}) collective-permute-start(bf16[80,1024]{1,0:T(8,128)(2,1)S(1)} %get-tuple-element.278), channel_id=1, source_target_pairs={{0,6},{1,7},{2,4},{3,5},{4,2},{5,3},{6,0},{7,1},{8,14},{9,15},{10,... | collective-permute-start | bytes 491528 | tf_op jit(solution)/shard_map/ppermute | solution.py:71
  234.1 13.2 %collective-permute-start.51 = (bf16[80,1024]{1,0:T(8,128)(2,1)S(1)}, bf16[80,1024]{1,0:T(8,128)(2,1)S(1)}, u32[]{:S(2)}, u32[]{:S(2)}) collective-permute-start(bf16[80,1024]{1,0:T(8,128)(2,1)S(1)} %get-tuple-element.253), channel_id=1, source_target_pairs={{0,4},{1,5},{2,6},{3,7},{4,0},{5,1},{6,2},{7,3},{8,12},{9,13},{10,... | collective-permute-start | bytes 491528 | tf_op jit(solution)/shard_map/ppermute | solution.py:71
  236.2 14.8 %collective-permute-start.52 = (bf16[80,1024]{1,0:T(8,128)(2,1)S(1)}, bf16[80,1024]{1,0:T(8,128)(2,1)S(1)}, u32[]{:S(2)}, u32[]{:S(2)}) collective-permute-start(bf16[80,1024]{1,0:T(8,128)(2,1)S(1)} %get-tuple-element.253), channel_id=1, source_target_pairs={{0,6},{1,7},{2,4},{3,5},{4,2},{5,3},{6,0},{7,1},{8,14},{9,15},{10,... | collective-permute-start | bytes 491528 | tf_op jit(solution)/shard_map/ppermute | solution.py:71
  256.2 7.6 %collective-permute-start.54 = (bf16[80,1376]{1,0:T(8,128)(2,1)S(1)}, bf16[80,1376]{1,0:T(8,128)(2,1)S(1)}, u32[]{:S(2)}, u32[]{:S(2)}) collective-permute-start(bf16[80,1376]{1,0:T(8,128)(2,1)S(1)} %get-tuple-element.293), channel_id=1, source_target_pairs={{0,16},{8,24},{16,0},{24,8},{1,17},{9,25},{17,1},{25,9},{2,18},{10... | collective-permute-start | bytes 660488 | tf_op jit(solution)/shard_map/ppermute | solution.py:65
  265.3 11.3 %collective-permute-start.56 = (bf16[2,80,1376]{2,1,0:T(8,128)(2,1)S(1)}, bf16[2,80,1376]{2,1,0:T(8,128)(2,1)S(1)}, u32[]{:S(2)}, u32[]{:S(2)}) collective-permute-start(bf16[2,80,1376]{2,1,0:T(8,128)(2,1)S(1)} %pad_maximum_fusion.4), channel_id=1, source_target_pairs={{0,8},{8,0},{16,24},{24,16},{1,9},{9,1},{17,25},{25,17},{2,10},{10... | collective-permute-start | bytes 1320968 | tf_op jit(solution)/shard_map/ppermute | solution.py:65
  265.8 10.9 %collective-permute-start.57 = (bf16[2,80,1376]{2,1,0:T(8,128)(2,1)S(1)}, bf16[2,80,1376]{2,1,0:T(8,128)(2,1)S(1)}, u32[]{:S(2)}, u32[]{:S(2)}) collective-permute-start(bf16[2,80,1376]{2,1,0:T(8,128)(2,1)S(1)} %pad_maximum_fusion.5), channel_id=1, source_target_pairs={{0,16},{8,24},{16,0},{24,8},{1,17},{9,25},{17,1},{25,9},{2,18},{10... | collective-permute-start | bytes 1320968 | tf_op jit(solution)/shard_map/ppermute | solution.py:65
  276.9 10.2 %collective-permute-start.58 = (bf16[2,80,1376]{2,1,0:T(8,128)(2,1)S(1)}, bf16[2,80,1376]{2,1,0:T(8,128)(2,1)S(1)}, u32[]{:S(2)}, u32[]{:S(2)}) collective-permute-start(bf16[2,80,1376]{2,1,0:T(8,128)(2,1)S(1)} %fusion.2), channel_id=1, source_target_pairs={{0,8},{8,0},{16,24},{24,16},{1,9},{9,1},{17,25},{25,17},{2,10},{10... | collective-permute-start | bytes 1320968 | tf_op jit(solution)/shard_map/ppermute | solution.py:65
  278.6 9.9 %collective-permute-start.59 = (bf16[2,80,1376]{2,1,0:T(8,128)(2,1)S(1)}, bf16[2,80,1376]{2,1,0:T(8,128)(2,1)S(1)}, u32[]{:S(2)}, u32[]{:S(2)}) collective-permute-start(bf16[2,80,1376]{2,1,0:T(8,128)(2,1)S(1)} %fusion.2), channel_id=1, source_target_pairs={{0,16},{8,24},{16,0},{24,8},{1,17},{9,25},{17,1},{25,9},{2,18},{10... | collective-permute-start | bytes 1320968 | tf_op jit(solution)/shard_map/ppermute | solution.py:65
  306.1 10.8 %collective-permute-start.63 = (bf16[80,1024]{1,0:T(8,128)(2,1)S(1)}, bf16[80,1024]{1,0:T(8,128)(2,1)S(1)}, u32[]{:S(2)}, u32[]{:S(2)}) collective-permute-start(bf16[80,1024]{1,0:T(8,128)(2,1)S(1)} %get-tuple-element.277), channel_id=1, source_target_pairs={{0,2},{1,3},{2,0},{3,1},{4,6},{5,7},{6,4},{7,5},{8,10},{9,11},{10,... | collective-permute-start | bytes 491528 | tf_op jit(solution)/shard_map/ppermute | solution.py:71
  306.2 13.8 %collective-permute-start.64 = (bf16[80,1024]{1,0:T(8,128)(2,1)S(1)}, bf16[80,1024]{1,0:T(8,128)(2,1)S(1)}, u32[]{:S(2)}, u32[]{:S(2)}) collective-permute-start(bf16[80,1024]{1,0:T(8,128)(2,1)S(1)} %get-tuple-element.276), channel_id=1, source_target_pairs={{0,4},{1,5},{2,6},{3,7},{4,0},{5,1},{6,2},{7,3},{8,12},{9,13},{10,... | collective-permute-start | bytes 491528 | tf_op jit(solution)/shard_map/ppermute | solution.py:71
  308.3 15.8 %collective-permute-start.65 = (bf16[80,1024]{1,0:T(8,128)(2,1)S(1)}, bf16[80,1024]{1,0:T(8,128)(2,1)S(1)}, u32[]{:S(2)}, u32[]{:S(2)}) collective-permute-start(bf16[80,1024]{1,0:T(8,128)(2,1)S(1)} %get-tuple-element.275), channel_id=1, source_target_pairs={{0,6},{1,7},{2,4},{3,5},{4,2},{5,3},{6,0},{7,1},{8,14},{9,15},{10,... | collective-permute-start | bytes 491528 | tf_op jit(solution)/shard_map/ppermute | solution.py:71
  (62 other events, 544.2 us)

commit v4 on v3

--- a/solution.py
+++ b/solution.py
@@ -285,29 +285,36 @@
 
 def pre_kernel(n, begun, index, *refs):
     pieces, (gate_w, up_w), refs = refs[:n], refs[n : n + 2], refs[n + 2 :]
-    start, (pre, lin) = refs[:begun], refs[begun:]
+    start, sums, sems = refs[:begun], refs[begun : begun + 2], refs[begun + 2 :]
+    copies = [pltpu.make_async_copy(start[i], sums[i], sems[0].at[i]) for i in range(begun)]
+    for copy in copies:
+        copy.start()
     value = jnp.concatenate([piece[...] for piece in pieces], 0)
-    for i, (weight, out) in enumerate(((gate_w, pre), (up_w, lin))):
+    for i, weight in enumerate((gate_w, up_w)):
         product = dot_nt(value, weight[...])
-        out[...] = start[i][...] + product if begun else product
+        if begun:
+            copies[i].wait()
+            sums[i][...] += product
+        else:
+            sums[i][...] = product
 
 
 def pre_product(index, offset, parts, gate_t, up_t, start=()):
     rows, depth = sum(part.shape[0] for part in parts), parts[0].shape[1]
     units = gate_t.shape[0]
     weight = pl.BlockSpec((units, depth), lambda i, index: (0, index[offset]), pipeline_mode=pl.Buffered(1))
-    both = [whole((rows, units))] * 2
     return call(
         functools.partial(pre_kernel, len(parts), len(start)),
         "head_pre",
         (1,),
         index,
-        [whole(part.shape) for part in parts] + [weight] * 2 + both[: len(start)],
-        both,
+        [whole(part.shape) for part in parts] + [weight] * 2 + [pl.BlockSpec(memory_space=pl.ANY)] * len(start),
+        [whole((rows, units))] * 2,
         [jax.ShapeDtypeStruct((rows, units), F32)] * 2,
         [*parts, gate_t, up_t, *start],
         4 * rows * depth * units,
         48,
+        [pltpu.SemaphoreType.DMA((2,))] if start else [],
     )
 
 
@@ -579,7 +586,7 @@
             return parts + [plan.core_swap(part) for part in parts]
 
         pre, lin = pre_product(index, 0, both_cores([top, low]), gate_t, up_t)
-        wide, rest, pre, lin = lax.optimization_barrier((wide, rest, pre, lin))
+        wide, rest, relayed, pre, lin = lax.optimization_barrier((wide, rest, relayed, pre, lin))
         have = have | rest
         gates, ups = ([have[k][i] for k in range(groups)] for i in range(2))
         relayed += [plan.group_swap(wide[1][1], 2)] if groups == 4 else []

time: 330 us -> 326 us (0.988)
  transfers between devices with their start and end apart: 66 -> 66, of which waited for: 36 -> 35; matrix products, arithmetic and copies ran while one was open for 4% -> 4% of each run, Pallas kernels for 25% -> 25%
where the time goes in v4:
time: 326 us; the launch traced here: 323 us
  Pallas kernels  117 us (36%)
  waiting for transfers between devices  117 us (36%)
  starting transfers between devices  60.1 us (18%)
  local copies, waits for them, and re-layouts  15.5 us (5%)
  other arithmetic  7.28 us (2%)
  matrix products  4.91 us (2%)
    pallas_call x19, Pallas kernels, call(): pl.pallas_call(kernel, grid_spec=pltpu.PrefetchScalarGridSpec(num_scalar_...  117 us
    ppermute x30, waiting for transfers between devices, group_swap(): lax.ppermute(value, 'group', [(i, i ^ mask) for i in range(self.groups)])  59.7 us
    ppermute x18, waiting for transfers between devices, place_swap(): lax.ppermute(value, 'mp', [(i, i ^ 2 * mask) for i in range(self.members)])  43.9 us
    ppermute x30, starting transfers between devices, group_swap(): lax.ppermute(value, 'group', [(i, i ^ mask) for i in range(self.groups)])  35.3 us
    ppermute x18, starting transfers between devices, place_swap(): lax.ppermute(value, 'mp', [(i, i ^ 2 * mask) for i in range(self.members)])  21.8 us
    ppermute x18, waiting for transfers between devices, core_swap(): return lax.ppermute(value, 'mp', [(i, i ^ 1) for i in range(self.members)])  13 us
    unnamed x93, local copies, waits for them, and re-layouts  9.92 us
  transfers between devices with their start and end apart: 66, of which 35 were waited for; matrix products, arithmetic and copies ran while one was open for 4% of the time, Pallas kernels for 25%

profile of v4, /device:TPU:18, one launch (start us, length us, event | category | flops | bytes accessed | tf_op | source)
XLA Modules:
  0.0 323.1 jit_solution(6332319724449720275)
XLA Ops:
  16.8 4.4 %head_hidden_grad.3.refs_3_ = f32[640,1376]{1,0:T(8,128)S(1)} custom-call(s32[28]{0:T(128)S(1)} %stack.137.index, bf16[640,512]{1,0:T(8,128)(2,1)S(1)} %bitcast.172, bf16[640,512]{1,0:T(8,128)(2,1)S(1)} %collective-permute-done.2.refs_1_, bf16[1376,4096]{1,0:T(8,128)(2,1)} %bitcast.191), custom_call_target="tpu_custom_call" | custom-call | flops 1803550720 | bytes 12582912 | tf_op jit(solution)/shard_map/head_hidden_grad/pallas_call | solution.py:46
  21.2 6.3 %collective-permute-done = bf16[2,160,1376]{2,1,0:T(8,128)(2,1)S(1)} collective-permute-done((bf16[2,160,1376]{2,1,0:T(8,128)(2,1)S(1)}, bf16[2,160,1376]{2,1,0:T(8,128)(2,1)S(1)}, u32[]{:S(2)}, u32[]{:S(2)}) %collective-permute-start) | collective-permute-done | bytes 880672 | tf_op jit(solution)/shard_map/ppermute | solution.py:65
  27.5 2.1 collective-permute-done.1
  33.2 7.7 %collective-permute-done.4 = bf16[1,160,1376]{2,1,0:T(8,128)(2,1)S(1)} collective-permute-done((bf16[1,160,1376]{2,1,0:T(8,128)(2,1)S(1)}, bf16[1,160,1376]{2,1,0:T(8,128)(2,1)S(1)}, u32[]{:S(2)}, u32[]{:S(2)}) %collective-permute-start.4) | collective-permute-done | bytes 440352 | tf_op jit(solution)/shard_map/ppermute | solution.py:65
  47.7 5.5 %collective-permute-done.7 = bf16[2,80,1376]{2,1,0:T(8,128)(2,1)S(1)} collective-permute-done((bf16[2,80,1376]{2,1,0:T(8,128)(2,1)S(1)}, bf16[2,80,1376]{2,1,0:T(8,128)(2,1)S(1)}, u32[]{:S(2)}, u32[]{:S(2)}) %collective-permute-start.7) | collective-permute-done | bytes 440352 | tf_op jit(solution)/shard_map/ppermute | solution.py:65
  56.5 6.2 %head_hidden_grad.4.refs_5_ = f32[640,1376]{1,0:T(8,128)S(1)} custom-call(s32[28]{0:T(128)S(1)} %stack.137.index, bf16[640,512]{1,0:T(8,128)(2,1)} %collective-permute-done.6.refs_0_, bf16[640,512]{1,0:T(8,128)(2,1)S(1)} %collective-permute-done.11.refs_1_, bf16[1376,4096]{1,0:T(8,128)(2,1)} %bitcast.192, f32[640,1376]{1,0:T(8,128)} %copy-done.5), custom_call_target="tpu_custom_call" | custom-call | flops 1803550720 | bytes 16105472 | tf_op jit(solution)/shard_map/head_hidden_grad/pallas_call | solution.py:46
  62.9 2.6 trunk_down.2
  70.1 2.8 trunk_down.3
  73.0 2.5 collective-permute-start.16
  77.1 11.0 %head_hidden_grad.5 = f32[640,1376]{1,0:T(8,128)} custom-call(s32[28]{0:T(128)S(1)} %stack.137.index, bf16[640,512]{1,0:T(8,128)(2,1)} %collective-permute-done.5.refs_0_, bf16[640,512]{1,0:T(8,128)(2,1)S(1)} %copy-done.22, bf16[640,512]{1,0:T(8,128)(2,1)} %collective-permute-done.13.refs_2_, bf16[640,512]{1,0:T(8,128)(2,1)} %collective-permute-done.15.refs_3_, ...), custom_call_target="tpu_custom_call" | custom-call | flops 3607101440 | bytes 17416192 | tf_op jit(solution)/shard_map/head_hidden_grad/pallas_call | solution.py:46
  88.1 3.1 collective-permute-done.18
  92.7 1.9 collective-permute-start.21
  95.8 2.2 head_output_grad_rows.1.refs_13_.cot
  103.3 1.9 collective-permute-done.21
  106.7 2.3 collective-permute-done.22
  109.1 2.0 slice_bitcast_fusion.4
  115.2 9.3 %head_pre.2 = (f32[640,1376]{1,0:T(8,128)S(1)}, f32[640,1376]{1,0:T(8,128)}) custom-call(s32[28]{0:T(128)S(1)} %stack.137.index, bf16[160,1024]{1,0:T(8,128)(2,1)S(1)} %constant_dynamic-update-slice_fusion.refs_0_, bf16[160,1024]{1,0:T(8,128)(2,1)S(1)} %constant_dynamic-update-slice_fusion.2.refs_1_, bf16[160,1024]{1,0:T(8,128)(2,1)S(1)} %collective-permute-done.31.refs_2_, ...), custom_call_target="tpu_custom_call" | custom-call | flops 3607101440 | bytes 23855104 | tf_op jit(solution)/shard_map/head_pre/pallas_call | solution.py:46
  124.5 1.8 copy-done.16
  126.3 4.6 %collective-permute-done.27.refs_1_ = bf16[160,1024]{1,0:T(8,128)(2,1)S(1)} collective-permute-done((bf16[160,1024]{1,0:T(8,128)(2,1)S(1)}, bf16[160,1024]{1,0:T(8,128)(2,1)S(1)}, u32[]{:S(2)}, u32[]{:S(2)}) %collective-permute-start.27) | collective-permute-done | bytes 327712 | tf_op jit(solution)/shard_map/ppermute | solution.py:65
  133.4 10.3 %head_pre.3 = (f32[640,1376]{1,0:T(8,128)S(1)}, f32[640,1376]{1,0:T(8,128)}) custom-call(s32[28]{0:T(128)S(1)} %stack.137.index, bf16[160,1024]{1,0:T(8,128)(2,1)S(1)} %collective-permute-done.24.refs_0_, bf16[160,1024]{1,0:T(8,128)(2,1)S(1)} %collective-permute-done.26.refs_1_, bf16[160,1024]{1,0:T(8,128)(2,1)S(1)} %collective-permute-done.36.refs_2_, ...), custom_call_target="tpu_custom_call" | custom-call | flops 3607101440 | bytes 30900224 | tf_op jit(solution)/shard_map/head_pre/pallas_call | solution.py:46
  143.8 1.8 copy-done.30
  148.8 21.5 %head_act.1 = (bf16[640,1376]{1,0:T(8,128)(2,1)}, bf16[640,1376]{1,0:T(8,128)(2,1)}, bf16[1,320,1024]{2,1,0:T(8,128)(2,1)}, bf16[1,320,1024]{2,1,0:T(8,128)(2,1)}) custom-call(s32[28]{0:T(128)} %copy-done.28, bf16[160,1024]{1,0:T(8,128)(2,1)} %copy-done.36, bf16[160,1024]{1,0:T(8,128)(2,1)} %copy-done.37, bf16[160,1024]{1,0:T(8,128)(2,1)} %copy-done.40, ...), custom_call_target="tpu_custom_call" | custom-call | flops 10821304320 | bytes 36388864 | tf_op jit(solution)/shard_map/head_act/pallas_call | solution.py:46
  170.5 2.2 collective-permute-done.40
  176.9 12.5 %head_back.2 = (bf16[2,320,1024]{2,1,0:T(8,128)(2,1)S(1)}, bf16[2,320,1024]{2,1,0:T(8,128)(2,1)S(1)}) custom-call(s32[28]{0:T(128)S(1)} %copy-done.29, bf16[640,1376]{1,0:T(8,128)(2,1)S(1)} %copy-done.12, bf16[640,1376]{1,0:T(8,128)(2,1)} %get-tuple-element.212.dup, bf16[1376,4096]{1,0:T(8,128)(2,1)} %bitcast.184, bf16[1376,4096]{1,0:T(8,128)(2,1)} %bitcast.189, ...), custom_call_target="tpu_custom_call" | custom-call | flops 7214202880 | bytes 26722304 | tf_op jit(solution)/shard_map/head_back/pallas_call | solution.py:46
  189.6 3.0 collective-permute-done.43
  195.0 7.4 %head_back.3 = (bf16[1,320,1024]{2,1,0:T(8,128)(2,1)S(1)}, bf16[1,320,1024]{2,1,0:T(8,128)(2,1)S(1)}) custom-call(s32[28]{0:T(128)S(1)} %copy-done.29, bf16[640,1376]{1,0:T(8,128)(2,1)S(1)} %copy-done.12, bf16[640,1376]{1,0:T(8,128)(2,1)S(1)} %copy-done.13, bf16[1376,4096]{1,0:T(8,128)(2,1)} %bitcast.185, bf16[1376,4096]{1,0:T(8,128)(2,1)} %bitcast.190, ...), custom_call_target="tpu_custom_call" | custom-call | flops 3607101440 | bytes 26722304 | tf_op jit(solution)/shard_map/head_back/pallas_call | solution.py:46
  202.4 8.0 %collective-permute-done.44 = bf16[2,160,1024]{2,1,0:T(8,128)(2,1)S(1)} collective-permute-done((bf16[2,160,1024]{2,1,0:T(8,128)(2,1)S(1)}, bf16[2,160,1024]{2,1,0:T(8,128)(2,1)S(1)}, u32[]{:S(2)}, u32[]{:S(2)}) %collective-permute-start.44) | collective-permute-done | bytes 655392 | tf_op jit(solution)/shard_map/ppermute | solution.py:65
  210.7 2.1 collective-permute-done.46
  216.9 3.8 %collective-permute-done.47 = bf16[80,1024]{1,0:T(8,128)(2,1)S(1)} collective-permute-done((bf16[80,1024]{1,0:T(8,128)(2,1)S(1)}, bf16[80,1024]{1,0:T(8,128)(2,1)S(1)}, u32[]{:S(2)}, u32[]{:S(2)}) %collective-permute-start.47) | collective-permute-done | bytes 163872 | tf_op jit(solution)/shard_map/ppermute | solution.py:71
  220.7 6.5 %collective-permute-done.48 = bf16[80,1024]{1,0:T(8,128)(2,1)S(1)} collective-permute-done((bf16[80,1024]{1,0:T(8,128)(2,1)S(1)}, bf16[80,1024]{1,0:T(8,128)(2,1)S(1)}, u32[]{:S(2)}, u32[]{:S(2)}) %collective-permute-start.48) | collective-permute-done | bytes 163872 | tf_op jit(solution)/shard_map/ppermute | solution.py:71
  227.2 4.2 %collective-permute-done.49 = bf16[80,1024]{1,0:T(8,128)(2,1)S(1)} collective-permute-done((bf16[80,1024]{1,0:T(8,128)(2,1)S(1)}, bf16[80,1024]{1,0:T(8,128)(2,1)S(1)}, u32[]{:S(2)}, u32[]{:S(2)}) %collective-permute-start.49) | collective-permute-done | bytes 163872 | tf_op jit(solution)/shard_map/ppermute | solution.py:71
  231.6 2.1 collective-permute-start.51
  235.1 3.6 %collective-permute-done.50 = bf16[80,1024]{1,0:T(8,128)(2,1)S(1)} collective-permute-done((bf16[80,1024]{1,0:T(8,128)(2,1)S(1)}, bf16[80,1024]{1,0:T(8,128)(2,1)S(1)}, u32[]{:S(2)}, u32[]{:S(2)}) %collective-permute-start.50) | collective-permute-done | bytes 163872 | tf_op jit(solution)/shard_map/ppermute | solution.py:71
  238.8 6.1 %collective-permute-done.51 = bf16[80,1024]{1,0:T(8,128)(2,1)S(1)} collective-permute-done((bf16[80,1024]{1,0:T(8,128)(2,1)S(1)}, bf16[80,1024]{1,0:T(8,128)(2,1)S(1)}, u32[]{:S(2)}, u32[]{:S(2)}) %collective-permute-start.51) | collective-permute-done | bytes 163872 | tf_op jit(solution)/shard_map/ppermute | solution.py:71
  244.9 3.6 %collective-permute-done.52 = bf16[80,1024]{1,0:T(8,128)(2,1)S(1)} collective-permute-done((bf16[80,1024]{1,0:T(8,128)(2,1)S(1)}, bf16[80,1024]{1,0:T(8,128)(2,1)S(1)}, u32[]{:S(2)}, u32[]{:S(2)}) %collective-permute-start.52) | collective-permute-done | bytes 163872 | tf_op jit(solution)/shard_map/ppermute | solution.py:71
  248.7 2.0 collective-permute-done.53
  250.7 2.8 trunk_hidden_grad.1
  256.1 5.1 %collective-permute-done.54 = bf16[80,1376]{1,0:T(8,128)(2,1)S(1)} collective-permute-done((bf16[80,1376]{1,0:T(8,128)(2,1)S(1)}, bf16[80,1376]{1,0:T(8,128)(2,1)S(1)}, u32[]{:S(2)}, u32[]{:S(2)}) %collective-permute-start.54) | collective-permute-done | bytes 220192 | tf_op jit(solution)/shard_map/ppermute | solution.py:65
  266.1 7.3 %collective-permute-done.56 = bf16[2,80,1376]{2,1,0:T(8,128)(2,1)S(1)} collective-permute-done((bf16[2,80,1376]{2,1,0:T(8,128)(2,1)S(1)}, bf16[2,80,1376]{2,1,0:T(8,128)(2,1)S(1)}, u32[]{:S(2)}, u32[]{:S(2)}) %collective-permute-start.56) | collective-permute-done | bytes 440352 | tf_op jit(solution)/shard_map/ppermute | solution.py:65
  276.6 4.9 %fusion.21 = f32[1376,1024]{1,0:T(8,128)} fusion(bf16[640,1376]{1,0:T(8,128)(2,1)S(1)} %bitcast.162, bf16[640,1024]{1,0:T(8,128)(2,1)S(1)} %constant_dynamic-update-slice_fusion.4.refs_0_.refs_1_.refs_2_.refs_3_), kind=kOutput, calls=%fused_computation.86 | convolution fusion | flops 1803550720 | bytes 8708096 | tf_op jit(solution)/shard_map/dot_general | solution.py:21
  281.5 3.7 %collective-permute-done.58 = bf16[2,80,1376]{2,1,0:T(8,128)(2,1)S(1)} collective-permute-done((bf16[2,80,1376]{2,1,0:T(8,128)(2,1)S(1)}, bf16[2,80,1376]{2,1,0:T(8,128)(2,1)S(1)}, u32[]{:S(2)}, u32[]{:S(2)}) %collective-permute-start.58) | collective-permute-done | bytes 440352 | tf_op jit(solution)/shard_map/ppermute | solution.py:65
  288.3 3.0 collective-permute-done.60.refs_6_
  293.1 8.5 %trunk_act.1 = (bf16[640,1376]{1,0:T(8,128)(2,1)S(1)}, bf16[640,1376]{1,0:T(8,128)(2,1)S(1)}, bf16[320,1024]{1,0:T(8,128)(2,1)S(1)}, bf16[320,1024]{1,0:T(8,128)(2,1)S(1)}) custom-call(s32[28]{0:T(128)S(1)} %copy-done.29, bf16[80,1376]{1,0:T(8,128)(2,1)S(1)} %get-tuple-element.293.refs_0_, bf16[80,1376]{1,0:T(8,128)(2,1)S(1)} %get-tuple-element.292.refs_1_, ...), custom_call_target="tpu_custom_call" | custom-call | flops 3607101440 | bytes 10919936 | tf_op jit(solution)/shard_map/trunk_act/pallas_call | solution.py:46
  301.6 2.1 collective-permute-done.62
  304.1 2.2 collective-permute-start.64
  307.6 7.3 %trunk_weight_grads.1 = (f32[1376,1024]{1,0:T(8,128)}, f32[1376,1024]{1,0:T(8,128)}) custom-call(s32[28]{0:T(128)S(1)} %copy-done.29, bf16[640,1376]{1,0:T(8,128)(2,1)S(1)} %get-tuple-element.243.dgate, bf16[640,1376]{1,0:T(8,128)(2,1)S(1)} %get-tuple-element.244.dup, bf16[640,1024]{1,0:T(8,128)(2,1)S(1)} %copy-done.24), custom_call_target="tpu_custom_call" | custom-call | flops 3607101440 | bytes 4833280 | tf_op jit(solution)/shard_map/trunk_weight_grads/pallas_call | solution.py:46
  314.9 3.1 collective-permute-done.64
  317.9 4.2 %collective-permute-done.65 = bf16[80,1024]{1,0:T(8,128)(2,1)S(1)} collective-permute-done((bf16[80,1024]{1,0:T(8,128)(2,1)S(1)}, bf16[80,1024]{1,0:T(8,128)(2,1)S(1)}, u32[]{:S(2)}, u32[]{:S(2)}) %collective-permute-start.65) | collective-permute-done | bytes 163872 | tf_op jit(solution)/shard_map/ppermute | solution.py:71
  (247 shorter events, 85.9 us)
Async XLA Ops:
  5.7 21.8 %collective-permute-start = (bf16[2,160,1376]{2,1,0:T(8,128)(2,1)S(1)}, bf16[2,160,1376]{2,1,0:T(8,128)(2,1)S(1)}, u32[]{:S(2)}, u32[]{:S(2)}) collective-permute-start(bf16[2,160,1376]{2,1,0:T(8,128)(2,1)S(1)} %bitcast.179), channel_id=1, source_target_pairs={{0,8},{8,0},{16,24},{24,16},{1,9},{9,1},{17,25},{25,17},{2,10},{10... | collective-permute-start | bytes 2641928 | tf_op jit(solution)/shard_map/ppermute | solution.py:65
  8.0 21.5 %collective-permute-start.1 = (bf16[2,160,1376]{2,1,0:T(8,128)(2,1)S(1)}, bf16[2,160,1376]{2,1,0:T(8,128)(2,1)S(1)}, u32[]{:S(2)}, u32[]{:S(2)}) collective-permute-start(bf16[2,160,1376]{2,1,0:T(8,128)(2,1)S(1)} %bitcast.180), channel_id=1, source_target_pairs={{0,16},{8,24},{16,0},{24,8},{1,17},{9,25},{17,1},{25,9},{2,18},{10... | collective-permute-start | bytes 2641928 | tf_op jit(solution)/shard_map/ppermute | solution.py:65
  9.8 32.7 %collective-permute-start.5 = (bf16[640,512]{1,0:T(8,128)(2,1)S(1)}, bf16[640,512]{1,0:T(8,128)(2,1)}, u32[]{:S(2)}, u32[]{:S(2)}) collective-permute-start(bf16[640,512]{1,0:T(8,128)(2,1)S(1)} %bitcast.170), channel_id=1, source_target_pairs={{0,2},{1,3},{2,0},{3,1},{4,6},{5,7},{6,4},{7,5},{8,10},{9,11},{10,... | collective-permute-start | bytes 1966088 | tf_op jit(solution)/shard_map/ppermute | solution.py:71
  11.4 31.1 %collective-permute-start.6 = (bf16[640,512]{1,0:T(8,128)(2,1)S(1)}, bf16[640,512]{1,0:T(8,128)(2,1)}, u32[]{:S(2)}, u32[]{:S(2)}) collective-permute-start(bf16[640,512]{1,0:T(8,128)(2,1)S(1)} %bitcast.171), channel_id=1, source_target_pairs={{0,4},{1,5},{2,6},{3,7},{4,0},{5,1},{6,2},{7,3},{8,12},{9,13},{10,... | collective-permute-start | bytes 1966088 | tf_op jit(solution)/shard_map/ppermute | solution.py:71
  29.8 11.1 %collective-permute-start.4 = (bf16[1,160,1376]{2,1,0:T(8,128)(2,1)S(1)}, bf16[1,160,1376]{2,1,0:T(8,128)(2,1)S(1)}, u32[]{:S(2)}, u32[]{:S(2)}) collective-permute-start(bf16[1,160,1376]{2,1,0:T(8,128)(2,1)S(1)} %slice.258), channel_id=1, source_target_pairs={{0,8},{8,0},{16,24},{24,16},{1,9},{9,1},{17,25},{25,17},{2,10},{10... | collective-permute-start | bytes 1320968 | tf_op jit(solution)/shard_map/ppermute | solution.py:65
  31.6 10.8 %collective-permute-start.3 = (bf16[1,160,1376]{2,1,0:T(8,128)(2,1)S(1)}, bf16[1,160,1376]{2,1,0:T(8,128)(2,1)S(1)}, u32[]{:S(2)}, u32[]{:S(2)}) collective-permute-start(bf16[1,160,1376]{2,1,0:T(8,128)(2,1)S(1)} %slice.259), channel_id=1, source_target_pairs={{0,16},{8,24},{16,0},{24,8},{1,17},{9,25},{17,1},{25,9},{2,18},{10... | collective-permute-start | bytes 1320968 | tf_op jit(solution)/shard_map/ppermute | solution.py:65
  42.8 10.5 %collective-permute-start.7 = (bf16[2,80,1376]{2,1,0:T(8,128)(2,1)S(1)}, bf16[2,80,1376]{2,1,0:T(8,128)(2,1)S(1)}, u32[]{:S(2)}, u32[]{:S(2)}) collective-permute-start(bf16[2,80,1376]{2,1,0:T(8,128)(2,1)S(1)} %bitcast.201), channel_id=1, source_target_pairs={{0,8},{8,0},{16,24},{24,16},{1,9},{9,1},{17,25},{25,17},{2,10},{10... | collective-permute-start | bytes 1320968 | tf_op jit(solution)/shard_map/ppermute | solution.py:65
  43.4 11.1 %collective-permute-start.8 = (bf16[2,80,1376]{2,1,0:T(8,128)(2,1)S(1)}, bf16[2,80,1376]{2,1,0:T(8,128)(2,1)S(1)}, u32[]{:S(2)}, u32[]{:S(2)}) collective-permute-start(bf16[2,80,1376]{2,1,0:T(8,128)(2,1)S(1)} %bitcast.202), channel_id=1, source_target_pairs={{0,16},{8,24},{16,0},{24,8},{1,17},{9,25},{17,1},{25,9},{2,18},{10... | collective-permute-start | bytes 1320968 | tf_op jit(solution)/shard_map/ppermute | solution.py:65
  44.9 11.6 %collective-permute-start.11 = (bf16[640,512]{1,0:T(8,128)(2,1)}, bf16[640,512]{1,0:T(8,128)(2,1)S(1)}, u32[]{:S(2)}, u32[]{:S(2)}) collective-permute-start(bf16[640,512]{1,0:T(8,128)(2,1)} %collective-permute-done.6.refs_0_), channel_id=1, source_target_pairs={{0,1},{1,0},{2,3},{3,2},{4,5},{5,4},{6,7},{7,6},{8,9},{9,8},{10,11... | collective-permute-start | bytes 1966088 | tf_op jit(solution)/shard_map/ppermute | solution.py:68
  44.9 17.9 %collective-permute-start.13 = (bf16[640,512]{1,0:T(8,128)(2,1)}, bf16[640,512]{1,0:T(8,128)(2,1)}, u32[]{:S(2)}, u32[]{:S(2)}) collective-permute-start(bf16[640,512]{1,0:T(8,128)(2,1)} %collective-permute-done.6.refs_0_), channel_id=1, source_target_pairs={{0,2},{1,3},{2,0},{3,1},{4,6},{5,7},{6,4},{7,5},{8,10},{9,11},{10,... | collective-permute-start | bytes 1966088 | tf_op jit(solution)/shard_map/ppermute | solution.py:71
  46.5 16.3 %collective-permute-start.12 = (bf16[640,512]{1,0:T(8,128)(2,1)}, bf16[640,512]{1,0:T(8,128)(2,1)S(1)}, u32[]{:S(2)}, u32[]{:S(2)}) collective-permute-start(bf16[640,512]{1,0:T(8,128)(2,1)} %collective-permute-done.5.refs_0_), channel_id=1, source_target_pairs={{0,1},{1,0},{2,3},{3,2},{4,5},{5,4},{6,7},{7,6},{8,9},{9,8},{10,11... | collective-permute-start | bytes 1966088 | tf_op jit(solution)/shard_map/ppermute | solution.py:68
  54.5 8.4 %collective-permute-start.10 = (bf16[80,1376]{1,0:T(8,128)(2,1)S(1)}, bf16[80,1376]{1,0:T(8,128)(2,1)S(1)}, u32[]{:S(2)}, u32[]{:S(2)}) collective-permute-start(bf16[80,1376]{1,0:T(8,128)(2,1)S(1)} %slice_bitcast_fusion.20), channel_id=1, source_target_pairs={{0,16},{8,24},{16,0},{24,8},{1,17},{9,25},{17,1},{25,9},{2,18},{10... | collective-permute-start | bytes 660488 | tf_op jit(solution)/shard_map/ppermute | solution.py:65
  55.1 7.8 %collective-permute-start.9 = (bf16[80,1376]{1,0:T(8,128)(2,1)S(1)}, bf16[80,1376]{1,0:T(8,128)(2,1)S(1)}, u32[]{:S(2)}, u32[]{:S(2)}) collective-permute-start(bf16[80,1376]{1,0:T(8,128)(2,1)S(1)} %slice_bitcast_fusion.21), channel_id=1, source_target_pairs={{0,8},{8,0},{16,24},{24,16},{1,9},{9,1},{17,25},{25,17},{2,10},{10... | collective-permute-start | bytes 660488 | tf_op jit(solution)/shard_map/ppermute | solution.py:65
  66.1 25.1 %collective-permute-start.19 = (bf16[2,160,1376]{2,1,0:T(8,128)(2,1)}, bf16[2,160,1376]{2,1,0:T(8,128)(2,1)}, u32[]{:S(2)}, u32[]{:S(2)}) collective-permute-start(bf16[2,160,1376]{2,1,0:T(8,128)(2,1)} %pad_maximum_fusion), channel_id=1, source_target_pairs={{0,8},{8,0},{16,24},{24,16},{1,9},{9,1},{17,25},{25,17},{2,10},{10... | collective-permute-start | bytes 2641928 | tf_op jit(solution)/shard_map/ppermute | solution.py:65
  67.1 24.1 %collective-permute-start.20 = (bf16[2,160,1376]{2,1,0:T(8,128)(2,1)}, bf16[2,160,1376]{2,1,0:T(8,128)(2,1)}, u32[]{:S(2)}, u32[]{:S(2)}) collective-permute-start(bf16[2,160,1376]{2,1,0:T(8,128)(2,1)} %pad_maximum_fusion), channel_id=1, source_target_pairs={{0,16},{8,24},{16,0},{24,8},{1,17},{9,25},{17,1},{25,9},{2,18},{10... | collective-permute-start | bytes 2641928 | tf_op jit(solution)/shard_map/ppermute | solution.py:65
  73.0 15.1 %collective-permute-start.16 = (bf16[80,1024]{1,0:T(8,128)(2,1)S(1)}, bf16[80,1024]{1,0:T(8,128)(2,1)S(1)}, u32[]{:S(2)}, u32[]{:S(2)}) collective-permute-start(bf16[80,1024]{1,0:T(8,128)(2,1)S(1)} %get-tuple-element.287), channel_id=1, source_target_pairs={{0,2},{1,3},{2,0},{3,1},{4,6},{5,7},{6,4},{7,5},{8,10},{9,11},{10,... | collective-permute-start | bytes 491528 | tf_op jit(solution)/shard_map/ppermute | solution.py:71
  75.5 12.6 %collective-permute-start.17 = (bf16[80,1024]{1,0:T(8,128)(2,1)S(1)}, bf16[80,1024]{1,0:T(8,128)(2,1)S(1)}, u32[]{:S(2)}, u32[]{:S(2)}) collective-permute-start(bf16[80,1024]{1,0:T(8,128)(2,1)S(1)} %get-tuple-element.286), channel_id=1, source_target_pairs={{0,4},{1,5},{2,6},{3,7},{4,0},{5,1},{6,2},{7,3},{8,12},{9,13},{10,... | collective-permute-start | bytes 491528 | tf_op jit(solution)/shard_map/ppermute | solution.py:71
  76.1 15.1 %collective-permute-start.18 = (bf16[80,1024]{1,0:T(8,128)(2,1)S(1)}, bf16[80,1024]{1,0:T(8,128)(2,1)S(1)}, u32[]{:S(2)}, u32[]{:S(2)}) collective-permute-start(bf16[80,1024]{1,0:T(8,128)(2,1)S(1)} %get-tuple-element.285), channel_id=1, source_target_pairs={{0,6},{1,7},{2,4},{3,5},{4,2},{5,3},{6,0},{7,1},{8,14},{9,15},{10,... | collective-permute-start | bytes 491528 | tf_op jit(solution)/shard_map/ppermute | solution.py:71
  92.7 12.6 %collective-permute-start.21 = (bf16[80,1024]{1,0:T(8,128)(2,1)S(1)}, bf16[80,1024]{1,0:T(8,128)(2,1)S(1)}, u32[]{:S(2)}, u32[]{:S(2)}) collective-permute-start(bf16[80,1024]{1,0:T(8,128)(2,1)S(1)} %fusion.12), channel_id=1, source_target_pairs={{0,4},{1,5},{2,6},{3,7},{4,0},{5,1},{6,2},{7,3},{8,12},{9,13},{10,... | collective-permute-start | bytes 491528 | tf_op jit(solution)/shard_map/ppermute | solution.py:71
  94.6 14.4 %collective-permute-start.22 = (bf16[80,1024]{1,0:T(8,128)(2,1)S(1)}, bf16[80,1024]{1,0:T(8,128)(2,1)S(1)}, u32[]{:S(2)}, u32[]{:S(2)}) collective-permute-start(bf16[80,1024]{1,0:T(8,128)(2,1)S(1)} %fusion.12), channel_id=1, source_target_pairs={{0,6},{1,7},{2,4},{3,5},{4,2},{5,3},{6,0},{7,1},{8,14},{9,15},{10,... | collective-permute-start | bytes 491528 | tf_op jit(solution)/shard_map/ppermute | solution.py:71
  99.5 9.5 %collective-permute-start.24 = (bf16[160,1024]{1,0:T(8,128)(2,1)S(1)}, bf16[160,1024]{1,0:T(8,128)(2,1)S(1)}, u32[]{:S(2)}, u32[]{:S(2)}) collective-permute-start(bf16[160,1024]{1,0:T(8,128)(2,1)S(1)} %constant_dynamic-update-slice_fusion.refs_0_), channel_id=1, source_target_pairs={{0,8},{8,0},{16,24},{24,16},{1,9},{9,1},{17,25},{25,17},{2,10},{10... | collective-permute-start | bytes 983048 | tf_op jit(solution)/shard_map/ppermute | solution.py:65
  100.6 8.4 %collective-permute-start.25 = (bf16[160,1024]{1,0:T(8,128)(2,1)S(1)}, bf16[160,1024]{1,0:T(8,128)(2,1)S(1)}, u32[]{:S(2)}, u32[]{:S(2)}) collective-permute-start(bf16[160,1024]{1,0:T(8,128)(2,1)S(1)} %constant_dynamic-update-slice_fusion.refs_0_), channel_id=1, source_target_pairs={{0,16},{8,24},{16,0},{24,8},{1,17},{9,25},{17,1},{25,9},{2,18},{10... | collective-permute-start | bytes 983048 | tf_op jit(solution)/shard_map/ppermute | solution.py:65
  102.1 12.1 %collective-permute-start.31 = (bf16[160,1024]{1,0:T(8,128)(2,1)S(1)}, bf16[160,1024]{1,0:T(8,128)(2,1)S(1)}, u32[]{:S(2)}, u32[]{:S(2)}) collective-permute-start(bf16[160,1024]{1,0:T(8,128)(2,1)S(1)} %constant_dynamic-update-slice_fusion.refs_0_), channel_id=1, source_target_pairs={{0,1},{1,0},{2,3},{3,2},{4,5},{5,4},{6,7},{7,6},{8,9},{9,8},{10,11... | collective-permute-start | bytes 983048 | tf_op jit(solution)/shard_map/ppermute | solution.py:68
  105.3 21.1 %collective-permute-start.28 = (bf16[160,1376]{1,0:T(8,128)(2,1)S(1)}, bf16[160,1376]{1,0:T(8,128)(2,1)S(1)}, u32[]{:S(2)}, u32[]{:S(2)}) collective-permute-start(bf16[160,1376]{1,0:T(8,128)(2,1)S(1)} %get-tuple-element.269.refs_10_), channel_id=1, source_target_pairs={{0,8},{8,0},{16,24},{24,16},{1,9},{9,1},{17,25},{25,17},{2,10},{10... | collective-permute-start | bytes 1320968 | tf_op jit(solution)/shard_map/ppermute | solution.py:65
  111.1 15.2 %collective-permute-start.29 = (bf16[160,1376]{1,0:T(8,128)(2,1)S(1)}, bf16[160,1376]{1,0:T(8,128)(2,1)S(1)}, u32[]{:S(2)}, u32[]{:S(2)}) collective-permute-start(bf16[160,1376]{1,0:T(8,128)(2,1)S(1)} %get-tuple-element.273.refs_13_), channel_id=1, source_target_pairs={{0,16},{8,24},{16,0},{24,8},{1,17},{9,25},{17,1},{25,9},{2,18},{10... | collective-permute-start | bytes 1320968 | tf_op jit(solution)/shard_map/ppermute | solution.py:65
  112.6 13.8 %collective-permute-start.26 = (bf16[160,1024]{1,0:T(8,128)(2,1)S(1)}, bf16[160,1024]{1,0:T(8,128)(2,1)S(1)}, u32[]{:S(2)}, u32[]{:S(2)}) collective-permute-start(bf16[160,1024]{1,0:T(8,128)(2,1)S(1)} %constant_dynamic-update-slice_fusion.2.refs_1_), channel_id=1, source_target_pairs={{0,8},{8,0},{16,24},{24,16},{1,9},{9,1},{17,25},{25,17},{2,10},{10... | collective-permute-start | bytes 983048 | tf_op jit(solution)/shard_map/ppermute | solution.py:65
  114.2 16.7 %collective-permute-start.27 = (bf16[160,1024]{1,0:T(8,128)(2,1)S(1)}, bf16[160,1024]{1,0:T(8,128)(2,1)S(1)}, u32[]{:S(2)}, u32[]{:S(2)}) collective-permute-start(bf16[160,1024]{1,0:T(8,128)(2,1)S(1)} %constant_dynamic-update-slice_fusion.2.refs_1_), channel_id=1, source_target_pairs={{0,16},{8,24},{16,0},{24,8},{1,17},{9,25},{17,1},{25,9},{2,18},{10... | collective-permute-start | bytes 983048 | tf_op jit(solution)/shard_map/ppermute | solution.py:65
  114.5 16.4 %collective-permute-start.30 = (bf16[160,1024]{1,0:T(8,128)(2,1)S(1)}, bf16[160,1024]{1,0:T(8,128)(2,1)S(1)}, u32[]{:S(2)}, u32[]{:S(2)}) collective-permute-start(bf16[160,1024]{1,0:T(8,128)(2,1)S(1)} %collective-permute-done.25.refs_0_), channel_id=1, source_target_pairs={{0,8},{8,0},{16,24},{24,16},{1,9},{9,1},{17,25},{25,17},{2,10},{10... | collective-permute-start | bytes 983048 | tf_op jit(solution)/shard_map/ppermute | solution.py:65
  131.5 14.1 %collective-permute-start.33 = (bf16[160,1024]{1,0:T(8,128)(2,1)S(1)}, bf16[160,1024]{1,0:T(8,128)(2,1)S(1)}, u32[]{:S(2)}, u32[]{:S(2)}) collective-permute-start(bf16[160,1024]{1,0:T(8,128)(2,1)S(1)} %collective-permute-done.26.refs_1_), channel_id=1, source_target_pairs={{0,16},{8,24},{16,0},{24,8},{1,17},{9,25},{17,1},{25,9},{2,18},{10... | collective-permute-start | bytes 983048 | tf_op jit(solution)/shard_map/ppermute | solution.py:65
  132.9 12.7 %collective-permute-start.34 = (bf16[160,1024]{1,0:T(8,128)(2,1)S(1)}, bf16[160,1024]{1,0:T(8,128)(2,1)S(1)}, u32[]{:S(2)}, u32[]{:S(2)}) collective-permute-start(bf16[160,1024]{1,0:T(8,128)(2,1)S(1)} %collective-permute-done.25.refs_0_), channel_id=1, source_target_pairs={{0,1},{1,0},{2,3},{3,2},{4,5},{5,4},{6,7},{7,6},{8,9},{9,8},{10,11... | collective-permute-start | bytes 983048 | tf_op jit(solution)/shard_map/ppermute | solution.py:68
  132.9 12.7 %collective-permute-start.35 = (bf16[160,1024]{1,0:T(8,128)(2,1)S(1)}, bf16[160,1024]{1,0:T(8,128)(2,1)S(1)}, u32[]{:S(2)}, u32[]{:S(2)}) collective-permute-start(bf16[160,1024]{1,0:T(8,128)(2,1)S(1)} %collective-permute-done.27.refs_1_), channel_id=1, source_target_pairs={{0,1},{1,0},{2,3},{3,2},{4,5},{5,4},{6,7},{7,6},{8,9},{9,8},{10,11... | collective-permute-start | bytes 983048 | tf_op jit(solution)/shard_map/ppermute | solution.py:68
  174.1 15.4 %collective-permute-start.41 = (bf16[160,1024]{1,0:T(8,128)(2,1)S(1)}, bf16[160,1024]{1,0:T(8,128)(2,1)S(1)}, u32[]{:S(2)}, u32[]{:S(2)}) collective-permute-start(bf16[160,1024]{1,0:T(8,128)(2,1)S(1)} %get-tuple-element.284), channel_id=1, source_target_pairs={{0,8},{8,0},{16,24},{24,16},{1,9},{9,1},{17,25},{25,17},{2,10},{10... | collective-permute-start | bytes 983048 | tf_op jit(solution)/shard_map/ppermute | solution.py:65
  175.7 13.7 %collective-permute-start.42 = (bf16[160,1024]{1,0:T(8,128)(2,1)S(1)}, bf16[160,1024]{1,0:T(8,128)(2,1)S(1)}, u32[]{:S(2)}, u32[]{:S(2)}) collective-permute-start(bf16[160,1024]{1,0:T(8,128)(2,1)S(1)} %get-tuple-element.283), channel_id=1, source_target_pairs={{0,16},{8,24},{16,0},{24,8},{1,17},{9,25},{17,1},{25,9},{2,18},{10... | collective-permute-start | bytes 983048 | tf_op jit(solution)/shard_map/ppermute | solution.py:65
  193.6 16.8 %collective-permute-start.44 = (bf16[2,160,1024]{2,1,0:T(8,128)(2,1)S(1)}, bf16[2,160,1024]{2,1,0:T(8,128)(2,1)S(1)}, u32[]{:S(2)}, u32[]{:S(2)}) collective-permute-start(bf16[2,160,1024]{2,1,0:T(8,128)(2,1)S(1)} %get-tuple-element.215), channel_id=1, source_target_pairs={{0,8},{8,0},{16,24},{24,16},{1,9},{9,1},{17,25},{25,17},{2,10},{10... | collective-permute-start | bytes 1966088 | tf_op jit(solution)/shard_map/ppermute | solution.py:65
  194.2 16.5 %collective-permute-start.45 = (bf16[2,160,1024]{2,1,0:T(8,128)(2,1)S(1)}, bf16[2,160,1024]{2,1,0:T(8,128)(2,1)S(1)}, u32[]{:S(2)}, u32[]{:S(2)}) collective-permute-start(bf16[2,160,1024]{2,1,0:T(8,128)(2,1)S(1)} %get-tuple-element.216), channel_id=1, source_target_pairs={{0,16},{8,24},{16,0},{24,8},{1,17},{9,25},{17,1},{25,9},{2,18},{10... | collective-permute-start | bytes 1966088 | tf_op jit(solution)/shard_map/ppermute | solution.py:65
  213.4 7.4 %collective-permute-start.47 = (bf16[80,1024]{1,0:T(8,128)(2,1)S(1)}, bf16[80,1024]{1,0:T(8,128)(2,1)S(1)}, u32[]{:S(2)}, u32[]{:S(2)}) collective-permute-start(bf16[80,1024]{1,0:T(8,128)(2,1)S(1)} %get-tuple-element.282), channel_id=1, source_target_pairs={{0,2},{1,3},{2,0},{3,1},{4,6},{5,7},{6,4},{7,5},{8,10},{9,11},{10,... | collective-permute-start | bytes 491528 | tf_op jit(solution)/shard_map/ppermute | solution.py:71
  214.5 12.7 %collective-permute-start.48 = (bf16[80,1024]{1,0:T(8,128)(2,1)S(1)}, bf16[80,1024]{1,0:T(8,128)(2,1)S(1)}, u32[]{:S(2)}, u32[]{:S(2)}) collective-permute-start(bf16[80,1024]{1,0:T(8,128)(2,1)S(1)} %get-tuple-element.281), channel_id=1, source_target_pairs={{0,4},{1,5},{2,6},{3,7},{4,0},{5,1},{6,2},{7,3},{8,12},{9,13},{10,... | collective-permute-start | bytes 491528 | tf_op jit(solution)/shard_map/ppermute | solution.py:71
  215.6 15.8 %collective-permute-start.49 = (bf16[80,1024]{1,0:T(8,128)(2,1)S(1)}, bf16[80,1024]{1,0:T(8,128)(2,1)S(1)}, u32[]{:S(2)}, u32[]{:S(2)}) collective-permute-start(bf16[80,1024]{1,0:T(8,128)(2,1)S(1)} %get-tuple-element.280), channel_id=1, source_target_pairs={{0,6},{1,7},{2,4},{3,5},{4,2},{5,3},{6,0},{7,1},{8,14},{9,15},{10,... | collective-permute-start | bytes 491528 | tf_op jit(solution)/shard_map/ppermute | solution.py:71
  231.6 13.3 %collective-permute-start.51 = (bf16[80,1024]{1,0:T(8,128)(2,1)S(1)}, bf16[80,1024]{1,0:T(8,128)(2,1)S(1)}, u32[]{:S(2)}, u32[]{:S(2)}) collective-permute-start(bf16[80,1024]{1,0:T(8,128)(2,1)S(1)} %get-tuple-element.255), channel_id=1, source_target_pairs={{0,4},{1,5},{2,6},{3,7},{4,0},{5,1},{6,2},{7,3},{8,12},{9,13},{10,... | collective-permute-start | bytes 491528 | tf_op jit(solution)/shard_map/ppermute | solution.py:71
  233.8 14.7 %collective-permute-start.52 = (bf16[80,1024]{1,0:T(8,128)(2,1)S(1)}, bf16[80,1024]{1,0:T(8,128)(2,1)S(1)}, u32[]{:S(2)}, u32[]{:S(2)}) collective-permute-start(bf16[80,1024]{1,0:T(8,128)(2,1)S(1)} %get-tuple-element.255), channel_id=1, source_target_pairs={{0,6},{1,7},{2,4},{3,5},{4,2},{5,3},{6,0},{7,1},{8,14},{9,15},{10,... | collective-permute-start | bytes 491528 | tf_op jit(solution)/shard_map/ppermute | solution.py:71
  253.6 7.6 %collective-permute-start.54 = (bf16[80,1376]{1,0:T(8,128)(2,1)S(1)}, bf16[80,1376]{1,0:T(8,128)(2,1)S(1)}, u32[]{:S(2)}, u32[]{:S(2)}) collective-permute-start(bf16[80,1376]{1,0:T(8,128)(2,1)S(1)} %get-tuple-element.295), channel_id=1, source_target_pairs={{0,16},{8,24},{16,0},{24,8},{1,17},{9,25},{17,1},{25,9},{2,18},{10... | collective-permute-start | bytes 660488 | tf_op jit(solution)/shard_map/ppermute | solution.py:65
  262.1 11.3 %collective-permute-start.56 = (bf16[2,80,1376]{2,1,0:T(8,128)(2,1)S(1)}, bf16[2,80,1376]{2,1,0:T(8,128)(2,1)S(1)}, u32[]{:S(2)}, u32[]{:S(2)}) collective-permute-start(bf16[2,80,1376]{2,1,0:T(8,128)(2,1)S(1)} %pad_maximum_fusion.4), channel_id=1, source_target_pairs={{0,8},{8,0},{16,24},{24,16},{1,9},{9,1},{17,25},{25,17},{2,10},{10... | collective-permute-start | bytes 1320968 | tf_op jit(solution)/shard_map/ppermute | solution.py:65
  263.7 11.0 %collective-permute-start.57 = (bf16[2,80,1376]{2,1,0:T(8,128)(2,1)S(1)}, bf16[2,80,1376]{2,1,0:T(8,128)(2,1)S(1)}, u32[]{:S(2)}, u32[]{:S(2)}) collective-permute-start(bf16[2,80,1376]{2,1,0:T(8,128)(2,1)S(1)} %pad_maximum_fusion.5), channel_id=1, source_target_pairs={{0,16},{8,24},{16,0},{24,8},{1,17},{9,25},{17,1},{25,9},{2,18},{10... | collective-permute-start | bytes 1320968 | tf_op jit(solution)/shard_map/ppermute | solution.py:65
  274.9 10.3 %collective-permute-start.58 = (bf16[2,80,1376]{2,1,0:T(8,128)(2,1)S(1)}, bf16[2,80,1376]{2,1,0:T(8,128)(2,1)S(1)}, u32[]{:S(2)}, u32[]{:S(2)}) collective-permute-start(bf16[2,80,1376]{2,1,0:T(8,128)(2,1)S(1)} %fusion.2), channel_id=1, source_target_pairs={{0,8},{8,0},{16,24},{24,16},{1,9},{9,1},{17,25},{25,17},{2,10},{10... | collective-permute-start | bytes 1320968 | tf_op jit(solution)/shard_map/ppermute | solution.py:65
  275.4 9.9 %collective-permute-start.59 = (bf16[2,80,1376]{2,1,0:T(8,128)(2,1)S(1)}, bf16[2,80,1376]{2,1,0:T(8,128)(2,1)S(1)}, u32[]{:S(2)}, u32[]{:S(2)}) collective-permute-start(bf16[2,80,1376]{2,1,0:T(8,128)(2,1)S(1)} %fusion.2), channel_id=1, source_target_pairs={{0,16},{8,24},{16,0},{24,8},{1,17},{9,25},{17,1},{25,9},{2,18},{10... | collective-permute-start | bytes 1320968 | tf_op jit(solution)/shard_map/ppermute | solution.py:65
  304.0 10.8 %collective-permute-start.63 = (bf16[80,1024]{1,0:T(8,128)(2,1)S(1)}, bf16[80,1024]{1,0:T(8,128)(2,1)S(1)}, u32[]{:S(2)}, u32[]{:S(2)}) collective-permute-start(bf16[80,1024]{1,0:T(8,128)(2,1)S(1)} %get-tuple-element.279), channel_id=1, source_target_pairs={{0,2},{1,3},{2,0},{3,1},{4,6},{5,7},{6,4},{7,5},{8,10},{9,11},{10,... | collective-permute-start | bytes 491528 | tf_op jit(solution)/shard_map/ppermute | solution.py:71
  304.1 13.8 %collective-permute-start.64 = (bf16[80,1024]{1,0:T(8,128)(2,1)S(1)}, bf16[80,1024]{1,0:T(8,128)(2,1)S(1)}, u32[]{:S(2)}, u32[]{:S(2)}) collective-permute-start(bf16[80,1024]{1,0:T(8,128)(2,1)S(1)} %get-tuple-element.278), channel_id=1, source_target_pairs={{0,4},{1,5},{2,6},{3,7},{4,0},{5,1},{6,2},{7,3},{8,12},{9,13},{10,... | collective-permute-start | bytes 491528 | tf_op jit(solution)/shard_map/ppermute | solution.py:71
  306.3 15.8 %collective-permute-start.65 = (bf16[80,1024]{1,0:T(8,128)(2,1)S(1)}, bf16[80,1024]{1,0:T(8,128)(2,1)S(1)}, u32[]{:S(2)}, u32[]{:S(2)}) collective-permute-start(bf16[80,1024]{1,0:T(8,128)(2,1)S(1)} %get-tuple-element.277), channel_id=1, source_target_pairs={{0,6},{1,7},{2,4},{3,5},{4,2},{5,3},{6,0},{7,1},{8,14},{9,15},{10,... | collective-permute-start | bytes 491528 | tf_op jit(solution)/shard_map/ppermute | solution.py:71
  (62 other events, 549.6 us)

commit v5 on v4

--- a/solution.py
+++ b/solution.py
@@ -326,12 +326,17 @@
     own[0] = jnp.concatenate([first, product[mine:half]], 0).astype(BF)
 
 
+def gradients(gate, up, hidden):
+    sig = jax.nn.sigmoid(gate)
+    act = gate * sig
+    return (hidden * up * (sig + act * (1.0 - sig))).astype(BF), (hidden * act).astype(BF)
+
+
 def act_kernel(counts, places, blocks_at, index, *refs):
     n = sum(counts)
     parts, (gate_w, up_w, pre, lin, ghid, cot, dgate, dup, own, mate) = refs[:n], refs[n : n + 10]
-    pre_held, lin_held, ghid_held, sems = refs[n + 10 :]
+    gate_sum, up_sum, pre_held, lin_held, ghid_held, sems = refs[n + 10 :]
     half = own.shape[1]
-    held = (pre_held, lin_held)
     copies = [pltpu.make_async_copy(pre, pre_held, sems.at[0]), pltpu.make_async_copy(lin, lin_held, sems.at[1])]
     rows_each = half // places
     for block in range(2 * places):
@@ -344,24 +349,23 @@
             if j == 0:
                 for copy in copies:
                     copy.start()
-            last = j == len(counts) - 1
             begin = sum(counts[:j])
             value = jnp.concatenate([part[...] for part in parts[begin : begin + count]], 0)
-            products = [dot_nt(value, gate_w[...]), dot_nt(value, up_w[...])]
-            if j == 0:
+            for sums, weight in ((gate_sum, gate_w), (up_sum, up_w)):
+                if j == 0:
+                    sums[...] = dot_nt(value, weight[...])
+                else:
+                    sums[...] += dot_nt(value, weight[...])
+            if j == len(counts) - 1:
                 for copy in copies:
                     copy.wait()
-            if not last:
-                for sums, product in zip(held, products):
-                    sums[...] += product
-            else:
-                for side in range(2):
-                    rows = slice(side * half, side * half + half)
-                    gate = pre_held[rows] + products[0][rows]
-                    up = lin_held[rows] + products[1][rows]
-                    h, sig = ghid_held[rows], jax.nn.sigmoid(gate)
-                    dgate[rows] = (h * up * (sig * (1.0 + gate * (1.0 - sig)))).astype(BF)
-                    dup[rows] = (h * (gate * sig)).astype(BF)
+
+                @pl.loop(0, 2 * half // 16)
+                def _(step):
+                    rows = pl.ds(pl.multiple_of(step * 16, 16), 16)
+                    gate, up = gate_sum[rows] + pre_held[rows], up_sum[rows] + lin_held[rows]
+                    dgate[rows], dup[rows] = gradients(gate, up, ghid_held[rows])
+
                 product = dot_nn(dgate[...], gate_w[...]) + dot_nn(dup[...], up_w[...])
                 back_rows(product, cot, own, mate)
 
@@ -388,7 +392,7 @@
         [*flat, gate_t, up_t, pre, lin, ghid.reshape(2 * places, half // places, units), cot],
         4 * rows * depth * units * (len(pieces) + 1),
         60,
-        [pltpu.VMEM((rows, units), F32)] * 3 + [pltpu.SemaphoreType.DMA((2 + 2 * places,))],
+        [pltpu.VMEM((rows, units), F32)] * 5 + [pltpu.SemaphoreType.DMA((2 + 2 * places,))],
     )
 
 
@@ -401,13 +405,14 @@
     rows, units = dgate.shape
     depth = gate_t.shape[1] // groups
     half = rows // 2
-    weight = pl.BlockSpec((units, depth), lambda i, index: (0, index[offset + i]))
-    cot_spec = pl.BlockSpec((cot.shape[0], depth), lambda i, index: (0, index[offset + i]))
-    out = pl.BlockSpec((1, half, depth), lambda i, index: (i, 0, 0))
+    cut = 2
+    weight = pl.BlockSpec((units, depth // cut), lambda i, j, index: (0, index[offset + i] * cut + j))
+    cot_spec = pl.BlockSpec((cot.shape[0], depth // cut), lambda i, j, index: (0, index[offset + i] * cut + j))
+    out = pl.BlockSpec((1, half, depth // cut), lambda i, j, index: (i, 0, j))
     return call(
         back_kernel,
         "head_back",
-        (count,),
+        (count, cut),
         index,
         [whole((rows, units))] * 2 + [weight] * 2 + [cot_spec],
         [out] * 2,
@@ -423,12 +428,19 @@
     gate_w, up_w, dgate, dup, own, mate = refs[4 * groups :]
     for k in range(groups):
         share = gates[k].shape[0]
-        ghid = jnp.concatenate([ghids[2 * k][...], ghids[2 * k + 1][...]], 0).astype(F32)
-        gate, up = gates[k][...].astype(F32), ups[k][...].astype(F32)
-        sig = jax.nn.sigmoid(gate)
-        rows = pl.ds(pl.multiple_of(index[k] * share, share), share)
-        dgate[rows] = (ghid * up * (sig * (1.0 + gate * (1.0 - sig)))).astype(BF)
-        dup[rows] = (ghid * (gate * sig)).astype(BF)
+        for side in range(2):
+            part = share // 2
+            tile = 16 if part % 16 == 0 else part
+
+            @pl.loop(0, part // tile)
+            def _(step, k=k, side=side, part=part, tile=tile):
+                at = pl.multiple_of(step * tile, tile)
+                ghid = ghids[2 * k + side][pl.ds(at, tile)].astype(F32)
+                rows = pl.ds(pl.multiple_of(side * part + at, tile), tile)
+                gate, up = gates[k][rows].astype(F32), ups[k][rows].astype(F32)
+                rows = pl.ds(pl.multiple_of(index[k] * share + side * part + at, tile), tile)
+                dgate[rows], dup[rows] = gradients(gate, up, ghid)
+
     half = own.shape[0]
     for side, out in enumerate((own, mate)):
         rows = slice(side * half, side * half + half)

time: 326 us -> 325 us (level)
  no operation moved by 1% of the time
where the time goes in v5:
time: 325 us; the launch traced here: 321 us
  waiting for transfers between devices  117 us (36%)
  Pallas kernels  115 us (35%)
  starting transfers between devices  59.8 us (18%)
  local copies, waits for them, and re-layouts  15.5 us (5%)
  other arithmetic  7.28 us (2%)
  matrix products  4.91 us (2%)
    pallas_call x19, Pallas kernels, call(): pl.pallas_call(kernel, grid_spec=pltpu.PrefetchScalarGridSpec(num_scalar_...  115 us
    ppermute x30, waiting for transfers between devices, group_swap(): lax.ppermute(value, 'group', [(i, i ^ mask) for i in range(self.groups)])  60.1 us
    ppermute x18, waiting for transfers between devices, place_swap(): lax.ppermute(value, 'mp', [(i, i ^ 2 * mask) for i in range(self.members)])  44.1 us
    ppermute x30, starting transfers between devices, group_swap(): lax.ppermute(value, 'group', [(i, i ^ mask) for i in range(self.groups)])  35 us
    ppermute x18, starting transfers between devices, place_swap(): lax.ppermute(value, 'mp', [(i, i ^ 2 * mask) for i in range(self.members)])  21.8 us
    ppermute x18, waiting for transfers between devices, core_swap(): return lax.ppermute(value, 'mp', [(i, i ^ 1) for i in range(self.members)])  13 us
    unnamed x93, local copies, waits for them, and re-layouts  9.92 us
  transfers between devices with their start and end apart: 66, of which 35 were waited for; matrix products, arithmetic and copies ran while one was open for 4% of the time, Pallas kernels for 25%

profile of v5, /device:TPU:18, one launch (start us, length us, event | category | flops | bytes accessed | tf_op | source)
XLA Modules:
  0.0 321.3 jit_solution(5798177342198998690)
XLA Ops:
  17.1 4.4 %head_hidden_grad.3.refs_3_ = f32[640,1376]{1,0:T(8,128)S(1)} custom-call(s32[28]{0:T(128)S(1)} %stack.137.index, bf16[640,512]{1,0:T(8,128)(2,1)S(1)} %bitcast.172, bf16[640,512]{1,0:T(8,128)(2,1)S(1)} %collective-permute-done.2.refs_1_, bf16[1376,4096]{1,0:T(8,128)(2,1)} %bitcast.191), custom_call_target="tpu_custom_call" | custom-call | flops 1803550720 | bytes 12582912 | tf_op jit(solution)/shard_map/head_hidden_grad/pallas_call | solution.py:46
  21.5 5.9 %collective-permute-done = bf16[2,160,1376]{2,1,0:T(8,128)(2,1)S(1)} collective-permute-done((bf16[2,160,1376]{2,1,0:T(8,128)(2,1)S(1)}, bf16[2,160,1376]{2,1,0:T(8,128)(2,1)S(1)}, u32[]{:S(2)}, u32[]{:S(2)}) %collective-permute-start) | collective-permute-done | bytes 880672 | tf_op jit(solution)/shard_map/ppermute | solution.py:65
  27.5 2.1 collective-permute-done.1
  33.2 7.7 %collective-permute-done.4 = bf16[1,160,1376]{2,1,0:T(8,128)(2,1)S(1)} collective-permute-done((bf16[1,160,1376]{2,1,0:T(8,128)(2,1)S(1)}, bf16[1,160,1376]{2,1,0:T(8,128)(2,1)S(1)}, u32[]{:S(2)}, u32[]{:S(2)}) %collective-permute-start.4) | collective-permute-done | bytes 440352 | tf_op jit(solution)/shard_map/ppermute | solution.py:65
  47.7 5.5 %collective-permute-done.7 = bf16[2,80,1376]{2,1,0:T(8,128)(2,1)S(1)} collective-permute-done((bf16[2,80,1376]{2,1,0:T(8,128)(2,1)S(1)}, bf16[2,80,1376]{2,1,0:T(8,128)(2,1)S(1)}, u32[]{:S(2)}, u32[]{:S(2)}) %collective-permute-start.7) | collective-permute-done | bytes 440352 | tf_op jit(solution)/shard_map/ppermute | solution.py:65
  56.5 6.2 %head_hidden_grad.4.refs_5_ = f32[640,1376]{1,0:T(8,128)S(1)} custom-call(s32[28]{0:T(128)S(1)} %stack.137.index, bf16[640,512]{1,0:T(8,128)(2,1)} %collective-permute-done.6.refs_0_, bf16[640,512]{1,0:T(8,128)(2,1)S(1)} %collective-permute-done.11.refs_1_, bf16[1376,4096]{1,0:T(8,128)(2,1)} %bitcast.192, f32[640,1376]{1,0:T(8,128)} %copy-done.5), custom_call_target="tpu_custom_call" | custom-call | flops 1803550720 | bytes 16105472 | tf_op jit(solution)/shard_map/head_hidden_grad/pallas_call | solution.py:46
  62.9 2.6 trunk_down.2
  70.1 2.8 trunk_down.3
  73.0 2.5 collective-permute-start.16
  77.1 10.8 %head_hidden_grad.5 = f32[640,1376]{1,0:T(8,128)} custom-call(s32[28]{0:T(128)S(1)} %stack.137.index, bf16[640,512]{1,0:T(8,128)(2,1)} %collective-permute-done.5.refs_0_, bf16[640,512]{1,0:T(8,128)(2,1)S(1)} %copy-done.22, bf16[640,512]{1,0:T(8,128)(2,1)} %collective-permute-done.13.refs_2_, bf16[640,512]{1,0:T(8,128)(2,1)} %collective-permute-done.15.refs_3_, ...), custom_call_target="tpu_custom_call" | custom-call | flops 3607101440 | bytes 17416192 | tf_op jit(solution)/shard_map/head_hidden_grad/pallas_call | solution.py:46
  87.9 3.4 %collective-permute-done.18 = bf16[80,1024]{1,0:T(8,128)(2,1)S(1)} collective-permute-done((bf16[80,1024]{1,0:T(8,128)(2,1)S(1)}, bf16[80,1024]{1,0:T(8,128)(2,1)S(1)}, u32[]{:S(2)}, u32[]{:S(2)}) %collective-permute-start.18) | collective-permute-done | bytes 163872 | tf_op jit(solution)/shard_map/ppermute | solution.py:71
  92.7 2.0 collective-permute-start.21
  95.8 2.2 head_output_grad_rows.1.refs_13_.cot
  103.3 1.9 collective-permute-done.21
  106.7 2.3 collective-permute-done.22
  109.1 2.0 slice_bitcast_fusion.4
  115.2 9.3 %head_pre.2 = (f32[640,1376]{1,0:T(8,128)S(1)}, f32[640,1376]{1,0:T(8,128)}) custom-call(s32[28]{0:T(128)S(1)} %stack.137.index, bf16[160,1024]{1,0:T(8,128)(2,1)S(1)} %constant_dynamic-update-slice_fusion.refs_0_, bf16[160,1024]{1,0:T(8,128)(2,1)S(1)} %constant_dynamic-update-slice_fusion.2.refs_1_, bf16[160,1024]{1,0:T(8,128)(2,1)S(1)} %collective-permute-done.31.refs_2_, ...), custom_call_target="tpu_custom_call" | custom-call | flops 3607101440 | bytes 23855104 | tf_op jit(solution)/shard_map/head_pre/pallas_call | solution.py:46
  124.5 1.8 copy-done.16
  126.3 4.6 %collective-permute-done.27.refs_1_ = bf16[160,1024]{1,0:T(8,128)(2,1)S(1)} collective-permute-done((bf16[160,1024]{1,0:T(8,128)(2,1)S(1)}, bf16[160,1024]{1,0:T(8,128)(2,1)S(1)}, u32[]{:S(2)}, u32[]{:S(2)}) %collective-permute-start.27) | collective-permute-done | bytes 327712 | tf_op jit(solution)/shard_map/ppermute | solution.py:65
  133.4 10.3 %head_pre.3 = (f32[640,1376]{1,0:T(8,128)S(1)}, f32[640,1376]{1,0:T(8,128)}) custom-call(s32[28]{0:T(128)S(1)} %stack.137.index, bf16[160,1024]{1,0:T(8,128)(2,1)S(1)} %collective-permute-done.24.refs_0_, bf16[160,1024]{1,0:T(8,128)(2,1)S(1)} %collective-permute-done.26.refs_1_, bf16[160,1024]{1,0:T(8,128)(2,1)S(1)} %collective-permute-done.36.refs_2_, ...), custom_call_target="tpu_custom_call" | custom-call | flops 3607101440 | bytes 30900224 | tf_op jit(solution)/shard_map/head_pre/pallas_call | solution.py:46
  143.8 1.8 copy-done.30
  148.8 21.3 %head_act.1 = (bf16[640,1376]{1,0:T(8,128)(2,1)}, bf16[640,1376]{1,0:T(8,128)(2,1)}, bf16[1,320,1024]{2,1,0:T(8,128)(2,1)}, bf16[1,320,1024]{2,1,0:T(8,128)(2,1)}) custom-call(s32[28]{0:T(128)} %copy-done.28, bf16[160,1024]{1,0:T(8,128)(2,1)} %copy-done.36, bf16[160,1024]{1,0:T(8,128)(2,1)} %copy-done.37, bf16[160,1024]{1,0:T(8,128)(2,1)} %copy-done.40, ...), custom_call_target="tpu_custom_call" | custom-call | flops 10821304320 | bytes 36388864 | tf_op jit(solution)/shard_map/head_act/pallas_call | solution.py:46
  170.3 2.2 collective-permute-done.40
  176.6 12.5 %head_back.2 = (bf16[2,320,1024]{2,1,0:T(8,128)(2,1)S(1)}, bf16[2,320,1024]{2,1,0:T(8,128)(2,1)S(1)}) custom-call(s32[28]{0:T(128)S(1)} %copy-done.29, bf16[640,1376]{1,0:T(8,128)(2,1)S(1)} %copy-done.12, bf16[640,1376]{1,0:T(8,128)(2,1)} %get-tuple-element.212.dup, bf16[1376,4096]{1,0:T(8,128)(2,1)} %bitcast.184, bf16[1376,4096]{1,0:T(8,128)(2,1)} %bitcast.189, ...), custom_call_target="tpu_custom_call" | custom-call | flops 7214202880 | bytes 26722304 | tf_op jit(solution)/shard_map/head_back/pallas_call | solution.py:46
  189.2 3.0 collective-permute-done.43
  194.8 6.9 %head_back.3 = (bf16[1,320,1024]{2,1,0:T(8,128)(2,1)S(1)}, bf16[1,320,1024]{2,1,0:T(8,128)(2,1)S(1)}) custom-call(s32[28]{0:T(128)S(1)} %copy-done.29, bf16[640,1376]{1,0:T(8,128)(2,1)S(1)} %copy-done.12, bf16[640,1376]{1,0:T(8,128)(2,1)S(1)} %copy-done.13, bf16[1376,4096]{1,0:T(8,128)(2,1)} %bitcast.185, bf16[1376,4096]{1,0:T(8,128)(2,1)} %bitcast.190, ...), custom_call_target="tpu_custom_call" | custom-call | flops 3607101440 | bytes 26722304 | tf_op jit(solution)/shard_map/head_back/pallas_call | solution.py:46
  201.7 8.5 %collective-permute-done.44 = bf16[2,160,1024]{2,1,0:T(8,128)(2,1)S(1)} collective-permute-done((bf16[2,160,1024]{2,1,0:T(8,128)(2,1)S(1)}, bf16[2,160,1024]{2,1,0:T(8,128)(2,1)S(1)}, u32[]{:S(2)}, u32[]{:S(2)}) %collective-permute-start.44) | collective-permute-done | bytes 655392 | tf_op jit(solution)/shard_map/ppermute | solution.py:65
  210.3 2.1 collective-permute-done.46
  216.5 3.9 %collective-permute-done.47 = bf16[80,1024]{1,0:T(8,128)(2,1)S(1)} collective-permute-done((bf16[80,1024]{1,0:T(8,128)(2,1)S(1)}, bf16[80,1024]{1,0:T(8,128)(2,1)S(1)}, u32[]{:S(2)}, u32[]{:S(2)}) %collective-permute-start.47) | collective-permute-done | bytes 163872 | tf_op jit(solution)/shard_map/ppermute | solution.py:71
  220.4 6.4 %collective-permute-done.48 = bf16[80,1024]{1,0:T(8,128)(2,1)S(1)} collective-permute-done((bf16[80,1024]{1,0:T(8,128)(2,1)S(1)}, bf16[80,1024]{1,0:T(8,128)(2,1)S(1)}, u32[]{:S(2)}, u32[]{:S(2)}) %collective-permute-start.48) | collective-permute-done | bytes 163872 | tf_op jit(solution)/shard_map/ppermute | solution.py:71
  226.9 4.2 %collective-permute-done.49 = bf16[80,1024]{1,0:T(8,128)(2,1)S(1)} collective-permute-done((bf16[80,1024]{1,0:T(8,128)(2,1)S(1)}, bf16[80,1024]{1,0:T(8,128)(2,1)S(1)}, u32[]{:S(2)}, u32[]{:S(2)}) %collective-permute-start.49) | collective-permute-done | bytes 163872 | tf_op jit(solution)/shard_map/ppermute | solution.py:71
  231.2 2.2 collective-permute-start.51
  234.7 3.6 %collective-permute-done.50 = bf16[80,1024]{1,0:T(8,128)(2,1)S(1)} collective-permute-done((bf16[80,1024]{1,0:T(8,128)(2,1)S(1)}, bf16[80,1024]{1,0:T(8,128)(2,1)S(1)}, u32[]{:S(2)}, u32[]{:S(2)}) %collective-permute-start.50) | collective-permute-done | bytes 163872 | tf_op jit(solution)/shard_map/ppermute | solution.py:71
  238.4 6.1 %collective-permute-done.51 = bf16[80,1024]{1,0:T(8,128)(2,1)S(1)} collective-permute-done((bf16[80,1024]{1,0:T(8,128)(2,1)S(1)}, bf16[80,1024]{1,0:T(8,128)(2,1)S(1)}, u32[]{:S(2)}, u32[]{:S(2)}) %collective-permute-start.51) | collective-permute-done | bytes 163872 | tf_op jit(solution)/shard_map/ppermute | solution.py:71
  244.5 3.6 %collective-permute-done.52 = bf16[80,1024]{1,0:T(8,128)(2,1)S(1)} collective-permute-done((bf16[80,1024]{1,0:T(8,128)(2,1)S(1)}, bf16[80,1024]{1,0:T(8,128)(2,1)S(1)}, u32[]{:S(2)}, u32[]{:S(2)}) %collective-permute-start.52) | collective-permute-done | bytes 163872 | tf_op jit(solution)/shard_map/ppermute | solution.py:71
  248.3 2.0 collective-permute-done.53
  250.3 2.8 trunk_hidden_grad.1
  255.9 5.0 %collective-permute-done.54 = bf16[80,1376]{1,0:T(8,128)(2,1)S(1)} collective-permute-done((bf16[80,1376]{1,0:T(8,128)(2,1)S(1)}, bf16[80,1376]{1,0:T(8,128)(2,1)S(1)}, u32[]{:S(2)}, u32[]{:S(2)}) %collective-permute-start.54) | collective-permute-done | bytes 220192 | tf_op jit(solution)/shard_map/ppermute | solution.py:65
  265.8 7.4 %collective-permute-done.56 = bf16[2,80,1376]{2,1,0:T(8,128)(2,1)S(1)} collective-permute-done((bf16[2,80,1376]{2,1,0:T(8,128)(2,1)S(1)}, bf16[2,80,1376]{2,1,0:T(8,128)(2,1)S(1)}, u32[]{:S(2)}, u32[]{:S(2)}) %collective-permute-start.56) | collective-permute-done | bytes 440352 | tf_op jit(solution)/shard_map/ppermute | solution.py:65
  276.2 4.9 %fusion.21 = f32[1376,1024]{1,0:T(8,128)} fusion(bf16[640,1376]{1,0:T(8,128)(2,1)S(1)} %bitcast.162, bf16[640,1024]{1,0:T(8,128)(2,1)S(1)} %constant_dynamic-update-slice_fusion.4.refs_0_.refs_1_.refs_2_.refs_3_), kind=kOutput, calls=%fused_computation.86 | convolution fusion | flops 1803550720 | bytes 8708096 | tf_op jit(solution)/shard_map/dot_general | solution.py:21
  281.1 3.8 %collective-permute-done.58 = bf16[2,80,1376]{2,1,0:T(8,128)(2,1)S(1)} collective-permute-done((bf16[2,80,1376]{2,1,0:T(8,128)(2,1)S(1)}, bf16[2,80,1376]{2,1,0:T(8,128)(2,1)S(1)}, u32[]{:S(2)}, u32[]{:S(2)}) %collective-permute-start.58) | collective-permute-done | bytes 440352 | tf_op jit(solution)/shard_map/ppermute | solution.py:65
  287.9 3.2 collective-permute-done.60.refs_6_
  292.8 6.9 %trunk_act.1 = (bf16[640,1376]{1,0:T(8,128)(2,1)S(1)}, bf16[640,1376]{1,0:T(8,128)(2,1)S(1)}, bf16[320,1024]{1,0:T(8,128)(2,1)S(1)}, bf16[320,1024]{1,0:T(8,128)(2,1)S(1)}) custom-call(s32[28]{0:T(128)S(1)} %copy-done.29, bf16[80,1376]{1,0:T(8,128)(2,1)S(1)} %get-tuple-element.293.refs_0_, bf16[80,1376]{1,0:T(8,128)(2,1)S(1)} %get-tuple-element.292.refs_1_, ...), custom_call_target="tpu_custom_call" | custom-call | flops 3607101440 | bytes 10919936 | tf_op jit(solution)/shard_map/trunk_act/pallas_call | solution.py:46
  299.8 2.1 collective-permute-done.62
  302.3 2.2 collective-permute-start.64
  305.8 7.3 %trunk_weight_grads.1 = (f32[1376,1024]{1,0:T(8,128)}, f32[1376,1024]{1,0:T(8,128)}) custom-call(s32[28]{0:T(128)S(1)} %copy-done.29, bf16[640,1376]{1,0:T(8,128)(2,1)S(1)} %get-tuple-element.243.dgate, bf16[640,1376]{1,0:T(8,128)(2,1)S(1)} %get-tuple-element.244.dup, bf16[640,1024]{1,0:T(8,128)(2,1)S(1)} %copy-done.24), custom_call_target="tpu_custom_call" | custom-call | flops 3607101440 | bytes 4833280 | tf_op jit(solution)/shard_map/trunk_weight_grads/pallas_call | solution.py:46
  313.0 3.1 collective-permute-done.64
  316.1 4.2 %collective-permute-done.65 = bf16[80,1024]{1,0:T(8,128)(2,1)S(1)} collective-permute-done((bf16[80,1024]{1,0:T(8,128)(2,1)S(1)}, bf16[80,1024]{1,0:T(8,128)(2,1)S(1)}, u32[]{:S(2)}, u32[]{:S(2)}) %collective-permute-start.65) | collective-permute-done | bytes 163872 | tf_op jit(solution)/shard_map/ppermute | solution.py:71
  (247 shorter events, 86.1 us)
Async XLA Ops:
  5.7 21.8 %collective-permute-start = (bf16[2,160,1376]{2,1,0:T(8,128)(2,1)S(1)}, bf16[2,160,1376]{2,1,0:T(8,128)(2,1)S(1)}, u32[]{:S(2)}, u32[]{:S(2)}) collective-permute-start(bf16[2,160,1376]{2,1,0:T(8,128)(2,1)S(1)} %bitcast.179), channel_id=1, source_target_pairs={{0,8},{8,0},{16,24},{24,16},{1,9},{9,1},{17,25},{25,17},{2,10},{10... | collective-permute-start | bytes 2641928 | tf_op jit(solution)/shard_map/ppermute | solution.py:65
  8.0 21.5 %collective-permute-start.1 = (bf16[2,160,1376]{2,1,0:T(8,128)(2,1)S(1)}, bf16[2,160,1376]{2,1,0:T(8,128)(2,1)S(1)}, u32[]{:S(2)}, u32[]{:S(2)}) collective-permute-start(bf16[2,160,1376]{2,1,0:T(8,128)(2,1)S(1)} %bitcast.180), channel_id=1, source_target_pairs={{0,16},{8,24},{16,0},{24,8},{1,17},{9,25},{17,1},{25,9},{2,18},{10... | collective-permute-start | bytes 2641928 | tf_op jit(solution)/shard_map/ppermute | solution.py:65
  9.7 7.4 %collective-permute-start.2 = (bf16[640,512]{1,0:T(8,128)(2,1)S(1)}, bf16[640,512]{1,0:T(8,128)(2,1)S(1)}, u32[]{:S(2)}, u32[]{:S(2)}) collective-permute-start(bf16[640,512]{1,0:T(8,128)(2,1)S(1)} %bitcast.169), channel_id=1, source_target_pairs={{0,1},{1,0},{2,3},{3,2},{4,5},{5,4},{6,7},{7,6},{8,9},{9,8},{10,11... | collective-permute-start | bytes 1966088 | tf_op jit(solution)/shard_map/ppermute | solution.py:68
  9.8 32.7 %collective-permute-start.5 = (bf16[640,512]{1,0:T(8,128)(2,1)S(1)}, bf16[640,512]{1,0:T(8,128)(2,1)}, u32[]{:S(2)}, u32[]{:S(2)}) collective-permute-start(bf16[640,512]{1,0:T(8,128)(2,1)S(1)} %bitcast.170), channel_id=1, source_target_pairs={{0,2},{1,3},{2,0},{3,1},{4,6},{5,7},{6,4},{7,5},{8,10},{9,11},{10,... | collective-permute-start | bytes 1966088 | tf_op jit(solution)/shard_map/ppermute | solution.py:71
  11.4 31.1 %collective-permute-start.6 = (bf16[640,512]{1,0:T(8,128)(2,1)S(1)}, bf16[640,512]{1,0:T(8,128)(2,1)}, u32[]{:S(2)}, u32[]{:S(2)}) collective-permute-start(bf16[640,512]{1,0:T(8,128)(2,1)S(1)} %bitcast.171), channel_id=1, source_target_pairs={{0,4},{1,5},{2,6},{3,7},{4,0},{5,1},{6,2},{7,3},{8,12},{9,13},{10,... | collective-permute-start | bytes 1966088 | tf_op jit(solution)/shard_map/ppermute | solution.py:71
  29.8 11.1 %collective-permute-start.4 = (bf16[1,160,1376]{2,1,0:T(8,128)(2,1)S(1)}, bf16[1,160,1376]{2,1,0:T(8,128)(2,1)S(1)}, u32[]{:S(2)}, u32[]{:S(2)}) collective-permute-start(bf16[1,160,1376]{2,1,0:T(8,128)(2,1)S(1)} %slice.258), channel_id=1, source_target_pairs={{0,8},{8,0},{16,24},{24,16},{1,9},{9,1},{17,25},{25,17},{2,10},{10... | collective-permute-start | bytes 1320968 | tf_op jit(solution)/shard_map/ppermute | solution.py:65
  31.6 10.8 %collective-permute-start.3 = (bf16[1,160,1376]{2,1,0:T(8,128)(2,1)S(1)}, bf16[1,160,1376]{2,1,0:T(8,128)(2,1)S(1)}, u32[]{:S(2)}, u32[]{:S(2)}) collective-permute-start(bf16[1,160,1376]{2,1,0:T(8,128)(2,1)S(1)} %slice.259), channel_id=1, source_target_pairs={{0,16},{8,24},{16,0},{24,8},{1,17},{9,25},{17,1},{25,9},{2,18},{10... | collective-permute-start | bytes 1320968 | tf_op jit(solution)/shard_map/ppermute | solution.py:65
  42.8 10.5 %collective-permute-start.7 = (bf16[2,80,1376]{2,1,0:T(8,128)(2,1)S(1)}, bf16[2,80,1376]{2,1,0:T(8,128)(2,1)S(1)}, u32[]{:S(2)}, u32[]{:S(2)}) collective-permute-start(bf16[2,80,1376]{2,1,0:T(8,128)(2,1)S(1)} %bitcast.201), channel_id=1, source_target_pairs={{0,8},{8,0},{16,24},{24,16},{1,9},{9,1},{17,25},{25,17},{2,10},{10... | collective-permute-start | bytes 1320968 | tf_op jit(solution)/shard_map/ppermute | solution.py:65
  43.4 11.1 %collective-permute-start.8 = (bf16[2,80,1376]{2,1,0:T(8,128)(2,1)S(1)}, bf16[2,80,1376]{2,1,0:T(8,128)(2,1)S(1)}, u32[]{:S(2)}, u32[]{:S(2)}) collective-permute-start(bf16[2,80,1376]{2,1,0:T(8,128)(2,1)S(1)} %bitcast.202), channel_id=1, source_target_pairs={{0,16},{8,24},{16,0},{24,8},{1,17},{9,25},{17,1},{25,9},{2,18},{10... | collective-permute-start | bytes 1320968 | tf_op jit(solution)/shard_map/ppermute | solution.py:65
  44.9 11.6 %collective-permute-start.11 = (bf16[640,512]{1,0:T(8,128)(2,1)}, bf16[640,512]{1,0:T(8,128)(2,1)S(1)}, u32[]{:S(2)}, u32[]{:S(2)}) collective-permute-start(bf16[640,512]{1,0:T(8,128)(2,1)} %collective-permute-done.6.refs_0_), channel_id=1, source_target_pairs={{0,1},{1,0},{2,3},{3,2},{4,5},{5,4},{6,7},{7,6},{8,9},{9,8},{10,11... | collective-permute-start | bytes 1966088 | tf_op jit(solution)/shard_map/ppermute | solution.py:68
  44.9 17.9 %collective-permute-start.13 = (bf16[640,512]{1,0:T(8,128)(2,1)}, bf16[640,512]{1,0:T(8,128)(2,1)}, u32[]{:S(2)}, u32[]{:S(2)}) collective-permute-start(bf16[640,512]{1,0:T(8,128)(2,1)} %collective-permute-done.6.refs_0_), channel_id=1, source_target_pairs={{0,2},{1,3},{2,0},{3,1},{4,6},{5,7},{6,4},{7,5},{8,10},{9,11},{10,... | collective-permute-start | bytes 1966088 | tf_op jit(solution)/shard_map/ppermute | solution.py:71
  46.5 16.3 %collective-permute-start.12 = (bf16[640,512]{1,0:T(8,128)(2,1)}, bf16[640,512]{1,0:T(8,128)(2,1)S(1)}, u32[]{:S(2)}, u32[]{:S(2)}) collective-permute-start(bf16[640,512]{1,0:T(8,128)(2,1)} %collective-permute-done.5.refs_0_), channel_id=1, source_target_pairs={{0,1},{1,0},{2,3},{3,2},{4,5},{5,4},{6,7},{7,6},{8,9},{9,8},{10,11... | collective-permute-start | bytes 1966088 | tf_op jit(solution)/shard_map/ppermute | solution.py:68
  54.5 8.3 %collective-permute-start.10 = (bf16[80,1376]{1,0:T(8,128)(2,1)S(1)}, bf16[80,1376]{1,0:T(8,128)(2,1)S(1)}, u32[]{:S(2)}, u32[]{:S(2)}) collective-permute-start(bf16[80,1376]{1,0:T(8,128)(2,1)S(1)} %slice_bitcast_fusion.20), channel_id=1, source_target_pairs={{0,16},{8,24},{16,0},{24,8},{1,17},{9,25},{17,1},{25,9},{2,18},{10... | collective-permute-start | bytes 660488 | tf_op jit(solution)/shard_map/ppermute | solution.py:65
  55.1 7.8 %collective-permute-start.9 = (bf16[80,1376]{1,0:T(8,128)(2,1)S(1)}, bf16[80,1376]{1,0:T(8,128)(2,1)S(1)}, u32[]{:S(2)}, u32[]{:S(2)}) collective-permute-start(bf16[80,1376]{1,0:T(8,128)(2,1)S(1)} %slice_bitcast_fusion.21), channel_id=1, source_target_pairs={{0,8},{8,0},{16,24},{24,16},{1,9},{9,1},{17,25},{25,17},{2,10},{10... | collective-permute-start | bytes 660488 | tf_op jit(solution)/shard_map/ppermute | solution.py:65
  66.1 25.1 %collective-permute-start.19 = (bf16[2,160,1376]{2,1,0:T(8,128)(2,1)}, bf16[2,160,1376]{2,1,0:T(8,128)(2,1)}, u32[]{:S(2)}, u32[]{:S(2)}) collective-permute-start(bf16[2,160,1376]{2,1,0:T(8,128)(2,1)} %pad_maximum_fusion), channel_id=1, source_target_pairs={{0,8},{8,0},{16,24},{24,16},{1,9},{9,1},{17,25},{25,17},{2,10},{10... | collective-permute-start | bytes 2641928 | tf_op jit(solution)/shard_map/ppermute | solution.py:65
  67.1 24.1 %collective-permute-start.20 = (bf16[2,160,1376]{2,1,0:T(8,128)(2,1)}, bf16[2,160,1376]{2,1,0:T(8,128)(2,1)}, u32[]{:S(2)}, u32[]{:S(2)}) collective-permute-start(bf16[2,160,1376]{2,1,0:T(8,128)(2,1)} %pad_maximum_fusion), channel_id=1, source_target_pairs={{0,16},{8,24},{16,0},{24,8},{1,17},{9,25},{17,1},{25,9},{2,18},{10... | collective-permute-start | bytes 2641928 | tf_op jit(solution)/shard_map/ppermute | solution.py:65
  73.0 14.8 %collective-permute-start.16 = (bf16[80,1024]{1,0:T(8,128)(2,1)S(1)}, bf16[80,1024]{1,0:T(8,128)(2,1)S(1)}, u32[]{:S(2)}, u32[]{:S(2)}) collective-permute-start(bf16[80,1024]{1,0:T(8,128)(2,1)S(1)} %get-tuple-element.287), channel_id=1, source_target_pairs={{0,2},{1,3},{2,0},{3,1},{4,6},{5,7},{6,4},{7,5},{8,10},{9,11},{10,... | collective-permute-start | bytes 491528 | tf_op jit(solution)/shard_map/ppermute | solution.py:71
  75.5 12.3 %collective-permute-start.17 = (bf16[80,1024]{1,0:T(8,128)(2,1)S(1)}, bf16[80,1024]{1,0:T(8,128)(2,1)S(1)}, u32[]{:S(2)}, u32[]{:S(2)}) collective-permute-start(bf16[80,1024]{1,0:T(8,128)(2,1)S(1)} %get-tuple-element.286), channel_id=1, source_target_pairs={{0,4},{1,5},{2,6},{3,7},{4,0},{5,1},{6,2},{7,3},{8,12},{9,13},{10,... | collective-permute-start | bytes 491528 | tf_op jit(solution)/shard_map/ppermute | solution.py:71
  76.1 15.1 %collective-permute-start.18 = (bf16[80,1024]{1,0:T(8,128)(2,1)S(1)}, bf16[80,1024]{1,0:T(8,128)(2,1)S(1)}, u32[]{:S(2)}, u32[]{:S(2)}) collective-permute-start(bf16[80,1024]{1,0:T(8,128)(2,1)S(1)} %get-tuple-element.285), channel_id=1, source_target_pairs={{0,6},{1,7},{2,4},{3,5},{4,2},{5,3},{6,0},{7,1},{8,14},{9,15},{10,... | collective-permute-start | bytes 491528 | tf_op jit(solution)/shard_map/ppermute | solution.py:71
  92.7 12.6 %collective-permute-start.21 = (bf16[80,1024]{1,0:T(8,128)(2,1)S(1)}, bf16[80,1024]{1,0:T(8,128)(2,1)S(1)}, u32[]{:S(2)}, u32[]{:S(2)}) collective-permute-start(bf16[80,1024]{1,0:T(8,128)(2,1)S(1)} %fusion.12), channel_id=1, source_target_pairs={{0,4},{1,5},{2,6},{3,7},{4,0},{5,1},{6,2},{7,3},{8,12},{9,13},{10,... | collective-permute-start | bytes 491528 | tf_op jit(solution)/shard_map/ppermute | solution.py:71
  94.6 14.4 %collective-permute-start.22 = (bf16[80,1024]{1,0:T(8,128)(2,1)S(1)}, bf16[80,1024]{1,0:T(8,128)(2,1)S(1)}, u32[]{:S(2)}, u32[]{:S(2)}) collective-permute-start(bf16[80,1024]{1,0:T(8,128)(2,1)S(1)} %fusion.12), channel_id=1, source_target_pairs={{0,6},{1,7},{2,4},{3,5},{4,2},{5,3},{6,0},{7,1},{8,14},{9,15},{10,... | collective-permute-start | bytes 491528 | tf_op jit(solution)/shard_map/ppermute | solution.py:71
  99.5 9.5 %collective-permute-start.24 = (bf16[160,1024]{1,0:T(8,128)(2,1)S(1)}, bf16[160,1024]{1,0:T(8,128)(2,1)S(1)}, u32[]{:S(2)}, u32[]{:S(2)}) collective-permute-start(bf16[160,1024]{1,0:T(8,128)(2,1)S(1)} %constant_dynamic-update-slice_fusion.refs_0_), channel_id=1, source_target_pairs={{0,8},{8,0},{16,24},{24,16},{1,9},{9,1},{17,25},{25,17},{2,10},{10... | collective-permute-start | bytes 983048 | tf_op jit(solution)/shard_map/ppermute | solution.py:65
  100.6 8.4 %collective-permute-start.25 = (bf16[160,1024]{1,0:T(8,128)(2,1)S(1)}, bf16[160,1024]{1,0:T(8,128)(2,1)S(1)}, u32[]{:S(2)}, u32[]{:S(2)}) collective-permute-start(bf16[160,1024]{1,0:T(8,128)(2,1)S(1)} %constant_dynamic-update-slice_fusion.refs_0_), channel_id=1, source_target_pairs={{0,16},{8,24},{16,0},{24,8},{1,17},{9,25},{17,1},{25,9},{2,18},{10... | collective-permute-start | bytes 983048 | tf_op jit(solution)/shard_map/ppermute | solution.py:65
  102.1 12.1 %collective-permute-start.31 = (bf16[160,1024]{1,0:T(8,128)(2,1)S(1)}, bf16[160,1024]{1,0:T(8,128)(2,1)S(1)}, u32[]{:S(2)}, u32[]{:S(2)}) collective-permute-start(bf16[160,1024]{1,0:T(8,128)(2,1)S(1)} %constant_dynamic-update-slice_fusion.refs_0_), channel_id=1, source_target_pairs={{0,1},{1,0},{2,3},{3,2},{4,5},{5,4},{6,7},{7,6},{8,9},{9,8},{10,11... | collective-permute-start | bytes 983048 | tf_op jit(solution)/shard_map/ppermute | solution.py:68
  105.3 21.0 %collective-permute-start.28 = (bf16[160,1376]{1,0:T(8,128)(2,1)S(1)}, bf16[160,1376]{1,0:T(8,128)(2,1)S(1)}, u32[]{:S(2)}, u32[]{:S(2)}) collective-permute-start(bf16[160,1376]{1,0:T(8,128)(2,1)S(1)} %get-tuple-element.269.refs_10_), channel_id=1, source_target_pairs={{0,8},{8,0},{16,24},{24,16},{1,9},{9,1},{17,25},{25,17},{2,10},{10... | collective-permute-start | bytes 1320968 | tf_op jit(solution)/shard_map/ppermute | solution.py:65
  111.1 15.2 %collective-permute-start.29 = (bf16[160,1376]{1,0:T(8,128)(2,1)S(1)}, bf16[160,1376]{1,0:T(8,128)(2,1)S(1)}, u32[]{:S(2)}, u32[]{:S(2)}) collective-permute-start(bf16[160,1376]{1,0:T(8,128)(2,1)S(1)} %get-tuple-element.273.refs_13_), channel_id=1, source_target_pairs={{0,16},{8,24},{16,0},{24,8},{1,17},{9,25},{17,1},{25,9},{2,18},{10... | collective-permute-start | bytes 1320968 | tf_op jit(solution)/shard_map/ppermute | solution.py:65
  112.6 13.8 %collective-permute-start.26 = (bf16[160,1024]{1,0:T(8,128)(2,1)S(1)}, bf16[160,1024]{1,0:T(8,128)(2,1)S(1)}, u32[]{:S(2)}, u32[]{:S(2)}) collective-permute-start(bf16[160,1024]{1,0:T(8,128)(2,1)S(1)} %constant_dynamic-update-slice_fusion.2.refs_1_), channel_id=1, source_target_pairs={{0,8},{8,0},{16,24},{24,16},{1,9},{9,1},{17,25},{25,17},{2,10},{10... | collective-permute-start | bytes 983048 | tf_op jit(solution)/shard_map/ppermute | solution.py:65
  114.2 16.7 %collective-permute-start.27 = (bf16[160,1024]{1,0:T(8,128)(2,1)S(1)}, bf16[160,1024]{1,0:T(8,128)(2,1)S(1)}, u32[]{:S(2)}, u32[]{:S(2)}) collective-permute-start(bf16[160,1024]{1,0:T(8,128)(2,1)S(1)} %constant_dynamic-update-slice_fusion.2.refs_1_), channel_id=1, source_target_pairs={{0,16},{8,24},{16,0},{24,8},{1,17},{9,25},{17,1},{25,9},{2,18},{10... | collective-permute-start | bytes 983048 | tf_op jit(solution)/shard_map/ppermute | solution.py:65
  114.5 16.4 %collective-permute-start.30 = (bf16[160,1024]{1,0:T(8,128)(2,1)S(1)}, bf16[160,1024]{1,0:T(8,128)(2,1)S(1)}, u32[]{:S(2)}, u32[]{:S(2)}) collective-permute-start(bf16[160,1024]{1,0:T(8,128)(2,1)S(1)} %collective-permute-done.25.refs_0_), channel_id=1, source_target_pairs={{0,8},{8,0},{16,24},{24,16},{1,9},{9,1},{17,25},{25,17},{2,10},{10... | collective-permute-start | bytes 983048 | tf_op jit(solution)/shard_map/ppermute | solution.py:65
  131.5 14.1 %collective-permute-start.33 = (bf16[160,1024]{1,0:T(8,128)(2,1)S(1)}, bf16[160,1024]{1,0:T(8,128)(2,1)S(1)}, u32[]{:S(2)}, u32[]{:S(2)}) collective-permute-start(bf16[160,1024]{1,0:T(8,128)(2,1)S(1)} %collective-permute-done.26.refs_1_), channel_id=1, source_target_pairs={{0,16},{8,24},{16,0},{24,8},{1,17},{9,25},{17,1},{25,9},{2,18},{10... | collective-permute-start | bytes 983048 | tf_op jit(solution)/shard_map/ppermute | solution.py:65
  132.9 12.7 %collective-permute-start.34 = (bf16[160,1024]{1,0:T(8,128)(2,1)S(1)}, bf16[160,1024]{1,0:T(8,128)(2,1)S(1)}, u32[]{:S(2)}, u32[]{:S(2)}) collective-permute-start(bf16[160,1024]{1,0:T(8,128)(2,1)S(1)} %collective-permute-done.25.refs_0_), channel_id=1, source_target_pairs={{0,1},{1,0},{2,3},{3,2},{4,5},{5,4},{6,7},{7,6},{8,9},{9,8},{10,11... | collective-permute-start | bytes 983048 | tf_op jit(solution)/shard_map/ppermute | solution.py:68
  132.9 12.7 %collective-permute-start.35 = (bf16[160,1024]{1,0:T(8,128)(2,1)S(1)}, bf16[160,1024]{1,0:T(8,128)(2,1)S(1)}, u32[]{:S(2)}, u32[]{:S(2)}) collective-permute-start(bf16[160,1024]{1,0:T(8,128)(2,1)S(1)} %collective-permute-done.27.refs_1_), channel_id=1, source_target_pairs={{0,1},{1,0},{2,3},{3,2},{4,5},{5,4},{6,7},{7,6},{8,9},{9,8},{10,11... | collective-permute-start | bytes 983048 | tf_op jit(solution)/shard_map/ppermute | solution.py:68
  173.9 15.3 %collective-permute-start.41 = (bf16[160,1024]{1,0:T(8,128)(2,1)S(1)}, bf16[160,1024]{1,0:T(8,128)(2,1)S(1)}, u32[]{:S(2)}, u32[]{:S(2)}) collective-permute-start(bf16[160,1024]{1,0:T(8,128)(2,1)S(1)} %get-tuple-element.284), channel_id=1, source_target_pairs={{0,8},{8,0},{16,24},{24,16},{1,9},{9,1},{17,25},{25,17},{2,10},{10... | collective-permute-start | bytes 983048 | tf_op jit(solution)/shard_map/ppermute | solution.py:65
  175.5 13.6 %collective-permute-start.42 = (bf16[160,1024]{1,0:T(8,128)(2,1)S(1)}, bf16[160,1024]{1,0:T(8,128)(2,1)S(1)}, u32[]{:S(2)}, u32[]{:S(2)}) collective-permute-start(bf16[160,1024]{1,0:T(8,128)(2,1)S(1)} %get-tuple-element.283), channel_id=1, source_target_pairs={{0,16},{8,24},{16,0},{24,8},{1,17},{9,25},{17,1},{25,9},{2,18},{10... | collective-permute-start | bytes 983048 | tf_op jit(solution)/shard_map/ppermute | solution.py:65
  193.3 16.8 %collective-permute-start.44 = (bf16[2,160,1024]{2,1,0:T(8,128)(2,1)S(1)}, bf16[2,160,1024]{2,1,0:T(8,128)(2,1)S(1)}, u32[]{:S(2)}, u32[]{:S(2)}) collective-permute-start(bf16[2,160,1024]{2,1,0:T(8,128)(2,1)S(1)} %get-tuple-element.215), channel_id=1, source_target_pairs={{0,8},{8,0},{16,24},{24,16},{1,9},{9,1},{17,25},{25,17},{2,10},{10... | collective-permute-start | bytes 1966088 | tf_op jit(solution)/shard_map/ppermute | solution.py:65
  193.8 16.5 %collective-permute-start.45 = (bf16[2,160,1024]{2,1,0:T(8,128)(2,1)S(1)}, bf16[2,160,1024]{2,1,0:T(8,128)(2,1)S(1)}, u32[]{:S(2)}, u32[]{:S(2)}) collective-permute-start(bf16[2,160,1024]{2,1,0:T(8,128)(2,1)S(1)} %get-tuple-element.216), channel_id=1, source_target_pairs={{0,16},{8,24},{16,0},{24,8},{1,17},{9,25},{17,1},{25,9},{2,18},{10... | collective-permute-start | bytes 1966088 | tf_op jit(solution)/shard_map/ppermute | solution.py:65
  214.2 12.7 %collective-permute-start.48 = (bf16[80,1024]{1,0:T(8,128)(2,1)S(1)}, bf16[80,1024]{1,0:T(8,128)(2,1)S(1)}, u32[]{:S(2)}, u32[]{:S(2)}) collective-permute-start(bf16[80,1024]{1,0:T(8,128)(2,1)S(1)} %get-tuple-element.281), channel_id=1, source_target_pairs={{0,4},{1,5},{2,6},{3,7},{4,0},{5,1},{6,2},{7,3},{8,12},{9,13},{10,... | collective-permute-start | bytes 491528 | tf_op jit(solution)/shard_map/ppermute | solution.py:71
  215.2 15.8 %collective-permute-start.49 = (bf16[80,1024]{1,0:T(8,128)(2,1)S(1)}, bf16[80,1024]{1,0:T(8,128)(2,1)S(1)}, u32[]{:S(2)}, u32[]{:S(2)}) collective-permute-start(bf16[80,1024]{1,0:T(8,128)(2,1)S(1)} %get-tuple-element.280), channel_id=1, source_target_pairs={{0,6},{1,7},{2,4},{3,5},{4,2},{5,3},{6,0},{7,1},{8,14},{9,15},{10,... | collective-permute-start | bytes 491528 | tf_op jit(solution)/shard_map/ppermute | solution.py:71
  231.2 13.3 %collective-permute-start.51 = (bf16[80,1024]{1,0:T(8,128)(2,1)S(1)}, bf16[80,1024]{1,0:T(8,128)(2,1)S(1)}, u32[]{:S(2)}, u32[]{:S(2)}) collective-permute-start(bf16[80,1024]{1,0:T(8,128)(2,1)S(1)} %get-tuple-element.255), channel_id=1, source_target_pairs={{0,4},{1,5},{2,6},{3,7},{4,0},{5,1},{6,2},{7,3},{8,12},{9,13},{10,... | collective-permute-start | bytes 491528 | tf_op jit(solution)/shard_map/ppermute | solution.py:71
  233.4 14.7 %collective-permute-start.52 = (bf16[80,1024]{1,0:T(8,128)(2,1)S(1)}, bf16[80,1024]{1,0:T(8,128)(2,1)S(1)}, u32[]{:S(2)}, u32[]{:S(2)}) collective-permute-start(bf16[80,1024]{1,0:T(8,128)(2,1)S(1)} %get-tuple-element.255), channel_id=1, source_target_pairs={{0,6},{1,7},{2,4},{3,5},{4,2},{5,3},{6,0},{7,1},{8,14},{9,15},{10,... | collective-permute-start | bytes 491528 | tf_op jit(solution)/shard_map/ppermute | solution.py:71
  253.3 7.6 %collective-permute-start.54 = (bf16[80,1376]{1,0:T(8,128)(2,1)S(1)}, bf16[80,1376]{1,0:T(8,128)(2,1)S(1)}, u32[]{:S(2)}, u32[]{:S(2)}) collective-permute-start(bf16[80,1376]{1,0:T(8,128)(2,1)S(1)} %get-tuple-element.295), channel_id=1, source_target_pairs={{0,16},{8,24},{16,0},{24,8},{1,17},{9,25},{17,1},{25,9},{2,18},{10... | collective-permute-start | bytes 660488 | tf_op jit(solution)/shard_map/ppermute | solution.py:65
  261.8 11.3 %collective-permute-start.56 = (bf16[2,80,1376]{2,1,0:T(8,128)(2,1)S(1)}, bf16[2,80,1376]{2,1,0:T(8,128)(2,1)S(1)}, u32[]{:S(2)}, u32[]{:S(2)}) collective-permute-start(bf16[2,80,1376]{2,1,0:T(8,128)(2,1)S(1)} %pad_maximum_fusion.4), channel_id=1, source_target_pairs={{0,8},{8,0},{16,24},{24,16},{1,9},{9,1},{17,25},{25,17},{2,10},{10... | collective-permute-start | bytes 1320968 | tf_op jit(solution)/shard_map/ppermute | solution.py:65
  263.5 11.0 %collective-permute-start.57 = (bf16[2,80,1376]{2,1,0:T(8,128)(2,1)S(1)}, bf16[2,80,1376]{2,1,0:T(8,128)(2,1)S(1)}, u32[]{:S(2)}, u32[]{:S(2)}) collective-permute-start(bf16[2,80,1376]{2,1,0:T(8,128)(2,1)S(1)} %pad_maximum_fusion.5), channel_id=1, source_target_pairs={{0,16},{8,24},{16,0},{24,8},{1,17},{9,25},{17,1},{25,9},{2,18},{10... | collective-permute-start | bytes 1320968 | tf_op jit(solution)/shard_map/ppermute | solution.py:65
  274.6 10.3 %collective-permute-start.58 = (bf16[2,80,1376]{2,1,0:T(8,128)(2,1)S(1)}, bf16[2,80,1376]{2,1,0:T(8,128)(2,1)S(1)}, u32[]{:S(2)}, u32[]{:S(2)}) collective-permute-start(bf16[2,80,1376]{2,1,0:T(8,128)(2,1)S(1)} %fusion.2), channel_id=1, source_target_pairs={{0,8},{8,0},{16,24},{24,16},{1,9},{9,1},{17,25},{25,17},{2,10},{10... | collective-permute-start | bytes 1320968 | tf_op jit(solution)/shard_map/ppermute | solution.py:65
  275.1 9.9 %collective-permute-start.59 = (bf16[2,80,1376]{2,1,0:T(8,128)(2,1)S(1)}, bf16[2,80,1376]{2,1,0:T(8,128)(2,1)S(1)}, u32[]{:S(2)}, u32[]{:S(2)}) collective-permute-start(bf16[2,80,1376]{2,1,0:T(8,128)(2,1)S(1)} %fusion.2), channel_id=1, source_target_pairs={{0,16},{8,24},{16,0},{24,8},{1,17},{9,25},{17,1},{25,9},{2,18},{10... | collective-permute-start | bytes 1320968 | tf_op jit(solution)/shard_map/ppermute | solution.py:65
  302.2 10.8 %collective-permute-start.63 = (bf16[80,1024]{1,0:T(8,128)(2,1)S(1)}, bf16[80,1024]{1,0:T(8,128)(2,1)S(1)}, u32[]{:S(2)}, u32[]{:S(2)}) collective-permute-start(bf16[80,1024]{1,0:T(8,128)(2,1)S(1)} %get-tuple-element.279), channel_id=1, source_target_pairs={{0,2},{1,3},{2,0},{3,1},{4,6},{5,7},{6,4},{7,5},{8,10},{9,11},{10,... | collective-permute-start | bytes 491528 | tf_op jit(solution)/shard_map/ppermute | solution.py:71
  302.3 13.8 %collective-permute-start.64 = (bf16[80,1024]{1,0:T(8,128)(2,1)S(1)}, bf16[80,1024]{1,0:T(8,128)(2,1)S(1)}, u32[]{:S(2)}, u32[]{:S(2)}) collective-permute-start(bf16[80,1024]{1,0:T(8,128)(2,1)S(1)} %get-tuple-element.278), channel_id=1, source_target_pairs={{0,4},{1,5},{2,6},{3,7},{4,0},{5,1},{6,2},{7,3},{8,12},{9,13},{10,... | collective-permute-start | bytes 491528 | tf_op jit(solution)/shard_map/ppermute | solution.py:71
  304.5 15.8 %collective-permute-start.65 = (bf16[80,1024]{1,0:T(8,128)(2,1)S(1)}, bf16[80,1024]{1,0:T(8,128)(2,1)S(1)}, u32[]{:S(2)}, u32[]{:S(2)}) collective-permute-start(bf16[80,1024]{1,0:T(8,128)(2,1)S(1)} %get-tuple-element.277), channel_id=1, source_target_pairs={{0,6},{1,7},{2,4},{3,5},{4,2},{5,3},{6,0},{7,1},{8,14},{9,15},{10,... | collective-permute-start | bytes 491528 | tf_op jit(solution)/shard_map/ppermute | solution.py:71
  (62 other events, 550.1 us)

commit v6 on v5

--- a/solution.py
+++ b/solution.py
@@ -616,7 +616,10 @@
             else:
                 own, mate = back_product(index, offset, count, *hold, gate_t, up_t, cot_rows, groups)
             if hops is not None:
-                own, mate, hops = lax.optimization_barrier((own, mate, hops))
+                if offset:
+                    own, mate, hops = lax.optimization_barrier((own, mate, hops))
+                else:
+                    own, hops = lax.optimization_barrier((own, hops))
             total = own.astype(F32) + plan.core_swap(mate).astype(F32)
             parts = {offset + i: total[i].reshape(2, half_rows // 2, width) for i in range(count)}
             return parts if hops is None else (parts, hops)

time: 325 us -> 321 us (0.988)
  transfers between devices with their start and end apart: 66 -> 66, of which waited for: 35 -> 34; matrix products, arithmetic and copies ran while one was open for 4% -> 4% of each run, Pallas kernels for 25% -> 25%
where the time goes in v6:
time: 321 us; the launch traced here: 318 us
  Pallas kernels  115 us (36%)
  waiting for transfers between devices  114 us (36%)
  starting transfers between devices  59.8 us (19%)
  local copies, waits for them, and re-layouts  15.5 us (5%)
  other arithmetic  7.28 us (2%)
  matrix products  4.91 us (2%)
    pallas_call x19, Pallas kernels, call(): pl.pallas_call(kernel, grid_spec=pltpu.PrefetchScalarGridSpec(num_scalar_...  115 us
    ppermute x30, waiting for transfers between devices, group_swap(): lax.ppermute(value, 'group', [(i, i ^ mask) for i in range(self.groups)])  60.1 us
    ppermute x18, waiting for transfers between devices, place_swap(): lax.ppermute(value, 'mp', [(i, i ^ 2 * mask) for i in range(self.members)])  42.8 us
    ppermute x30, starting transfers between devices, group_swap(): lax.ppermute(value, 'group', [(i, i ^ mask) for i in range(self.groups)])  34.9 us
    ppermute x18, starting transfers between devices, place_swap(): lax.ppermute(value, 'mp', [(i, i ^ 2 * mask) for i in range(self.members)])  21.8 us
    ppermute x18, waiting for transfers between devices, core_swap(): return lax.ppermute(value, 'mp', [(i, i ^ 1) for i in range(self.members)])  10.9 us
    unnamed x93, local copies, waits for them, and re-layouts  9.92 us
  transfers between devices with their start and end apart: 66, of which 34 were waited for; matrix products, arithmetic and copies ran while one was open for 4% of the time, Pallas kernels for 25%

profile of v6, /device:TPU:18, one launch (start us, length us, event | category | flops | bytes accessed | tf_op | source)
XLA Modules:
  0.0 317.7 jit_solution(8164388408377461868)
XLA Ops:
  2.1 1.8 copy-done.7
  17.1 4.4 %head_hidden_grad.3.refs_3_ = f32[640,1376]{1,0:T(8,128)S(1)} custom-call(s32[28]{0:T(128)S(1)} %stack.137.index, bf16[640,512]{1,0:T(8,128)(2,1)S(1)} %bitcast.172, bf16[640,512]{1,0:T(8,128)(2,1)S(1)} %collective-permute-done.2.refs_1_, bf16[1376,4096]{1,0:T(8,128)(2,1)} %bitcast.191), custom_call_target="tpu_custom_call" | custom-call | flops 1803550720 | bytes 12582912 | tf_op jit(solution)/shard_map/head_hidden_grad/pallas_call | solution.py:46
  21.5 5.9 %collective-permute-done = bf16[2,160,1376]{2,1,0:T(8,128)(2,1)S(1)} collective-permute-done((bf16[2,160,1376]{2,1,0:T(8,128)(2,1)S(1)}, bf16[2,160,1376]{2,1,0:T(8,128)(2,1)S(1)}, u32[]{:S(2)}, u32[]{:S(2)}) %collective-permute-start) | collective-permute-done | bytes 880672 | tf_op jit(solution)/shard_map/ppermute | solution.py:65
  27.5 2.1 collective-permute-done.1
  33.2 7.7 %collective-permute-done.4 = bf16[1,160,1376]{2,1,0:T(8,128)(2,1)S(1)} collective-permute-done((bf16[1,160,1376]{2,1,0:T(8,128)(2,1)S(1)}, bf16[1,160,1376]{2,1,0:T(8,128)(2,1)S(1)}, u32[]{:S(2)}, u32[]{:S(2)}) %collective-permute-start.4) | collective-permute-done | bytes 440352 | tf_op jit(solution)/shard_map/ppermute | solution.py:65
  47.7 5.5 %collective-permute-done.7 = bf16[2,80,1376]{2,1,0:T(8,128)(2,1)S(1)} collective-permute-done((bf16[2,80,1376]{2,1,0:T(8,128)(2,1)S(1)}, bf16[2,80,1376]{2,1,0:T(8,128)(2,1)S(1)}, u32[]{:S(2)}, u32[]{:S(2)}) %collective-permute-start.7) | collective-permute-done | bytes 440352 | tf_op jit(solution)/shard_map/ppermute | solution.py:65
  56.5 6.2 %head_hidden_grad.4.refs_5_ = f32[640,1376]{1,0:T(8,128)S(1)} custom-call(s32[28]{0:T(128)S(1)} %stack.137.index, bf16[640,512]{1,0:T(8,128)(2,1)} %collective-permute-done.6.refs_0_, bf16[640,512]{1,0:T(8,128)(2,1)S(1)} %collective-permute-done.11.refs_1_, bf16[1376,4096]{1,0:T(8,128)(2,1)} %bitcast.192, f32[640,1376]{1,0:T(8,128)} %copy-done.5), custom_call_target="tpu_custom_call" | custom-call | flops 1803550720 | bytes 16105472 | tf_op jit(solution)/shard_map/head_hidden_grad/pallas_call | solution.py:46
  62.9 2.6 trunk_down.2
  70.1 2.8 trunk_down.3
  73.0 2.5 collective-permute-start.16
  77.1 10.8 %head_hidden_grad.5 = f32[640,1376]{1,0:T(8,128)} custom-call(s32[28]{0:T(128)S(1)} %stack.137.index, bf16[640,512]{1,0:T(8,128)(2,1)} %collective-permute-done.5.refs_0_, bf16[640,512]{1,0:T(8,128)(2,1)S(1)} %copy-done.22, bf16[640,512]{1,0:T(8,128)(2,1)} %collective-permute-done.13.refs_2_, bf16[640,512]{1,0:T(8,128)(2,1)} %collective-permute-done.15.refs_3_, ...), custom_call_target="tpu_custom_call" | custom-call | flops 3607101440 | bytes 17416192 | tf_op jit(solution)/shard_map/head_hidden_grad/pallas_call | solution.py:46
  87.9 3.4 %collective-permute-done.18 = bf16[80,1024]{1,0:T(8,128)(2,1)S(1)} collective-permute-done((bf16[80,1024]{1,0:T(8,128)(2,1)S(1)}, bf16[80,1024]{1,0:T(8,128)(2,1)S(1)}, u32[]{:S(2)}, u32[]{:S(2)}) %collective-permute-start.18) | collective-permute-done | bytes 163872 | tf_op jit(solution)/shard_map/ppermute | solution.py:71
  92.7 2.0 collective-permute-start.21
  95.8 2.2 head_output_grad_rows.1.refs_13_.cot
  103.3 1.9 collective-permute-done.21
  106.7 2.3 collective-permute-done.22
  109.1 2.0 slice_bitcast_fusion.4
  115.2 9.3 %head_pre.2 = (f32[640,1376]{1,0:T(8,128)S(1)}, f32[640,1376]{1,0:T(8,128)}) custom-call(s32[28]{0:T(128)S(1)} %stack.137.index, bf16[160,1024]{1,0:T(8,128)(2,1)S(1)} %constant_dynamic-update-slice_fusion.refs_0_, bf16[160,1024]{1,0:T(8,128)(2,1)S(1)} %constant_dynamic-update-slice_fusion.2.refs_1_, bf16[160,1024]{1,0:T(8,128)(2,1)S(1)} %collective-permute-done.31.refs_2_, ...), custom_call_target="tpu_custom_call" | custom-call | flops 3607101440 | bytes 23855104 | tf_op jit(solution)/shard_map/head_pre/pallas_call | solution.py:46
  124.5 1.8 copy-done.16
  126.3 4.6 %collective-permute-done.27.refs_1_ = bf16[160,1024]{1,0:T(8,128)(2,1)S(1)} collective-permute-done((bf16[160,1024]{1,0:T(8,128)(2,1)S(1)}, bf16[160,1024]{1,0:T(8,128)(2,1)S(1)}, u32[]{:S(2)}, u32[]{:S(2)}) %collective-permute-start.27) | collective-permute-done | bytes 327712 | tf_op jit(solution)/shard_map/ppermute | solution.py:65
  133.4 10.3 %head_pre.3 = (f32[640,1376]{1,0:T(8,128)S(1)}, f32[640,1376]{1,0:T(8,128)}) custom-call(s32[28]{0:T(128)S(1)} %stack.137.index, bf16[160,1024]{1,0:T(8,128)(2,1)S(1)} %collective-permute-done.24.refs_0_, bf16[160,1024]{1,0:T(8,128)(2,1)S(1)} %collective-permute-done.26.refs_1_, bf16[160,1024]{1,0:T(8,128)(2,1)S(1)} %collective-permute-done.36.refs_2_, ...), custom_call_target="tpu_custom_call" | custom-call | flops 3607101440 | bytes 30900224 | tf_op jit(solution)/shard_map/head_pre/pallas_call | solution.py:46
  143.8 1.8 copy-done.30
  148.8 21.3 %head_act.1 = (bf16[640,1376]{1,0:T(8,128)(2,1)}, bf16[640,1376]{1,0:T(8,128)(2,1)}, bf16[1,320,1024]{2,1,0:T(8,128)(2,1)}, bf16[1,320,1024]{2,1,0:T(8,128)(2,1)}) custom-call(s32[28]{0:T(128)} %copy-done.28, bf16[160,1024]{1,0:T(8,128)(2,1)} %copy-done.36, bf16[160,1024]{1,0:T(8,128)(2,1)} %copy-done.37, bf16[160,1024]{1,0:T(8,128)(2,1)} %copy-done.40, ...), custom_call_target="tpu_custom_call" | custom-call | flops 10821304320 | bytes 36388864 | tf_op jit(solution)/shard_map/head_act/pallas_call | solution.py:46
  170.3 2.2 collective-permute-done.40
  176.6 12.5 %head_back.2 = (bf16[2,320,1024]{2,1,0:T(8,128)(2,1)S(1)}, bf16[2,320,1024]{2,1,0:T(8,128)(2,1)S(1)}) custom-call(s32[28]{0:T(128)S(1)} %copy-done.29, bf16[640,1376]{1,0:T(8,128)(2,1)S(1)} %copy-done.12, bf16[640,1376]{1,0:T(8,128)(2,1)} %get-tuple-element.211.dup, bf16[1376,4096]{1,0:T(8,128)(2,1)} %bitcast.184, bf16[1376,4096]{1,0:T(8,128)(2,1)} %bitcast.189, ...), custom_call_target="tpu_custom_call" | custom-call | flops 7214202880 | bytes 26722304 | tf_op jit(solution)/shard_map/head_back/pallas_call | solution.py:46
  189.2 3.0 collective-permute-done.43
  194.8 6.9 %head_back.3 = (bf16[1,320,1024]{2,1,0:T(8,128)(2,1)S(1)}, bf16[1,320,1024]{2,1,0:T(8,128)(2,1)S(1)}) custom-call(s32[28]{0:T(128)S(1)} %copy-done.29, bf16[640,1376]{1,0:T(8,128)(2,1)S(1)} %copy-done.12, bf16[640,1376]{1,0:T(8,128)(2,1)S(1)} %copy-done.13, bf16[1376,4096]{1,0:T(8,128)(2,1)} %bitcast.185, bf16[1376,4096]{1,0:T(8,128)(2,1)} %bitcast.190, ...), custom_call_target="tpu_custom_call" | custom-call | flops 3607101440 | bytes 26722304 | tf_op jit(solution)/shard_map/head_back/pallas_call | solution.py:46
  201.7 8.4 %collective-permute-done.44 = bf16[2,160,1024]{2,1,0:T(8,128)(2,1)S(1)} collective-permute-done((bf16[2,160,1024]{2,1,0:T(8,128)(2,1)S(1)}, bf16[2,160,1024]{2,1,0:T(8,128)(2,1)S(1)}, u32[]{:S(2)}, u32[]{:S(2)}) %collective-permute-start.44) | collective-permute-done | bytes 655392 | tf_op jit(solution)/shard_map/ppermute | solution.py:65
  214.5 3.6 %collective-permute-done.47 = bf16[80,1024]{1,0:T(8,128)(2,1)S(1)} collective-permute-done((bf16[80,1024]{1,0:T(8,128)(2,1)S(1)}, bf16[80,1024]{1,0:T(8,128)(2,1)S(1)}, u32[]{:S(2)}, u32[]{:S(2)}) %collective-permute-start.47) | collective-permute-done | bytes 163872 | tf_op jit(solution)/shard_map/ppermute | solution.py:71
  218.1 6.2 %collective-permute-done.48 = bf16[80,1024]{1,0:T(8,128)(2,1)S(1)} collective-permute-done((bf16[80,1024]{1,0:T(8,128)(2,1)S(1)}, bf16[80,1024]{1,0:T(8,128)(2,1)S(1)}, u32[]{:S(2)}, u32[]{:S(2)}) %collective-permute-start.48) | collective-permute-done | bytes 163872 | tf_op jit(solution)/shard_map/ppermute | solution.py:71
  224.4 3.6 %collective-permute-done.49 = bf16[80,1024]{1,0:T(8,128)(2,1)S(1)} collective-permute-done((bf16[80,1024]{1,0:T(8,128)(2,1)S(1)}, bf16[80,1024]{1,0:T(8,128)(2,1)S(1)}, u32[]{:S(2)}, u32[]{:S(2)}) %collective-permute-start.49) | collective-permute-done | bytes 163872 | tf_op jit(solution)/shard_map/ppermute | solution.py:71
  228.1 2.1 collective-permute-start.51
  231.6 3.6 %collective-permute-done.50 = bf16[80,1024]{1,0:T(8,128)(2,1)S(1)} collective-permute-done((bf16[80,1024]{1,0:T(8,128)(2,1)S(1)}, bf16[80,1024]{1,0:T(8,128)(2,1)S(1)}, u32[]{:S(2)}, u32[]{:S(2)}) %collective-permute-start.50) | collective-permute-done | bytes 163872 | tf_op jit(solution)/shard_map/ppermute | solution.py:71
  235.2 5.2 %collective-permute-done.51 = bf16[80,1024]{1,0:T(8,128)(2,1)S(1)} collective-permute-done((bf16[80,1024]{1,0:T(8,128)(2,1)S(1)}, bf16[80,1024]{1,0:T(8,128)(2,1)S(1)}, u32[]{:S(2)}, u32[]{:S(2)}) %collective-permute-start.51) | collective-permute-done | bytes 163872 | tf_op jit(solution)/shard_map/ppermute | solution.py:71
  240.4 4.2 %collective-permute-done.52 = bf16[80,1024]{1,0:T(8,128)(2,1)S(1)} collective-permute-done((bf16[80,1024]{1,0:T(8,128)(2,1)S(1)}, bf16[80,1024]{1,0:T(8,128)(2,1)S(1)}, u32[]{:S(2)}, u32[]{:S(2)}) %collective-permute-start.52) | collective-permute-done | bytes 163872 | tf_op jit(solution)/shard_map/ppermute | solution.py:71
  244.8 2.0 collective-permute-done.53
  246.9 2.8 trunk_hidden_grad.1
  252.3 5.1 %collective-permute-done.54 = bf16[80,1376]{1,0:T(8,128)(2,1)S(1)} collective-permute-done((bf16[80,1376]{1,0:T(8,128)(2,1)S(1)}, bf16[80,1376]{1,0:T(8,128)(2,1)S(1)}, u32[]{:S(2)}, u32[]{:S(2)}) %collective-permute-start.54) | collective-permute-done | bytes 220192 | tf_op jit(solution)/shard_map/ppermute | solution.py:65
  262.1 7.5 %collective-permute-done.56 = bf16[2,80,1376]{2,1,0:T(8,128)(2,1)S(1)} collective-permute-done((bf16[2,80,1376]{2,1,0:T(8,128)(2,1)S(1)}, bf16[2,80,1376]{2,1,0:T(8,128)(2,1)S(1)}, u32[]{:S(2)}, u32[]{:S(2)}) %collective-permute-start.56) | collective-permute-done | bytes 440352 | tf_op jit(solution)/shard_map/ppermute | solution.py:65
  272.7 4.9 %fusion.21 = f32[1376,1024]{1,0:T(8,128)} fusion(bf16[640,1376]{1,0:T(8,128)(2,1)S(1)} %bitcast.162, bf16[640,1024]{1,0:T(8,128)(2,1)S(1)} %constant_dynamic-update-slice_fusion.4.refs_0_.refs_1_.refs_2_.refs_3_), kind=kOutput, calls=%fused_computation.86 | convolution fusion | flops 1803550720 | bytes 8708096 | tf_op jit(solution)/shard_map/dot_general | solution.py:21
  277.6 3.8 %collective-permute-done.58 = bf16[2,80,1376]{2,1,0:T(8,128)(2,1)S(1)} collective-permute-done((bf16[2,80,1376]{2,1,0:T(8,128)(2,1)S(1)}, bf16[2,80,1376]{2,1,0:T(8,128)(2,1)S(1)}, u32[]{:S(2)}, u32[]{:S(2)}) %collective-permute-start.58) | collective-permute-done | bytes 440352 | tf_op jit(solution)/shard_map/ppermute | solution.py:65
  284.4 3.1 collective-permute-done.60.refs_6_
  289.3 6.9 %trunk_act.1 = (bf16[640,1376]{1,0:T(8,128)(2,1)S(1)}, bf16[640,1376]{1,0:T(8,128)(2,1)S(1)}, bf16[320,1024]{1,0:T(8,128)(2,1)S(1)}, bf16[320,1024]{1,0:T(8,128)(2,1)S(1)}) custom-call(s32[28]{0:T(128)S(1)} %copy-done.29, bf16[80,1376]{1,0:T(8,128)(2,1)S(1)} %get-tuple-element.291.refs_0_, bf16[80,1376]{1,0:T(8,128)(2,1)S(1)} %get-tuple-element.290.refs_1_, ...), custom_call_target="tpu_custom_call" | custom-call | flops 3607101440 | bytes 10919936 | tf_op jit(solution)/shard_map/trunk_act/pallas_call | solution.py:46
  296.3 2.1 collective-permute-done.62
  300.4 1.8 collective-permute-start.65
  302.2 7.3 %trunk_weight_grads.1 = (f32[1376,1024]{1,0:T(8,128)}, f32[1376,1024]{1,0:T(8,128)}) custom-call(s32[28]{0:T(128)S(1)} %copy-done.29, bf16[640,1376]{1,0:T(8,128)(2,1)S(1)} %get-tuple-element.241.dgate, bf16[640,1376]{1,0:T(8,128)(2,1)S(1)} %get-tuple-element.242.dup, bf16[640,1024]{1,0:T(8,128)(2,1)S(1)} %copy-done.24), custom_call_target="tpu_custom_call" | custom-call | flops 3607101440 | bytes 4833280 | tf_op jit(solution)/shard_map/trunk_weight_grads/pallas_call | solution.py:46
  309.5 2.5 collective-permute-done.64
  312.0 4.7 %collective-permute-done.65 = bf16[80,1024]{1,0:T(8,128)(2,1)S(1)} collective-permute-done((bf16[80,1024]{1,0:T(8,128)(2,1)S(1)}, bf16[80,1024]{1,0:T(8,128)(2,1)S(1)}, u32[]{:S(2)}, u32[]{:S(2)}) %collective-permute-start.65) | collective-permute-done | bytes 163872 | tf_op jit(solution)/shard_map/ppermute | solution.py:71
  (247 shorter events, 84.6 us)
Async XLA Ops:
  5.7 21.8 %collective-permute-start = (bf16[2,160,1376]{2,1,0:T(8,128)(2,1)S(1)}, bf16[2,160,1376]{2,1,0:T(8,128)(2,1)S(1)}, u32[]{:S(2)}, u32[]{:S(2)}) collective-permute-start(bf16[2,160,1376]{2,1,0:T(8,128)(2,1)S(1)} %bitcast.179), channel_id=1, source_target_pairs={{0,8},{8,0},{16,24},{24,16},{1,9},{9,1},{17,25},{25,17},{2,10},{10... | collective-permute-start | bytes 2641928 | tf_op jit(solution)/shard_map/ppermute | solution.py:65
  8.0 21.5 %collective-permute-start.1 = (bf16[2,160,1376]{2,1,0:T(8,128)(2,1)S(1)}, bf16[2,160,1376]{2,1,0:T(8,128)(2,1)S(1)}, u32[]{:S(2)}, u32[]{:S(2)}) collective-permute-start(bf16[2,160,1376]{2,1,0:T(8,128)(2,1)S(1)} %bitcast.180), channel_id=1, source_target_pairs={{0,16},{8,24},{16,0},{24,8},{1,17},{9,25},{17,1},{25,9},{2,18},{10... | collective-permute-start | bytes 2641928 | tf_op jit(solution)/shard_map/ppermute | solution.py:65
  9.8 32.7 %collective-permute-start.5 = (bf16[640,512]{1,0:T(8,128)(2,1)S(1)}, bf16[640,512]{1,0:T(8,128)(2,1)}, u32[]{:S(2)}, u32[]{:S(2)}) collective-permute-start(bf16[640,512]{1,0:T(8,128)(2,1)S(1)} %bitcast.170), channel_id=1, source_target_pairs={{0,2},{1,3},{2,0},{3,1},{4,6},{5,7},{6,4},{7,5},{8,10},{9,11},{10,... | collective-permute-start | bytes 1966088 | tf_op jit(solution)/shard_map/ppermute | solution.py:71
  11.4 31.1 %collective-permute-start.6 = (bf16[640,512]{1,0:T(8,128)(2,1)S(1)}, bf16[640,512]{1,0:T(8,128)(2,1)}, u32[]{:S(2)}, u32[]{:S(2)}) collective-permute-start(bf16[640,512]{1,0:T(8,128)(2,1)S(1)} %bitcast.171), channel_id=1, source_target_pairs={{0,4},{1,5},{2,6},{3,7},{4,0},{5,1},{6,2},{7,3},{8,12},{9,13},{10,... | collective-permute-start | bytes 1966088 | tf_op jit(solution)/shard_map/ppermute | solution.py:71
  29.8 11.1 %collective-permute-start.4 = (bf16[1,160,1376]{2,1,0:T(8,128)(2,1)S(1)}, bf16[1,160,1376]{2,1,0:T(8,128)(2,1)S(1)}, u32[]{:S(2)}, u32[]{:S(2)}) collective-permute-start(bf16[1,160,1376]{2,1,0:T(8,128)(2,1)S(1)} %slice.258), channel_id=1, source_target_pairs={{0,8},{8,0},{16,24},{24,16},{1,9},{9,1},{17,25},{25,17},{2,10},{10... | collective-permute-start | bytes 1320968 | tf_op jit(solution)/shard_map/ppermute | solution.py:65
  31.6 10.8 %collective-permute-start.3 = (bf16[1,160,1376]{2,1,0:T(8,128)(2,1)S(1)}, bf16[1,160,1376]{2,1,0:T(8,128)(2,1)S(1)}, u32[]{:S(2)}, u32[]{:S(2)}) collective-permute-start(bf16[1,160,1376]{2,1,0:T(8,128)(2,1)S(1)} %slice.259), channel_id=1, source_target_pairs={{0,16},{8,24},{16,0},{24,8},{1,17},{9,25},{17,1},{25,9},{2,18},{10... | collective-permute-start | bytes 1320968 | tf_op jit(solution)/shard_map/ppermute | solution.py:65
  42.8 10.5 %collective-permute-start.7 = (bf16[2,80,1376]{2,1,0:T(8,128)(2,1)S(1)}, bf16[2,80,1376]{2,1,0:T(8,128)(2,1)S(1)}, u32[]{:S(2)}, u32[]{:S(2)}) collective-permute-start(bf16[2,80,1376]{2,1,0:T(8,128)(2,1)S(1)} %bitcast.201), channel_id=1, source_target_pairs={{0,8},{8,0},{16,24},{24,16},{1,9},{9,1},{17,25},{25,17},{2,10},{10... | collective-permute-start | bytes 1320968 | tf_op jit(solution)/shard_map/ppermute | solution.py:65
  43.4 11.1 %collective-permute-start.8 = (bf16[2,80,1376]{2,1,0:T(8,128)(2,1)S(1)}, bf16[2,80,1376]{2,1,0:T(8,128)(2,1)S(1)}, u32[]{:S(2)}, u32[]{:S(2)}) collective-permute-start(bf16[2,80,1376]{2,1,0:T(8,128)(2,1)S(1)} %bitcast.202), channel_id=1, source_target_pairs={{0,16},{8,24},{16,0},{24,8},{1,17},{9,25},{17,1},{25,9},{2,18},{10... | collective-permute-start | bytes 1320968 | tf_op jit(solution)/shard_map/ppermute | solution.py:65
  44.9 11.6 %collective-permute-start.11 = (bf16[640,512]{1,0:T(8,128)(2,1)}, bf16[640,512]{1,0:T(8,128)(2,1)S(1)}, u32[]{:S(2)}, u32[]{:S(2)}) collective-permute-start(bf16[640,512]{1,0:T(8,128)(2,1)} %collective-permute-done.6.refs_0_), channel_id=1, source_target_pairs={{0,1},{1,0},{2,3},{3,2},{4,5},{5,4},{6,7},{7,6},{8,9},{9,8},{10,11... | collective-permute-start | bytes 1966088 | tf_op jit(solution)/shard_map/ppermute | solution.py:68
  44.9 17.9 %collective-permute-start.13 = (bf16[640,512]{1,0:T(8,128)(2,1)}, bf16[640,512]{1,0:T(8,128)(2,1)}, u32[]{:S(2)}, u32[]{:S(2)}) collective-permute-start(bf16[640,512]{1,0:T(8,128)(2,1)} %collective-permute-done.6.refs_0_), channel_id=1, source_target_pairs={{0,2},{1,3},{2,0},{3,1},{4,6},{5,7},{6,4},{7,5},{8,10},{9,11},{10,... | collective-permute-start | bytes 1966088 | tf_op jit(solution)/shard_map/ppermute | solution.py:71
  46.5 16.3 %collective-permute-start.12 = (bf16[640,512]{1,0:T(8,128)(2,1)}, bf16[640,512]{1,0:T(8,128)(2,1)S(1)}, u32[]{:S(2)}, u32[]{:S(2)}) collective-permute-start(bf16[640,512]{1,0:T(8,128)(2,1)} %collective-permute-done.5.refs_0_), channel_id=1, source_target_pairs={{0,1},{1,0},{2,3},{3,2},{4,5},{5,4},{6,7},{7,6},{8,9},{9,8},{10,11... | collective-permute-start | bytes 1966088 | tf_op jit(solution)/shard_map/ppermute | solution.py:68
  54.5 8.3 %collective-permute-start.10 = (bf16[80,1376]{1,0:T(8,128)(2,1)S(1)}, bf16[80,1376]{1,0:T(8,128)(2,1)S(1)}, u32[]{:S(2)}, u32[]{:S(2)}) collective-permute-start(bf16[80,1376]{1,0:T(8,128)(2,1)S(1)} %slice_bitcast_fusion.20), channel_id=1, source_target_pairs={{0,16},{8,24},{16,0},{24,8},{1,17},{9,25},{17,1},{25,9},{2,18},{10... | collective-permute-start | bytes 660488 | tf_op jit(solution)/shard_map/ppermute | solution.py:65
  55.1 7.8 %collective-permute-start.9 = (bf16[80,1376]{1,0:T(8,128)(2,1)S(1)}, bf16[80,1376]{1,0:T(8,128)(2,1)S(1)}, u32[]{:S(2)}, u32[]{:S(2)}) collective-permute-start(bf16[80,1376]{1,0:T(8,128)(2,1)S(1)} %slice_bitcast_fusion.21), channel_id=1, source_target_pairs={{0,8},{8,0},{16,24},{24,16},{1,9},{9,1},{17,25},{25,17},{2,10},{10... | collective-permute-start | bytes 660488 | tf_op jit(solution)/shard_map/ppermute | solution.py:65
  66.1 25.1 %collective-permute-start.19 = (bf16[2,160,1376]{2,1,0:T(8,128)(2,1)}, bf16[2,160,1376]{2,1,0:T(8,128)(2,1)}, u32[]{:S(2)}, u32[]{:S(2)}) collective-permute-start(bf16[2,160,1376]{2,1,0:T(8,128)(2,1)} %pad_maximum_fusion), channel_id=1, source_target_pairs={{0,8},{8,0},{16,24},{24,16},{1,9},{9,1},{17,25},{25,17},{2,10},{10... | collective-permute-start | bytes 2641928 | tf_op jit(solution)/shard_map/ppermute | solution.py:65
  67.1 24.1 %collective-permute-start.20 = (bf16[2,160,1376]{2,1,0:T(8,128)(2,1)}, bf16[2,160,1376]{2,1,0:T(8,128)(2,1)}, u32[]{:S(2)}, u32[]{:S(2)}) collective-permute-start(bf16[2,160,1376]{2,1,0:T(8,128)(2,1)} %pad_maximum_fusion), channel_id=1, source_target_pairs={{0,16},{8,24},{16,0},{24,8},{1,17},{9,25},{17,1},{25,9},{2,18},{10... | collective-permute-start | bytes 2641928 | tf_op jit(solution)/shard_map/ppermute | solution.py:65
  73.0 14.8 %collective-permute-start.16 = (bf16[80,1024]{1,0:T(8,128)(2,1)S(1)}, bf16[80,1024]{1,0:T(8,128)(2,1)S(1)}, u32[]{:S(2)}, u32[]{:S(2)}) collective-permute-start(bf16[80,1024]{1,0:T(8,128)(2,1)S(1)} %get-tuple-element.285), channel_id=1, source_target_pairs={{0,2},{1,3},{2,0},{3,1},{4,6},{5,7},{6,4},{7,5},{8,10},{9,11},{10,... | collective-permute-start | bytes 491528 | tf_op jit(solution)/shard_map/ppermute | solution.py:71
  75.5 12.3 %collective-permute-start.17 = (bf16[80,1024]{1,0:T(8,128)(2,1)S(1)}, bf16[80,1024]{1,0:T(8,128)(2,1)S(1)}, u32[]{:S(2)}, u32[]{:S(2)}) collective-permute-start(bf16[80,1024]{1,0:T(8,128)(2,1)S(1)} %get-tuple-element.284), channel_id=1, source_target_pairs={{0,4},{1,5},{2,6},{3,7},{4,0},{5,1},{6,2},{7,3},{8,12},{9,13},{10,... | collective-permute-start | bytes 491528 | tf_op jit(solution)/shard_map/ppermute | solution.py:71
  76.1 15.1 %collective-permute-start.18 = (bf16[80,1024]{1,0:T(8,128)(2,1)S(1)}, bf16[80,1024]{1,0:T(8,128)(2,1)S(1)}, u32[]{:S(2)}, u32[]{:S(2)}) collective-permute-start(bf16[80,1024]{1,0:T(8,128)(2,1)S(1)} %get-tuple-element.283), channel_id=1, source_target_pairs={{0,6},{1,7},{2,4},{3,5},{4,2},{5,3},{6,0},{7,1},{8,14},{9,15},{10,... | collective-permute-start | bytes 491528 | tf_op jit(solution)/shard_map/ppermute | solution.py:71
  92.7 12.6 %collective-permute-start.21 = (bf16[80,1024]{1,0:T(8,128)(2,1)S(1)}, bf16[80,1024]{1,0:T(8,128)(2,1)S(1)}, u32[]{:S(2)}, u32[]{:S(2)}) collective-permute-start(bf16[80,1024]{1,0:T(8,128)(2,1)S(1)} %fusion.12), channel_id=1, source_target_pairs={{0,4},{1,5},{2,6},{3,7},{4,0},{5,1},{6,2},{7,3},{8,12},{9,13},{10,... | collective-permute-start | bytes 491528 | tf_op jit(solution)/shard_map/ppermute | solution.py:71
  94.6 14.4 %collective-permute-start.22 = (bf16[80,1024]{1,0:T(8,128)(2,1)S(1)}, bf16[80,1024]{1,0:T(8,128)(2,1)S(1)}, u32[]{:S(2)}, u32[]{:S(2)}) collective-permute-start(bf16[80,1024]{1,0:T(8,128)(2,1)S(1)} %fusion.12), channel_id=1, source_target_pairs={{0,6},{1,7},{2,4},{3,5},{4,2},{5,3},{6,0},{7,1},{8,14},{9,15},{10,... | collective-permute-start | bytes 491528 | tf_op jit(solution)/shard_map/ppermute | solution.py:71
  99.5 9.5 %collective-permute-start.24 = (bf16[160,1024]{1,0:T(8,128)(2,1)S(1)}, bf16[160,1024]{1,0:T(8,128)(2,1)S(1)}, u32[]{:S(2)}, u32[]{:S(2)}) collective-permute-start(bf16[160,1024]{1,0:T(8,128)(2,1)S(1)} %constant_dynamic-update-slice_fusion.refs_0_), channel_id=1, source_target_pairs={{0,8},{8,0},{16,24},{24,16},{1,9},{9,1},{17,25},{25,17},{2,10},{10... | collective-permute-start | bytes 983048 | tf_op jit(solution)/shard_map/ppermute | solution.py:65
  100.6 8.4 %collective-permute-start.25 = (bf16[160,1024]{1,0:T(8,128)(2,1)S(1)}, bf16[160,1024]{1,0:T(8,128)(2,1)S(1)}, u32[]{:S(2)}, u32[]{:S(2)}) collective-permute-start(bf16[160,1024]{1,0:T(8,128)(2,1)S(1)} %constant_dynamic-update-slice_fusion.refs_0_), channel_id=1, source_target_pairs={{0,16},{8,24},{16,0},{24,8},{1,17},{9,25},{17,1},{25,9},{2,18},{10... | collective-permute-start | bytes 983048 | tf_op jit(solution)/shard_map/ppermute | solution.py:65
  102.1 12.1 %collective-permute-start.31 = (bf16[160,1024]{1,0:T(8,128)(2,1)S(1)}, bf16[160,1024]{1,0:T(8,128)(2,1)S(1)}, u32[]{:S(2)}, u32[]{:S(2)}) collective-permute-start(bf16[160,1024]{1,0:T(8,128)(2,1)S(1)} %constant_dynamic-update-slice_fusion.refs_0_), channel_id=1, source_target_pairs={{0,1},{1,0},{2,3},{3,2},{4,5},{5,4},{6,7},{7,6},{8,9},{9,8},{10,11... | collective-permute-start | bytes 983048 | tf_op jit(solution)/shard_map/ppermute | solution.py:68
  105.3 21.0 %collective-permute-start.28 = (bf16[160,1376]{1,0:T(8,128)(2,1)S(1)}, bf16[160,1376]{1,0:T(8,128)(2,1)S(1)}, u32[]{:S(2)}, u32[]{:S(2)}) collective-permute-start(bf16[160,1376]{1,0:T(8,128)(2,1)S(1)} %get-tuple-element.267.refs_10_), channel_id=1, source_target_pairs={{0,8},{8,0},{16,24},{24,16},{1,9},{9,1},{17,25},{25,17},{2,10},{10... | collective-permute-start | bytes 1320968 | tf_op jit(solution)/shard_map/ppermute | solution.py:65
  111.1 15.2 %collective-permute-start.29 = (bf16[160,1376]{1,0:T(8,128)(2,1)S(1)}, bf16[160,1376]{1,0:T(8,128)(2,1)S(1)}, u32[]{:S(2)}, u32[]{:S(2)}) collective-permute-start(bf16[160,1376]{1,0:T(8,128)(2,1)S(1)} %get-tuple-element.271.refs_13_), channel_id=1, source_target_pairs={{0,16},{8,24},{16,0},{24,8},{1,17},{9,25},{17,1},{25,9},{2,18},{10... | collective-permute-start | bytes 1320968 | tf_op jit(solution)/shard_map/ppermute | solution.py:65
  112.6 13.8 %collective-permute-start.26 = (bf16[160,1024]{1,0:T(8,128)(2,1)S(1)}, bf16[160,1024]{1,0:T(8,128)(2,1)S(1)}, u32[]{:S(2)}, u32[]{:S(2)}) collective-permute-start(bf16[160,1024]{1,0:T(8,128)(2,1)S(1)} %constant_dynamic-update-slice_fusion.2.refs_1_), channel_id=1, source_target_pairs={{0,8},{8,0},{16,24},{24,16},{1,9},{9,1},{17,25},{25,17},{2,10},{10... | collective-permute-start | bytes 983048 | tf_op jit(solution)/shard_map/ppermute | solution.py:65
  114.2 16.7 %collective-permute-start.27 = (bf16[160,1024]{1,0:T(8,128)(2,1)S(1)}, bf16[160,1024]{1,0:T(8,128)(2,1)S(1)}, u32[]{:S(2)}, u32[]{:S(2)}) collective-permute-start(bf16[160,1024]{1,0:T(8,128)(2,1)S(1)} %constant_dynamic-update-slice_fusion.2.refs_1_), channel_id=1, source_target_pairs={{0,16},{8,24},{16,0},{24,8},{1,17},{9,25},{17,1},{25,9},{2,18},{10... | collective-permute-start | bytes 983048 | tf_op jit(solution)/shard_map/ppermute | solution.py:65
  114.5 16.4 %collective-permute-start.30 = (bf16[160,1024]{1,0:T(8,128)(2,1)S(1)}, bf16[160,1024]{1,0:T(8,128)(2,1)S(1)}, u32[]{:S(2)}, u32[]{:S(2)}) collective-permute-start(bf16[160,1024]{1,0:T(8,128)(2,1)S(1)} %collective-permute-done.25.refs_0_), channel_id=1, source_target_pairs={{0,8},{8,0},{16,24},{24,16},{1,9},{9,1},{17,25},{25,17},{2,10},{10... | collective-permute-start | bytes 983048 | tf_op jit(solution)/shard_map/ppermute | solution.py:65
  131.5 14.1 %collective-permute-start.33 = (bf16[160,1024]{1,0:T(8,128)(2,1)S(1)}, bf16[160,1024]{1,0:T(8,128)(2,1)S(1)}, u32[]{:S(2)}, u32[]{:S(2)}) collective-permute-start(bf16[160,1024]{1,0:T(8,128)(2,1)S(1)} %collective-permute-done.26.refs_1_), channel_id=1, source_target_pairs={{0,16},{8,24},{16,0},{24,8},{1,17},{9,25},{17,1},{25,9},{2,18},{10... | collective-permute-start | bytes 983048 | tf_op jit(solution)/shard_map/ppermute | solution.py:65
  132.9 12.7 %collective-permute-start.34 = (bf16[160,1024]{1,0:T(8,128)(2,1)S(1)}, bf16[160,1024]{1,0:T(8,128)(2,1)S(1)}, u32[]{:S(2)}, u32[]{:S(2)}) collective-permute-start(bf16[160,1024]{1,0:T(8,128)(2,1)S(1)} %collective-permute-done.25.refs_0_), channel_id=1, source_target_pairs={{0,1},{1,0},{2,3},{3,2},{4,5},{5,4},{6,7},{7,6},{8,9},{9,8},{10,11... | collective-permute-start | bytes 983048 | tf_op jit(solution)/shard_map/ppermute | solution.py:68
  132.9 12.7 %collective-permute-start.35 = (bf16[160,1024]{1,0:T(8,128)(2,1)S(1)}, bf16[160,1024]{1,0:T(8,128)(2,1)S(1)}, u32[]{:S(2)}, u32[]{:S(2)}) collective-permute-start(bf16[160,1024]{1,0:T(8,128)(2,1)S(1)} %collective-permute-done.27.refs_1_), channel_id=1, source_target_pairs={{0,1},{1,0},{2,3},{3,2},{4,5},{5,4},{6,7},{7,6},{8,9},{9,8},{10,11... | collective-permute-start | bytes 983048 | tf_op jit(solution)/shard_map/ppermute | solution.py:68
  173.9 15.3 %collective-permute-start.41 = (bf16[160,1024]{1,0:T(8,128)(2,1)S(1)}, bf16[160,1024]{1,0:T(8,128)(2,1)S(1)}, u32[]{:S(2)}, u32[]{:S(2)}) collective-permute-start(bf16[160,1024]{1,0:T(8,128)(2,1)S(1)} %get-tuple-element.282), channel_id=1, source_target_pairs={{0,8},{8,0},{16,24},{24,16},{1,9},{9,1},{17,25},{25,17},{2,10},{10... | collective-permute-start | bytes 983048 | tf_op jit(solution)/shard_map/ppermute | solution.py:65
  175.5 13.6 %collective-permute-start.42 = (bf16[160,1024]{1,0:T(8,128)(2,1)S(1)}, bf16[160,1024]{1,0:T(8,128)(2,1)S(1)}, u32[]{:S(2)}, u32[]{:S(2)}) collective-permute-start(bf16[160,1024]{1,0:T(8,128)(2,1)S(1)} %get-tuple-element.281), channel_id=1, source_target_pairs={{0,16},{8,24},{16,0},{24,8},{1,17},{9,25},{17,1},{25,9},{2,18},{10... | collective-permute-start | bytes 983048 | tf_op jit(solution)/shard_map/ppermute | solution.py:65
  193.3 16.8 %collective-permute-start.44 = (bf16[2,160,1024]{2,1,0:T(8,128)(2,1)S(1)}, bf16[2,160,1024]{2,1,0:T(8,128)(2,1)S(1)}, u32[]{:S(2)}, u32[]{:S(2)}) collective-permute-start(bf16[2,160,1024]{2,1,0:T(8,128)(2,1)S(1)} %get-tuple-element.213), channel_id=1, source_target_pairs={{0,8},{8,0},{16,24},{24,16},{1,9},{9,1},{17,25},{25,17},{2,10},{10... | collective-permute-start | bytes 1966088 | tf_op jit(solution)/shard_map/ppermute | solution.py:65
  193.8 16.5 %collective-permute-start.45 = (bf16[2,160,1024]{2,1,0:T(8,128)(2,1)S(1)}, bf16[2,160,1024]{2,1,0:T(8,128)(2,1)S(1)}, u32[]{:S(2)}, u32[]{:S(2)}) collective-permute-start(bf16[2,160,1024]{2,1,0:T(8,128)(2,1)S(1)} %get-tuple-element.214), channel_id=1, source_target_pairs={{0,16},{8,24},{16,0},{24,8},{1,17},{9,25},{17,1},{25,9},{2,18},{10... | collective-permute-start | bytes 1966088 | tf_op jit(solution)/shard_map/ppermute | solution.py:65
  201.7 8.6 %collective-permute-start.46 = (bf16[1,320,1024]{2,1,0:T(8,128)(2,1)S(1)}, bf16[1,320,1024]{2,1,0:T(8,128)(2,1)S(1)}, u32[]{:S(2)}, u32[]{:S(2)}) collective-permute-start(bf16[1,320,1024]{2,1,0:T(8,128)(2,1)S(1)} %get-tuple-element.216), channel_id=1, source_target_pairs={{0,1},{1,0},{2,3},{3,2},{4,5},{5,4},{6,7},{7,6},{8,9},{9,8},{10,11... | collective-permute-start | bytes 1966088 | tf_op jit(solution)/shard_map/ppermute | solution.py:68
  212.1 12.3 %collective-permute-start.48 = (bf16[80,1024]{1,0:T(8,128)(2,1)S(1)}, bf16[80,1024]{1,0:T(8,128)(2,1)S(1)}, u32[]{:S(2)}, u32[]{:S(2)}) collective-permute-start(bf16[80,1024]{1,0:T(8,128)(2,1)S(1)} %get-tuple-element.279), channel_id=1, source_target_pairs={{0,4},{1,5},{2,6},{3,7},{4,0},{5,1},{6,2},{7,3},{8,12},{9,13},{10,... | collective-permute-start | bytes 491528 | tf_op jit(solution)/shard_map/ppermute | solution.py:71
  213.1 14.8 %collective-permute-start.49 = (bf16[80,1024]{1,0:T(8,128)(2,1)S(1)}, bf16[80,1024]{1,0:T(8,128)(2,1)S(1)}, u32[]{:S(2)}, u32[]{:S(2)}) collective-permute-start(bf16[80,1024]{1,0:T(8,128)(2,1)S(1)} %get-tuple-element.278), channel_id=1, source_target_pairs={{0,6},{1,7},{2,4},{3,5},{4,2},{5,3},{6,0},{7,1},{8,14},{9,15},{10,... | collective-permute-start | bytes 491528 | tf_op jit(solution)/shard_map/ppermute | solution.py:71
  228.1 12.3 %collective-permute-start.51 = (bf16[80,1024]{1,0:T(8,128)(2,1)S(1)}, bf16[80,1024]{1,0:T(8,128)(2,1)S(1)}, u32[]{:S(2)}, u32[]{:S(2)}) collective-permute-start(bf16[80,1024]{1,0:T(8,128)(2,1)S(1)} %get-tuple-element.253), channel_id=1, source_target_pairs={{0,4},{1,5},{2,6},{3,7},{4,0},{5,1},{6,2},{7,3},{8,12},{9,13},{10,... | collective-permute-start | bytes 491528 | tf_op jit(solution)/shard_map/ppermute | solution.py:71
  230.2 14.4 %collective-permute-start.52 = (bf16[80,1024]{1,0:T(8,128)(2,1)S(1)}, bf16[80,1024]{1,0:T(8,128)(2,1)S(1)}, u32[]{:S(2)}, u32[]{:S(2)}) collective-permute-start(bf16[80,1024]{1,0:T(8,128)(2,1)S(1)} %get-tuple-element.253), channel_id=1, source_target_pairs={{0,6},{1,7},{2,4},{3,5},{4,2},{5,3},{6,0},{7,1},{8,14},{9,15},{10,... | collective-permute-start | bytes 491528 | tf_op jit(solution)/shard_map/ppermute | solution.py:71
  249.8 7.6 %collective-permute-start.54 = (bf16[80,1376]{1,0:T(8,128)(2,1)S(1)}, bf16[80,1376]{1,0:T(8,128)(2,1)S(1)}, u32[]{:S(2)}, u32[]{:S(2)}) collective-permute-start(bf16[80,1376]{1,0:T(8,128)(2,1)S(1)} %get-tuple-element.293), channel_id=1, source_target_pairs={{0,16},{8,24},{16,0},{24,8},{1,17},{9,25},{17,1},{25,9},{2,18},{10... | collective-permute-start | bytes 660488 | tf_op jit(solution)/shard_map/ppermute | solution.py:65
  258.4 11.3 %collective-permute-start.56 = (bf16[2,80,1376]{2,1,0:T(8,128)(2,1)S(1)}, bf16[2,80,1376]{2,1,0:T(8,128)(2,1)S(1)}, u32[]{:S(2)}, u32[]{:S(2)}) collective-permute-start(bf16[2,80,1376]{2,1,0:T(8,128)(2,1)S(1)} %pad_maximum_fusion.4), channel_id=1, source_target_pairs={{0,8},{8,0},{16,24},{24,16},{1,9},{9,1},{17,25},{25,17},{2,10},{10... | collective-permute-start | bytes 1320968 | tf_op jit(solution)/shard_map/ppermute | solution.py:65
  259.9 10.9 %collective-permute-start.57 = (bf16[2,80,1376]{2,1,0:T(8,128)(2,1)S(1)}, bf16[2,80,1376]{2,1,0:T(8,128)(2,1)S(1)}, u32[]{:S(2)}, u32[]{:S(2)}) collective-permute-start(bf16[2,80,1376]{2,1,0:T(8,128)(2,1)S(1)} %pad_maximum_fusion.5), channel_id=1, source_target_pairs={{0,16},{8,24},{16,0},{24,8},{1,17},{9,25},{17,1},{25,9},{2,18},{10... | collective-permute-start | bytes 1320968 | tf_op jit(solution)/shard_map/ppermute | solution.py:65
  271.0 10.4 %collective-permute-start.58 = (bf16[2,80,1376]{2,1,0:T(8,128)(2,1)S(1)}, bf16[2,80,1376]{2,1,0:T(8,128)(2,1)S(1)}, u32[]{:S(2)}, u32[]{:S(2)}) collective-permute-start(bf16[2,80,1376]{2,1,0:T(8,128)(2,1)S(1)} %fusion.2), channel_id=1, source_target_pairs={{0,8},{8,0},{16,24},{24,16},{1,9},{9,1},{17,25},{25,17},{2,10},{10... | collective-permute-start | bytes 1320968 | tf_op jit(solution)/shard_map/ppermute | solution.py:65
  271.7 9.8 %collective-permute-start.59 = (bf16[2,80,1376]{2,1,0:T(8,128)(2,1)S(1)}, bf16[2,80,1376]{2,1,0:T(8,128)(2,1)S(1)}, u32[]{:S(2)}, u32[]{:S(2)}) collective-permute-start(bf16[2,80,1376]{2,1,0:T(8,128)(2,1)S(1)} %fusion.2), channel_id=1, source_target_pairs={{0,16},{8,24},{16,0},{24,8},{1,17},{9,25},{17,1},{25,9},{2,18},{10... | collective-permute-start | bytes 1320968 | tf_op jit(solution)/shard_map/ppermute | solution.py:65
  298.7 10.8 %collective-permute-start.63 = (bf16[80,1024]{1,0:T(8,128)(2,1)S(1)}, bf16[80,1024]{1,0:T(8,128)(2,1)S(1)}, u32[]{:S(2)}, u32[]{:S(2)}) collective-permute-start(bf16[80,1024]{1,0:T(8,128)(2,1)S(1)} %get-tuple-element.277), channel_id=1, source_target_pairs={{0,2},{1,3},{2,0},{3,1},{4,6},{5,7},{6,4},{7,5},{8,10},{9,11},{10,... | collective-permute-start | bytes 491528 | tf_op jit(solution)/shard_map/ppermute | solution.py:71
  298.7 13.3 %collective-permute-start.64 = (bf16[80,1024]{1,0:T(8,128)(2,1)S(1)}, bf16[80,1024]{1,0:T(8,128)(2,1)S(1)}, u32[]{:S(2)}, u32[]{:S(2)}) collective-permute-start(bf16[80,1024]{1,0:T(8,128)(2,1)S(1)} %get-tuple-element.276), channel_id=1, source_target_pairs={{0,4},{1,5},{2,6},{3,7},{4,0},{5,1},{6,2},{7,3},{8,12},{9,13},{10,... | collective-permute-start | bytes 491528 | tf_op jit(solution)/shard_map/ppermute | solution.py:71
  300.4 16.3 %collective-permute-start.65 = (bf16[80,1024]{1,0:T(8,128)(2,1)S(1)}, bf16[80,1024]{1,0:T(8,128)(2,1)S(1)}, u32[]{:S(2)}, u32[]{:S(2)}) collective-permute-start(bf16[80,1024]{1,0:T(8,128)(2,1)S(1)} %get-tuple-element.275), channel_id=1, source_target_pairs={{0,6},{1,7},{2,4},{3,5},{4,2},{5,3},{6,0},{7,1},{8,14},{9,15},{10,... | collective-permute-start | bytes 491528 | tf_op jit(solution)/shard_map/ppermute | solution.py:71
  (62 other events, 554.9 us)
